TPU v7x, 32 devices: a whole 2x2x4 slice. The times are simulated.
32 devices in a mesh: slab: 2 (over y), pulse: 4 (over z), rx: 2 (over x), rng: 2 (over core).
Axes of the slice: x: 2, y: 2, z: 4, core: 2. Of those that a mesh axis runs over, the one named last changes fastest.
Arguments:
- echoes: bfloat16 [2, 64, 16, 4096], P(None, ('slab', 'pulse'), 'rx', 'rng'), parts along dimension 1, may hold values from -6 to 6
- beam_angle: int32 [64], replicated, may hold values from 0 to 1023
- interp_table: int32 [32, 2, 64], replicated, may hold values from 0 to 11
Outputs:
- focused: float32 [2, 128, 4096], P(None, 'slab', ('rng', 'rx', 'pulse')), parts along dimension 1
There are 2 independent parts, one for each index of `slab`. A program takes and returns all parts, laid end to end along the dimension named above; an argument that names none is the same for every part. Nothing has to cross between parts.
All inputs are finite; a program needn't handle non-finite values.
Results may differ from a plain program's by a relative error of at most 0.0059.
Values may be sent and summed in bfloat16 or wider, within the bound.
No kernel may reach another device: no remote copies, remote signals or barrier semaphores. Data moves between devices by JAX's collectives and lax.ppermute only.
A program may use at most 64 MiB of HBM per device.

v0:
```python
import functools
import math

import jax
import jax.numpy as jnp
import ml_dtypes
import numpy as np
from jax import lax
from jax.experimental import pallas as pl
from jax.experimental.pallas import tpu as pltpu
from jax.sharding import PartitionSpec as P

RTAPS = 64
CTAPS = 512


half_root = 0.7071067811865476
full_turn = 2.0 * math.pi


def extended_2(block, sides, width):
    for axis, dim in sides:
        count = lax.axis_size(axis)
        forward = [(i, i + 1) for i in range(count - 1)]
        backward = [(target, source) for source, target in forward]
        low = lax.ppermute(
            lax.slice_in_dim(block, block.shape[dim] - width, None, axis=dim), axis, forward
        )
        high = lax.ppermute(lax.slice_in_dim(block, 0, width, axis=dim), axis, backward)
        block = jnp.concatenate([low, block, high], axis=dim)
    return block


def swapped(x, axis, distance):
    return lax.ppermute(x, axis, [(i, i ^ 1 << distance) for i in range(lax.axis_size(axis))])


def receiver_taps(channel_ids, tap_count):
    tap_index = jnp.arange(tap_count, dtype=jnp.float32)
    window = 0.5 - 0.5 * jnp.cos(full_turn * (tap_index + 0.5) / tap_count)
    window = window / jnp.sqrt(jnp.sum(window * window))
    channel = channel_ids.astype(jnp.float32)[:, None] + 1.0
    angle = full_turn * channel * (tap_index - tap_count // 2) / (4 * tap_count)
    return (
        (window * jnp.cos(angle)).astype(jnp.bfloat16),
        (window * jnp.sin(angle)).astype(jnp.bfloat16),
    )


def chirp_taps(tap_count):
    offset = jnp.arange(tap_count, dtype=jnp.int32) - tap_count // 2
    phase_step = jnp.mod(offset * offset, 2 * tap_count).astype(jnp.float32)
    angle = math.pi * phase_step / tap_count
    scale = 1.0 / math.sqrt(tap_count)
    return (
        (jnp.cos(angle) * scale).astype(jnp.bfloat16),
        (-jnp.sin(angle) * scale).astype(jnp.bfloat16),
    )


def steering(beam_angle, receivers):
    channel = jnp.arange(receivers, dtype=jnp.int32)
    turns = jnp.mod(beam_angle[:, None] * channel[None, :], 1024).astype(jnp.float32)
    angle = full_turn * turns / 1024.0
    scale = 1.0 / math.sqrt(receivers)
    return (
        (jnp.cos(angle) * scale).astype(jnp.bfloat16),
        (-jnp.sin(angle) * scale).astype(jnp.bfloat16),
    )


def interp_matrices(codes, beam_count):
    shifted = codes // 4 - 1
    fraction = jnp.mod(codes, 4).astype(jnp.float32) / 4.0
    weights = (
        -fraction * (fraction - 1.0) * (fraction - 2.0) / 6.0,
        (fraction + 1.0) * (fraction - 1.0) * (fraction - 2.0) / 2.0,
        -(fraction + 1.0) * fraction * (fraction - 2.0) / 2.0,
        (fraction + 1.0) * fraction * (fraction - 1.0) / 6.0,
    )
    columns = jnp.arange(beam_count, dtype=jnp.int32)
    matrices = jnp.zeros(codes.shape + (beam_count,), jnp.float32)
    for tap_index in range(4):
        target = jnp.mod(columns + shifted + tap_index - 1, beam_count)
        matrices = matrices + weights[tap_index][..., None] * (target[..., None] == columns).astype(
            jnp.float32
        )
    return matrices


def phases(node_ids, positions, beam_angle, side):
    base = jnp.mod(beam_angle[:, None] * (positions[None, :] + 1), 1024)
    factor = 2 * node_ids + side + 1
    turns = jnp.mod(base[:, None, :] * factor[None, :, None], 1024).astype(jnp.float32)
    angle = full_turn * turns / 1024.0
    return (jnp.cos(angle), jnp.sin(angle))


def side_term(picture, matrices, cosine, sine):
    moved = jnp.einsum("gqa,cagr->cqgr", matrices, picture, precision=lax.Precision.HIGHEST)
    return (cosine * moved[0] - sine * moved[1], sine * moved[0] + cosine * moved[1])


def merge_pair(left_image, right_image, node_ids, positions, beam_angle, interp_table):
    matrices = interp_matrices(interp_table[node_ids], left_image.shape[1])
    left_cos, left_sin = phases(node_ids, positions, beam_angle, 0)
    right_cos, right_sin = phases(node_ids, positions, beam_angle, 1)
    left_re, left_im = side_term(left_image, matrices[:, 0], left_cos, left_sin)
    right_re, right_im = side_term(right_image, matrices[:, 1], right_cos, right_sin)
    return jnp.stack([(left_re + right_re) * half_root, (left_im + right_im) * half_root])


def toeplitz_blocks(taps_re, taps_im):
    tap_count = taps_re.shape[-1]
    leading = taps_re.shape[:-1]

    def lay_out(taps):
        padded = jnp.concatenate([taps, jnp.zeros(leading + (tap_count + 1,), taps.dtype)], axis=-1)
        tiled = jnp.tile(padded, (1,) * len(leading) + (tap_count,))
        banded = tiled[..., : 2 * tap_count * tap_count].reshape(
            leading + (tap_count, 2 * tap_count)
        )
        return jnp.swapaxes(banded, -1, -2)

    real_band = lay_out(taps_re)
    imag_band = lay_out(taps_im)
    upper = jnp.concatenate([real_band, imag_band], axis=-1)
    lower = jnp.concatenate([-imag_band, real_band], axis=-1)
    return jnp.concatenate([upper, lower], axis=-2)


def block_filter(extended, matrices, tap_count, per_channel):
    pulses, channels, length = extended.shape[1:]
    blocks = length // tap_count - 1
    pieces = extended.reshape(2, pulses, channels, blocks + 1, tap_count)
    windows = jnp.concatenate([pieces[:, :, :, :-1], pieces[:, :, :, 1:]], axis=4)
    windows = jnp.transpose(windows, (1, 2, 3, 0, 4)).reshape(
        pulses, channels, blocks, 4 * tap_count
    )
    if per_channel:
        output = jnp.einsum("pcnw,cwo->pcno", windows, matrices, preferred_element_type=jnp.float32)
    else:
        output = jnp.einsum("pcnw,wo->pcno", windows, matrices, preferred_element_type=jnp.float32)
    output = output.reshape(pulses, channels, blocks, 2, tap_count)
    return jnp.transpose(output, (3, 0, 1, 2, 4)).reshape(2, pulses, channels, blocks * tap_count)


def local(echoes, beam_angle, interp_table):
    rx_count = lax.axis_size("rx")
    pulse_count = lax.axis_size("pulse")
    rng_place = lax.axis_index("rng")
    rx_place = lax.axis_index("rx")
    pulse_place = lax.axis_index("pulse")
    pulses, channels, length = echoes.shape[1:]
    beam_count = beam_angle.shape[0]
    receivers = channels * rx_count
    channel_ids = rx_place * channels + jnp.arange(channels, dtype=jnp.int32)
    rx_re, rx_im = receiver_taps(channel_ids, RTAPS)
    rx_bands = toeplitz_blocks(rx_re, rx_im)
    chirp_re, chirp_im = chirp_taps(CTAPS)
    chirp_band = toeplitz_blocks(chirp_re, chirp_im)
    extended = extended_2(echoes, (("rng", 3),), RTAPS // 2)
    filtered = block_filter(extended, rx_bands, RTAPS, True).astype(jnp.bfloat16)
    filtered = extended_2(filtered, (("rng", 3),), CTAPS // 2)
    compressed = block_filter(filtered, chirp_band, CTAPS, False).astype(jnp.bfloat16)
    steering_real, steering_imaginary = steering(beam_angle, receivers)
    steer_matrix = jnp.concatenate(
        [
            jnp.concatenate([steering_real, -steering_imaginary], axis=1),
            jnp.concatenate([steering_imaginary, steering_real], axis=1),
        ],
        axis=0,
    )
    arrived = lax.all_to_all(compressed, "rx", split_axis=3, concat_axis=2, tiled=True)
    item_count, recv_count, owned_cols = arrived.shape[1:]
    stacked = jnp.transpose(arrived, (0, 2, 1, 3)).reshape(2 * recv_count, item_count * owned_cols)
    formed = jnp.dot(steer_matrix, stacked, preferred_element_type=jnp.float32)
    picture = formed.reshape(2, beam_count, item_count, owned_cols)
    owned_width = length // rx_count
    positions = (
        rng_place * length + rx_place * owned_width + jnp.arange(owned_width, dtype=jnp.int32)
    )
    for level in range(pulses.bit_length() - 1):
        groups_now = pulses >> level + 1
        node_ids = (pulse_count + pulse_place) * groups_now + jnp.arange(
            groups_now, dtype=jnp.int32
        )
        paired = picture.reshape(2, beam_count, groups_now, 2, owned_width)
        picture = merge_pair(
            paired[:, :, :, 0], paired[:, :, :, 1], node_ids, positions, beam_angle, interp_table
        )
    picture = picture[:, :, 0]
    cross_levels = pulse_count.bit_length() - 1
    piece_width = owned_width // pulse_count
    pieces = picture.reshape(2, beam_count, pulse_count, piece_width)
    spots = positions.reshape(pulse_count, piece_width)
    for level in range(cross_levels):
        parity = jnp.right_shift(pulse_place, level) & 1
        count_now = pieces.shape[2]
        paired = pieces.reshape(2, beam_count, count_now // 2, 2, piece_width)
        kept_half = lax.dynamic_index_in_dim(paired, parity, 3, keepdims=False)
        sent_half = lax.dynamic_index_in_dim(paired, 1 - parity, 3, keepdims=False)
        partner = swapped(sent_half, "pulse", level)
        spot_pairs = spots.reshape(count_now // 2, 2, piece_width)
        spots = lax.dynamic_index_in_dim(spot_pairs, parity, 1, keepdims=False)
        own_part = kept_half.reshape(2, beam_count, -1)
        other_part = partner.reshape(2, beam_count, -1)
        left_image = jnp.where(parity == 0, own_part, other_part)
        right_image = jnp.where(parity == 0, other_part, own_part)
        combine_node_ids = jnp.reshape(
            (pulse_count >> level + 1) + jnp.right_shift(pulse_place, level + 1), (1,)
        )
        merged = merge_pair(
            left_image[:, :, None],
            right_image[:, :, None],
            combine_node_ids,
            spots.reshape(-1),
            beam_angle,
            interp_table,
        )
        flat = merged[:, :, 0]
        pieces = flat.reshape(2, beam_count, count_now // 2, piece_width)
    picture = pieces.reshape(2, beam_count, piece_width)
    return picture


LANES = 128
RX_TILE = 2 * LANES
CHIRP_TILE = 6 * LANES
HALO_TILES = 3
HALO = HALO_TILES * LANES


def vmem():
    return pl.BlockSpec(memory_space=pltpu.VMEM)


def rx_bands_table(receivers):
    step = np.arange(RTAPS, dtype=np.float64)
    window = 0.5 - 0.5 * np.cos(full_turn * (step + 0.5) / RTAPS)
    window = window / np.sqrt(np.sum(window * window))
    channel = np.arange(receivers, dtype=np.float64)[:, None] + 1.0
    angle = full_turn * channel * (step - RTAPS // 2) / (4 * RTAPS)
    offset = np.arange(RX_TILE)[:, None] - np.arange(LANES)[None, :]
    inside = (offset >= 0) & (offset < RTAPS)
    place = np.clip(offset, 0, RTAPS - 1)
    bands = [
        np.where(inside, taps[:, place], 0.0) for taps in (window * np.cos(angle), window * np.sin(angle))
    ]
    return np.concatenate(bands, axis=-1).astype(ml_dtypes.bfloat16)


def chirp_bands_table():
    offset = np.arange(CTAPS) - CTAPS // 2
    angle = math.pi * np.mod(offset * offset, 2 * CTAPS) / CTAPS
    scale = 1.0 / math.sqrt(CTAPS)
    offset = np.arange(CHIRP_TILE)[:, None] - np.arange(LANES)[None, :] - (LANES - RTAPS // 2)
    inside = (offset >= 0) & (offset < CTAPS)
    place = np.clip(offset, 0, CTAPS - 1)
    bands = [
        np.where(inside, taps[place], 0.0) for taps in (np.cos(angle) * scale, -np.sin(angle) * scale)
    ]
    return np.concatenate(bands, axis=-1).astype(ml_dtypes.bfloat16)


def chirp_piece(filtered_ref, chirp_ref, starts, out_ref):
    windows = [filtered_ref[:, pl.ds(start, CHIRP_TILE)] for start in starts]
    product = jnp.dot(
        jnp.concatenate(windows, axis=0), chirp_ref[...], preferred_element_type=jnp.float32
    )
    pulses, rows, _ = out_ref.shape
    channels = rows // 2
    product = product.reshape(len(starts), pulses, rows, 2 * LANES)
    for tile in range(len(starts)):
        block = product[tile]
        real = block[:, :channels, :LANES] - block[:, channels:, LANES:]
        imag = block[:, :channels, LANES:] + block[:, channels:, :LANES]
        out_ref[:, :, tile * LANES : (tile + 1) * LANES] = jnp.concatenate(
            [real, imag], axis=1
        ).astype(jnp.bfloat16)


def filter_kernel(sizes, echo_ref, edge_ref, bands_hbm, chirp_ref, *rest):
    rng_count, piece_count, piece_tiles = sizes
    send_refs, (filtered_ref, rows_in, rows_out, bands_ref, arrived) = (
        rest[:piece_count],
        rest[piece_count:],
    )
    _, pulses, channels, length = echo_ref.shape
    rng_place = lax.axis_index("rng")
    rx_place = lax.axis_index("rx")
    pulse_place = lax.axis_index("pulse")
    fetch = pltpu.make_async_copy(
        bands_hbm.at[pl.ds(rx_place * channels, channels)], bands_ref, arrived
    )
    fetch.start()
    tiles = length // LANES
    group = 2 * pulses
    has_low = jnp.where(rng_place > 0, 1.0, 0.0).astype(jnp.float32)
    has_high = jnp.where(rng_place < rng_count - 1, 1.0, 0.0).astype(jnp.float32)
    for part in range(2):
        for pulse in range(pulses):
            where = pl.ds(part * pulses + pulse, channels, stride=group)
            edge = edge_ref[part, pulse].astype(jnp.float32)
            block = echo_ref[part, pulse].astype(jnp.float32)
            for tile in range(HALO_TILES):
                span = edge[:, tile * LANES : (tile + 1) * LANES]
                rows_in[tile, where, :] = span * has_low
                rows_in[HALO_TILES + tiles + tile, where, :] = span * has_high
            for tile in range(tiles):
                span = block[:, tile * LANES : (tile + 1) * LANES]
                rows_in[HALO_TILES + tile, where, :] = span
    fetch.wait()
    out_tiles = tiles + 2 * HALO_TILES - 1
    lane = lax.broadcasted_iota(jnp.int32, (1, LANES), 1)
    total = rng_count * length
    for channel in range(channels):
        rows = rows_in[:, channel * group : (channel + 1) * group, :].astype(jnp.bfloat16)
        windows = jnp.concatenate(
            [
                rows[:-1].reshape(out_tiles * group, LANES),
                rows[1:].reshape(out_tiles * group, LANES),
            ],
            axis=1,
        )
        product = jnp.dot(windows, bands_ref[channel], preferred_element_type=jnp.float32)
        product = product.reshape(out_tiles, group, 2 * LANES)
        for tile in range(out_tiles):
            block = product[tile]
            real = block[:pulses, :LANES] - block[pulses:, LANES:]
            imag = block[:pulses, LANES:] + block[pulses:, :LANES]
            if tile <= HALO_TILES - 1 or tile >= out_tiles - HALO_TILES:
                spot = rng_place * length + (tile - HALO_TILES) * LANES + RTAPS // 2 + lane
                inside = (spot >= 0) & (spot < total)
                real = jnp.where(inside, real, 0.0)
                imag = jnp.where(inside, imag, 0.0)
            rows_out[tile, pl.ds(channel, pulses, stride=2 * channels), :] = real
            rows_out[tile, pl.ds(channels + channel, pulses, stride=2 * channels), :] = imag
    for tile in range(out_tiles):
        filtered_ref[:, tile * LANES : (tile + 1) * LANES] = rows_out[tile].astype(jnp.bfloat16)
    base = (1 - rx_place) * (piece_count * piece_tiles)
    for distance in range(piece_count):
        piece = jnp.bitwise_xor(pulse_place, distance)
        first = base + piece * piece_tiles
        starts = [pl.multiple_of((first + t) * LANES, LANES) for t in range(piece_tiles)]
        chirp_piece(filtered_ref, chirp_ref, starts, send_refs[distance])


def keep_kernel(sizes, filtered_ref, chirp_ref, *keep_refs):
    piece_count, piece_tiles = sizes
    rx_place = lax.axis_index("rx")
    pulse_place = lax.axis_index("pulse")
    base = rx_place * (piece_count * piece_tiles)
    for distance in range(piece_count):
        piece = jnp.bitwise_xor(pulse_place, distance)
        first = base + piece * piece_tiles
        starts = [pl.multiple_of((first + t) * LANES, LANES) for t in range(piece_tiles)]
        chirp_piece(filtered_ref, chirp_ref, starts, keep_refs[distance])


def turn_parts(step):
    shifted = step + 128
    angle = (jnp.bitwise_and(shifted, 255) - 128).astype(jnp.float32) * (full_turn / 1024.0)
    quarter = jnp.right_shift(shifted, 8)
    square = angle * angle
    cosine = 1.0 + square * (-1 / 2 + square * (1 / 24 + square * (-1 / 720 + square * (1 / 40320))))
    sine = angle * (1.0 + square * (-1 / 6 + square * (1 / 120 + square * (-1 / 5040))))
    odd = jnp.bitwise_and(quarter, 1) == 1
    real = jnp.where(odd, sine, cosine)
    imag = jnp.where(odd, cosine, sine)
    real = jnp.where(jnp.bitwise_and(quarter + 1, 2) == 2, -real, real)
    imag = jnp.where(jnp.bitwise_and(quarter, 2) == 2, -imag, imag)
    return real, imag


def as_column(row):
    count = row.shape[1]
    first = lax.broadcasted_iota(jnp.int32, (count, count), 0)
    second = lax.broadcasted_iota(jnp.int32, (count, count), 1)
    spread = jnp.where(first == second, row.astype(jnp.float32), 0.0)
    return jnp.sum(spread, axis=1, keepdims=True).astype(jnp.int32)


def interp_matrix(codes_ref, row):
    code = as_column(codes_ref[pl.ds(row, 1), :])
    beams = codes_ref.shape[1]
    shift = jnp.right_shift(code, 2) - 1
    part = jnp.bitwise_and(code, 3).astype(jnp.float32) * 0.25
    weights = (
        -part * (part - 1.0) * (part - 2.0) * (1.0 / 6.0),
        (part + 1.0) * (part - 1.0) * (part - 2.0) * 0.5,
        -(part + 1.0) * part * (part - 2.0) * 0.5,
        (part + 1.0) * part * (part - 1.0) * (1.0 / 6.0),
    )
    angle_bin = lax.broadcasted_iota(jnp.int32, (beams, beams), 0)
    column = lax.broadcasted_iota(jnp.int32, (beams, beams), 1)
    tap = jnp.bitwise_and(column - angle_bin - shift + 1, beams - 1)
    matrix = jnp.zeros((beams, beams), jnp.float32)
    for index in range(4):
        matrix = jnp.where(tap == index, weights[index], matrix)
    return matrix.astype(jnp.bfloat16)


def tables_kernel(
    sizes, angle_ref, codes_ref, first_ref, inner_ref, outer_ref, phase_ref, outer_phase_ref
):
    pulses, channels, rx_count, width = sizes
    rng_place = lax.axis_index("rng")
    rx_place = lax.axis_index("rx")
    pulse_place = lax.axis_index("pulse")
    beams = angle_ref.shape[1]
    piece_count = phase_ref.shape[0]
    piece_width = phase_ref.shape[4]
    images = pulses * piece_count
    angle = as_column(angle_ref[...])
    column = lax.broadcasted_iota(jnp.int32, (1, 4 * channels * 2), 1)
    within = jnp.bitwise_and(column, 4 * channels - 1)
    owner = jnp.bitwise_xor(rx_place, jnp.where(within >= 2 * channels, 1, 0))
    receiver = owner * channels + jnp.bitwise_and(column, channels - 1)
    is_imag = jnp.bitwise_and(within, channels) != 0
    scale = 1.0 / math.sqrt(channels * rx_count)
    steer_re, steer_im = turn_parts(jnp.bitwise_and(angle * receiver, 1023))
    steer_re = (steer_re * scale).astype(jnp.bfloat16).astype(jnp.float32)
    steer_im = (-steer_im * scale).astype(jnp.bfloat16).astype(jnp.float32)
    steer = jnp.concatenate(
        [
            jnp.where(is_imag, -steer_im, steer_re).astype(jnp.bfloat16),
            jnp.where(is_imag, steer_re, steer_im).astype(jnp.bfloat16),
        ],
        axis=1,
    )
    low_half = column >= 4 * channels
    entries = 8 * channels
    for index in range(pulses):
        matrix = interp_matrix(codes_ref, images + pulse_place * pulses + index)
        composed = jnp.dot(matrix, steer, preferred_element_type=jnp.float32)
        for part in range(2):
            value = composed[:, part * entries : (part + 1) * entries]
            high = value.astype(jnp.bfloat16)
            low = (value - high.astype(jnp.float32)).astype(jnp.bfloat16)
            first_ref[index, part * beams : (part + 1) * beams, :] = jnp.where(
                low_half, low.astype(jnp.float32), high.astype(jnp.float32)
            ).astype(jnp.bfloat16)
    factors = []
    slot = 0
    now = pulses
    while now > 1:
        factors.extend(now * piece_count + pulse_place * now + i + 1 for i in range(now))
        if now < pulses:
            for index in range(now):
                inner_ref[slot] = interp_matrix(
                    codes_ref, now * piece_count + pulse_place * now + index
                )
                slot += 1
        now //= 2
    lane = lax.broadcasted_iota(jnp.int32, (1, piece_width), 1)
    block = (rng_place * rx_count + rx_place) * width + 1

    def one_piece(distance, carry):
        piece = jnp.bitwise_xor(pulse_place, distance)
        base = jnp.bitwise_and(angle * (block + piece * piece_width + lane), 1023)
        for index, factor in enumerate(factors):
            real, imag = turn_parts(jnp.bitwise_and(base * factor, 1023))
            phase_ref[distance, index, 0] = real * half_root
            phase_ref[distance, index, 1] = imag * half_root
        return carry

    lax.fori_loop(0, piece_count, one_piece, 0)
    base = jnp.bitwise_and(angle * (block + pulse_place * piece_width + lane), 1023)
    slot = 0
    now = piece_count
    while now > 1:
        for index in range(now):
            outer_ref[slot] = interp_matrix(codes_ref, now + index)
            real, imag = turn_parts(jnp.bitwise_and(base * (now + index + 1), 1023))
            outer_phase_ref[slot, 0] = real * half_root
            outer_phase_ref[slot, 1] = imag * half_root
            slot += 1
        now //= 2


def turned(real, imag, phase_re, phase_im):
    return phase_re * real - phase_im * imag, phase_im * real + phase_re * imag


def inner_kernel(own_ref, other_ref, first_ref, inner_ref, phase_ref, out_ref):
    pulses = own_ref.shape[0]
    beams = inner_ref.shape[1]
    terms = []
    for index in range(pulses):
        rows = jnp.concatenate([own_ref[index], other_ref[index]], axis=0)
        moved = jnp.dot(
            first_ref[index],
            jnp.concatenate([rows, rows], axis=0),
            preferred_element_type=jnp.float32,
        )
        terms.append(
            turned(moved[:beams], moved[beams:], phase_ref[0, index, 0], phase_ref[0, index, 1])
        )
        if index & 1:
            right, left = terms.pop(), terms.pop()
            terms.append((left[0] + right[0], left[1] + right[1]))
    slot = 0
    phase_slot = pulses
    while len(terms) > 1:
        pictures, terms = terms, []
        for index, (real, imag) in enumerate(pictures):
            matrix = inner_ref[slot]
            moved_re = jnp.dot(
                matrix, real.astype(jnp.bfloat16), preferred_element_type=jnp.float32
            )
            moved_im = jnp.dot(
                matrix, imag.astype(jnp.bfloat16), preferred_element_type=jnp.float32
            )
            terms.append(
                turned(moved_re, moved_im, phase_ref[0, phase_slot, 0], phase_ref[0, phase_slot, 1])
            )
            if index & 1:
                right, left = terms.pop(), terms.pop()
                terms.append((left[0] + right[0], left[1] + right[1]))
            slot += 1
            phase_slot += 1
    out_ref[0] = terms[0][0].astype(jnp.bfloat16)
    out_ref[1] = terms[0][1].astype(jnp.bfloat16)


def outer_kernel(outer_ref, phase_ref, *rest):
    image_refs, out_ref = rest[:-1], rest[-1]
    pulse_place = lax.axis_index("pulse")
    pictures = [(ref[0], ref[1]) for ref in image_refs]
    base = 0
    level = 0
    while len(pictures) > 1:
        count = len(pictures)
        place = jnp.right_shift(pulse_place, level)
        merged = []
        for distance, (real, imag) in enumerate(pictures):
            slot = base + jnp.bitwise_xor(place, distance)
            matrix = outer_ref[slot]
            moved_re = jnp.dot(
                matrix, real.astype(jnp.bfloat16), preferred_element_type=jnp.float32
            )
            moved_im = jnp.dot(
                matrix, imag.astype(jnp.bfloat16), preferred_element_type=jnp.float32
            )
            merged.append(turned(moved_re, moved_im, phase_ref[slot, 0], phase_ref[slot, 1]))
            if distance & 1:
                right, left = merged.pop(), merged.pop()
                merged.append((left[0] + right[0], left[1] + right[1]))
        pictures = merged
        base += count
        level += 1
    out_ref[0] = pictures[0][0]
    out_ref[1] = pictures[0][1]


PARAMS = dict(compiler_params=pltpu.CompilerParams(vmem_limit_bytes=48 * 1024 * 1024))


def fast(echoes, beam_angle, interp_table):
    rng_count = lax.axis_size("rng")
    rx_count = lax.axis_size("rx")
    pulse_count = lax.axis_size("pulse")
    rng_place = lax.axis_index("rng")
    _, pulses, channels, length = echoes.shape
    beams = beam_angle.shape[0]
    width = length // rx_count
    piece_width = width // pulse_count
    piece_tiles = piece_width // LANES
    rows = 2 * channels
    bands = jnp.asarray(rx_bands_table(channels * rx_count))
    chirp = jnp.asarray(chirp_bands_table())
    bf16 = jnp.bfloat16
    f32 = jnp.float32
    edge = jnp.where(rng_place == 0, echoes[..., length - HALO :], echoes[..., :HALO])
    edge = swapped(edge, "rng", 0)
    shape = jax.ShapeDtypeStruct
    piece_shape = shape((pulses, rows, piece_width), bf16)
    tiles = length // LANES + 2 * HALO_TILES
    filtered_shape = shape((rows * pulses, (tiles - 1) * LANES), bf16)
    *sent, filtered = pl.pallas_call(
        functools.partial(filter_kernel, (rng_count, pulse_count, piece_tiles)),
        out_shape=[piece_shape] * pulse_count + [filtered_shape],
        in_specs=[vmem(), vmem(), pl.BlockSpec(memory_space=pl.ANY), vmem()],
        out_specs=[vmem()] * (pulse_count + 1),
        scratch_shapes=[
            pltpu.VMEM((tiles, rows * pulses, LANES), f32),
            pltpu.VMEM((tiles - 1, rows * pulses, LANES), f32),
            pltpu.VMEM((channels,) + bands.shape[1:], bf16),
            pltpu.SemaphoreType.DMA,
        ],
        name="filter",
        **PARAMS,
    )(echoes, edge, bands, chirp)
    received = [swapped(piece, "rx", 0) for piece in sent]
    kept = pl.pallas_call(
        functools.partial(keep_kernel, (pulse_count, piece_tiles)),
        out_shape=[piece_shape] * pulse_count,
        in_specs=[vmem()] * 2,
        out_specs=[vmem()] * pulse_count,
        name="keep",
        **PARAMS,
    )(filtered, chirp)
    inner_count = pulses - 2
    outer_count = 2 * pulse_count - 2
    first, inner, outer, phase, outer_phase = pl.pallas_call(
        functools.partial(tables_kernel, (pulses, channels, rx_count, width)),
        out_shape=[
            shape((pulses, 2 * beams, 8 * channels), bf16),
            shape((inner_count, beams, beams), bf16),
            shape((outer_count, beams, beams), bf16),
            shape((pulse_count, 2 * pulses - 2, 2, beams, piece_width), f32),
            shape((outer_count, 2, beams, piece_width), f32),
        ],
        in_specs=[vmem()] * 2,
        out_specs=[vmem()] * 5,
        name="tables",
        **PARAMS,
    )(beam_angle.reshape(1, beams), interp_table.reshape(-1, beams))
    images = []
    for distance in reversed(range(pulse_count)):
        image = pl.pallas_call(
            inner_kernel,
            out_shape=shape((2, beams, piece_width), bf16),
            grid=(1,),
            in_specs=[
                vmem(),
                vmem(),
                vmem(),
                vmem(),
                pl.BlockSpec(
                    (1,) + phase.shape[1:], lambda step, distance=distance: (distance, 0, 0, 0, 0)
                ),
            ],
            out_specs=vmem(),
            name="inner",
            **PARAMS,
        )(kept[distance], received[distance], first, inner, phase)
        if distance:
            image = lax.ppermute(
                image, "pulse", [(i, i ^ distance) for i in range(pulse_count)]
            )
        images.insert(0, image)
    return pl.pallas_call(
        outer_kernel,
        out_shape=shape((2, beams, piece_width), f32),
        in_specs=[vmem()] * (2 + pulse_count),
        out_specs=vmem(),
        name="outer",
        **PARAMS,
    )(outer, outer_phase, *images)


def power_of_two(count):
    return count > 0 and count & (count - 1) == 0


def per_device(echoes, beam_angle, interp_table):
    _, pulses, channels, length = echoes.shape
    rx_count = lax.axis_size("rx")
    pulse_count = lax.axis_size("pulse")
    piece_width = length // (rx_count * pulse_count)
    if (
        lax.axis_size("rng") == 2
        and rx_count == 2
        and channels == 8
        and pulses == 8
        and power_of_two(pulse_count)
        and pulse_count > 1
        and power_of_two(beam_angle.shape[0])
        and beam_angle.shape[0] % 16 == 0
        and piece_width % LANES == 0
    ):
        return fast(echoes, beam_angle, interp_table)
    return local(echoes, beam_angle, interp_table)


def solution(mesh):
    placed = (P(None, ("slab", "pulse"), "rx", "rng"), P(), P())
    return jax.shard_map(
        per_device,
        mesh=mesh,
        in_specs=placed,
        out_specs=P(None, "slab", ("rng", "rx", "pulse")),
        check_vma=False,
    )
```

profile of v0, /device:TPU:0, one launch (start us, length us, event | category | flops | bytes accessed | tf_op | source)
XLA Modules:
  0.0 42.2 jit_solution(7692183405147842421)
XLA Ops:
  0.0 1.0 %slice_select_fusion = bf16[2,8,8,384]{3,2,1,0:T(8,128)(2,1)S(1)} fusion(bf16[2,8,8,2048]{3,2,1,0:T(8,128)(2,1)} %echo_ref.1, pred[]{:T(512)S(6)} %eq.3), kind=kLoop, calls=%fused_computation | loop fusion | flops 49152 | bytes 294913 | tf_op jit(solution)/shard_map/jit(_where)/select_n | solution.py:575
  1.0 0.5 %collective-permute-start = (bf16[2,8,8,384]{3,2,1,0:T(8,128)(2,1)S(1)}, bf16[2,8,8,384]{3,2,1,0:T(8,128)(2,1)S(1)}, u32[]{:S(2)}, u32[]{:S(2)}) collective-permute-start(bf16[2,8,8,384]{3,2,1,0:T(8,128)(2,1)S(1)} %slice_select_fusion), channel_id=1, source_target_pairs={{0,1},{1,0},{2,3},{3,2},{4,5},{5,4},{6,7},{7,6},{8,9},{9,8},{10,11... | collective-permute-start | bytes 294920 | tf_op jit(solution)/shard_map/ppermute | solution.py:35
  1.5 0.9 %collective-permute-done.edge_ref = bf16[2,8,8,384]{3,2,1,0:T(8,128)(2,1)S(1)} collective-permute-done((bf16[2,8,8,384]{3,2,1,0:T(8,128)(2,1)S(1)}, bf16[2,8,8,384]{3,2,1,0:T(8,128)(2,1)S(1)}, u32[]{:S(2)}, u32[]{:S(2)}) %collective-permute-start) | collective-permute-done | bytes 98336 | tf_op jit(solution)/shard_map/ppermute | solution.py:35
  2.4 0.0 copy-start
  2.4 1.6 %copy-done = bf16[16,256,256]{2,1,0:T(8,128)(2,1)S(1)} copy-done((bf16[16,256,256]{2,1,0:T(8,128)(2,1)S(1)}, bf16[16,256,256]{2,1,0:T(8,128)(2,1)}, u32[]{:S(2)}) %copy-start) | copy-done | bytes 2097176
  4.0 0.0 copy-start.1
  4.0 1.0 %copy-done.1 = bf16[768,256]{1,0:T(8,128)(2,1)S(1)} copy-done((bf16[768,256]{1,0:T(8,128)(2,1)S(1)}, bf16[768,256]{1,0:T(8,128)(2,1)}, u32[]{:S(2)}) %copy-start.1) | copy-done | bytes 393240
  5.0 0.0 copy-start.2
  5.0 1.0 %copy-done.2 = bf16[2,8,8,2048]{3,2,1,0:T(8,128)(2,1)S(1)} copy-done((bf16[2,8,8,2048]{3,2,1,0:T(8,128)(2,1)S(1)}, bf16[2,8,8,2048]{3,2,1,0:T(8,128)(2,1)}, u32[]{:S(2)}) %copy-start.2) | copy-done | bytes 524312
  6.1 2.2 %filter.1 = (bf16[8,16,256]{2,1,0:T(8,128)(2,1)S(1)}, bf16[8,16,256]{2,1,0:T(8,128)(2,1)S(1)}, bf16[8,16,256]{2,1,0:T(8,128)(2,1)S(1)}, bf16[8,16,256]{2,1,0:T(8,128)(2,1)S(1)}, bf16[128,2688]{1,0:T(8,128)(2,1)S(1)}) custom-call(bf16[2,8,8,2048]{3,2,1,0:T(8,128)(2,1)S(1)} %copy-done.2, bf16[2,8,8,384]{3,2,1,0:T(8,128)(2,1)S(1)} %collective-permute-done.edge_ref, ...), custom_call_target="tpu_custom_call" | custom-call | tf_op jit(solution)/shard_map/filter/pallas_call | solution.py:581
  8.2 2.9 %collective-permute-start.2 = (bf16[8,16,256]{2,1,0:T(8,128)(2,1)S(1)}, bf16[8,16,256]{2,1,0:T(8,128)(2,1)S(1)}, u32[]{:S(2)}, u32[]{:S(2)}) collective-permute-start(bf16[8,16,256]{2,1,0:T(8,128)(2,1)S(1)} %get-tuple-element.28), channel_id=1, source_target_pairs={{0,2},{2,0},{1,3},{3,1},{4,6},{6,4},{5,7},{7,5},{8,10},{10,8},{9,1... | collective-permute-start | bytes 196616 | tf_op jit(solution)/shard_map/ppermute | solution.py:35
  11.1 0.1 collective-permute-start.4
  11.2 1.9 %collective-permute-start.6 = (bf16[8,16,256]{2,1,0:T(8,128)(2,1)S(1)}, bf16[8,16,256]{2,1,0:T(8,128)(2,1)S(1)}, u32[]{:S(2)}, u32[]{:S(2)}) collective-permute-start(bf16[8,16,256]{2,1,0:T(8,128)(2,1)S(1)} %get-tuple-element.32), channel_id=1, source_target_pairs={{0,2},{2,0},{1,3},{3,1},{4,6},{6,4},{5,7},{7,5},{8,10},{10,8},{9,1... | collective-permute-start | bytes 196616 | tf_op jit(solution)/shard_map/ppermute | solution.py:35
  13.2 0.0 copy-start.3
  13.2 0.8 %copy-done.3 = s32[32,2,64]{2,1,0:T(2,128)S(1)} copy-done((s32[32,2,64]{2,1,0:T(2,128)S(1)}, s32[32,2,64]{2,1,0:T(2,128)}, u32[]{:S(2)}) %copy-start.3) | copy-done | bytes 16408
  13.9 0.0 copy-start.4
  13.9 0.7 %copy-done.4 = s32[64]{0:T(128)S(1)} copy-done((s32[64]{0:T(128)S(1)}, s32[64]{0:T(128)}, u32[]{:S(2)}) %copy-start.4) | copy-done | bytes 280
  14.6 8.6 %tables.1 = (bf16[8,128,64]{2,1,0:T(8,128)(2,1)S(1)}, bf16[6,64,64]{2,1,0:T(8,128)(2,1)S(1)}, bf16[6,64,64]{2,1,0:T(8,128)(2,1)S(1)}, f32[4,14,2,64,256]{4,3,2,1,0:T(8,128)}, f32[6,2,64,256]{3,2,1,0:T(8,128)S(1)}) custom-call(s32[1,64]{1,0:T(1,128)S(1)} %bitcast.3, s32[64,64]{1,0:T(8,128)S(1)} %bitcast.2), custom_call_target="tpu_custom_call" | custom-call | tf_op jit(solution)/shard_map/tables/pallas_call | solution.py:606
  23.2 0.6 %keep.1 = (bf16[8,16,256]{2,1,0:T(8,128)(2,1)S(1)}, bf16[8,16,256]{2,1,0:T(8,128)(2,1)S(1)}, bf16[8,16,256]{2,1,0:T(8,128)(2,1)S(1)}, bf16[8,16,256]{2,1,0:T(8,128)(2,1)S(1)}) custom-call(bf16[128,2688]{1,0:T(8,128)(2,1)S(1)} %get-tuple-element.21.filtered_ref, bf16[768,256]{1,0:T(8,128)(2,1)S(1)} %copy-done.1), custom_call_target="tpu_custom_call" | custom-call | tf_op jit(solution)/shard_map/keep/pallas_call | solution.py:596
  23.8 0.1 collective-permute-start.1
  24.0 0.0 collective-permute-done.2.other_ref
  24.0 2.1 %inner.5 = bf16[2,64,256]{2,1,0:T(8,128)(2,1)S(1)} custom-call(bf16[8,16,256]{2,1,0:T(8,128)(2,1)S(1)} %get-tuple-element.27.own_ref, bf16[8,16,256]{2,1,0:T(8,128)(2,1)S(1)} %collective-permute-done.2.other_ref, bf16[8,128,64]{2,1,0:T(8,128)(2,1)S(1)} %get-tuple-element.24.first_ref, bf16[6,64,64]{2,1,0:T(8,128)(2,1)S(1)} %get-tuple-element.25.inner_ref, ...), custom_call_target="tpu_custom_call" | custom-call | tf_op jit(solution)/shard_map/inner/pallas_call | solution.py:622
  26.1 2.1 %collective-permute-start.3 = (bf16[2,64,256]{2,1,0:T(8,128)(2,1)S(1)}, bf16[2,64,256]{2,1,0:T(8,128)(2,1)S(1)}, u32[]{:S(2)}, u32[]{:S(2)}) collective-permute-start(bf16[2,64,256]{2,1,0:T(8,128)(2,1)S(1)} %inner.5), channel_id=1, source_target_pairs={{0,4},{4,0},{8,12},{12,8},{1,5},{5,1},{9,13},{13,9},{2,6},{6,2},{1... | collective-permute-start | bytes 196616 | tf_op jit(solution)/shard_map/ppermute | solution.py:640
  28.2 0.0 collective-permute-done.4.other_ref
  28.2 2.1 %inner.6 = bf16[2,64,256]{2,1,0:T(8,128)(2,1)S(1)} custom-call(bf16[8,16,256]{2,1,0:T(8,128)(2,1)S(1)} %get-tuple-element.29.own_ref, bf16[8,16,256]{2,1,0:T(8,128)(2,1)S(1)} %collective-permute-done.4.other_ref, bf16[8,128,64]{2,1,0:T(8,128)(2,1)S(1)} %get-tuple-element.24.first_ref, bf16[6,64,64]{2,1,0:T(8,128)(2,1)S(1)} %get-tuple-element.25.inner_ref, ...), custom_call_target="tpu_custom_call" | custom-call | tf_op jit(solution)/shard_map/inner/pallas_call | solution.py:622
  30.3 2.6 %collective-permute-start.5 = (bf16[2,64,256]{2,1,0:T(8,128)(2,1)S(1)}, bf16[2,64,256]{2,1,0:T(8,128)(2,1)S(1)}, u32[]{:S(2)}, u32[]{:S(2)}) collective-permute-start(bf16[2,64,256]{2,1,0:T(8,128)(2,1)S(1)} %inner.6), channel_id=1, source_target_pairs={{0,8},{4,12},{8,0},{12,4},{1,9},{5,13},{9,1},{13,5},{2,10},{6,14},... | collective-permute-start | bytes 196616 | tf_op jit(solution)/shard_map/ppermute | solution.py:640
  32.9 0.0 collective-permute-done.6.other_ref
  32.9 2.1 %inner.7 = bf16[2,64,256]{2,1,0:T(8,128)(2,1)S(1)} custom-call(bf16[8,16,256]{2,1,0:T(8,128)(2,1)S(1)} %get-tuple-element.31.own_ref, bf16[8,16,256]{2,1,0:T(8,128)(2,1)S(1)} %collective-permute-done.6.other_ref, bf16[8,128,64]{2,1,0:T(8,128)(2,1)S(1)} %get-tuple-element.24.first_ref, bf16[6,64,64]{2,1,0:T(8,128)(2,1)S(1)} %get-tuple-element.25.inner_ref, ...), custom_call_target="tpu_custom_call" | custom-call | tf_op jit(solution)/shard_map/inner/pallas_call | solution.py:622
  35.1 0.1 collective-permute-start.7
  35.1 0.0 collective-permute-done.1.other_ref
  35.2 2.1 %inner.4.rest_0_ = bf16[2,64,256]{2,1,0:T(8,128)(2,1)S(1)} custom-call(bf16[8,16,256]{2,1,0:T(8,128)(2,1)S(1)} %get-tuple-element.22.own_ref, bf16[8,16,256]{2,1,0:T(8,128)(2,1)S(1)} %collective-permute-done.1.other_ref, bf16[8,128,64]{2,1,0:T(8,128)(2,1)S(1)} %get-tuple-element.24.first_ref, bf16[6,64,64]{2,1,0:T(8,128)(2,1)S(1)} %get-tuple-element.25.inner_ref, ...), custom_call_target="tpu_custom_call" | custom-call | tf_op jit(solution)/shard_map/inner/pallas_call | solution.py:622
  37.3 0.0 collective-permute-done.3.rest_1_
  37.3 0.0 collective-permute-done.5.rest_2_
  37.3 3.9 %collective-permute-done.7.rest_3_ = bf16[2,64,256]{2,1,0:T(8,128)(2,1)S(1)} collective-permute-done((bf16[2,64,256]{2,1,0:T(8,128)(2,1)S(1)}, bf16[2,64,256]{2,1,0:T(8,128)(2,1)S(1)}, u32[]{:S(2)}, u32[]{:S(2)}) %collective-permute-start.7) | collective-permute-done | bytes 65568 | tf_op jit(solution)/shard_map/ppermute | solution.py:640
  41.2 1.0 %outer.1 = f32[2,64,256]{2,1,0:T(8,128)} custom-call(bf16[6,64,64]{2,1,0:T(8,128)(2,1)S(1)} %get-tuple-element.19.outer_ref, f32[6,2,64,256]{3,2,1,0:T(8,128)S(1)} %get-tuple-element.20.phase_ref, bf16[2,64,256]{2,1,0:T(8,128)(2,1)S(1)} %inner.4.rest_0_, bf16[2,64,256]{2,1,0:T(8,128)(2,1)S(1)} %collective-permute-done.3.rest_1_, ...), custom_call_target="tpu_custom_call" | custom-call | tf_op jit(solution)/shard_map/outer/pallas_call | solution.py:644
Async XLA Ops:
  1.0 1.5 %collective-permute-start = (bf16[2,8,8,384]{3,2,1,0:T(8,128)(2,1)S(1)}, bf16[2,8,8,384]{3,2,1,0:T(8,128)(2,1)S(1)}, u32[]{:S(2)}, u32[]{:S(2)}) collective-permute-start(bf16[2,8,8,384]{3,2,1,0:T(8,128)(2,1)S(1)} %slice_select_fusion), channel_id=1, source_target_pairs={{0,1},{1,0},{2,3},{3,2},{4,5},{5,4},{6,7},{7,6},{8,9},{9,8},{10,11... | collective-permute-start | bytes 294920 | tf_op jit(solution)/shard_map/ppermute | solution.py:35
  2.4 1.6 %copy-start = (bf16[16,256,256]{2,1,0:T(8,128)(2,1)S(1)}, bf16[16,256,256]{2,1,0:T(8,128)(2,1)}, u32[]{:S(2)}) copy-start(bf16[16,256,256]{2,1,0:T(8,128)(2,1)} %constant.10.clone.bands_hbm) | copy-start | bytes 6291460
  4.0 1.0 %copy-start.1 = (bf16[768,256]{1,0:T(8,128)(2,1)S(1)}, bf16[768,256]{1,0:T(8,128)(2,1)}, u32[]{:S(2)}) copy-start(bf16[768,256]{1,0:T(8,128)(2,1)} %constant.11.clone.chirp_ref) | copy-start | bytes 1179652
  5.0 1.0 %copy-start.2 = (bf16[2,8,8,2048]{3,2,1,0:T(8,128)(2,1)S(1)}, bf16[2,8,8,2048]{3,2,1,0:T(8,128)(2,1)}, u32[]{:S(2)}) copy-start(bf16[2,8,8,2048]{3,2,1,0:T(8,128)(2,1)} %echo_ref.1) | copy-start | bytes 1572868
  8.2 15.7 %collective-permute-start.2 = (bf16[8,16,256]{2,1,0:T(8,128)(2,1)S(1)}, bf16[8,16,256]{2,1,0:T(8,128)(2,1)S(1)}, u32[]{:S(2)}, u32[]{:S(2)}) collective-permute-start(bf16[8,16,256]{2,1,0:T(8,128)(2,1)S(1)} %get-tuple-element.28), channel_id=1, source_target_pairs={{0,2},{2,0},{1,3},{3,1},{4,6},{6,4},{5,7},{7,5},{8,10},{10,8},{9,1... | collective-permute-start | bytes 196616 | tf_op jit(solution)/shard_map/ppermute | solution.py:35
  11.1 17.0 %collective-permute-start.4 = (bf16[8,16,256]{2,1,0:T(8,128)(2,1)S(1)}, bf16[8,16,256]{2,1,0:T(8,128)(2,1)S(1)}, u32[]{:S(2)}, u32[]{:S(2)}) collective-permute-start(bf16[8,16,256]{2,1,0:T(8,128)(2,1)S(1)} %get-tuple-element.30), channel_id=1, source_target_pairs={{0,2},{2,0},{1,3},{3,1},{4,6},{6,4},{5,7},{7,5},{8,10},{10,8},{9,1... | collective-permute-start | bytes 196616 | tf_op jit(solution)/shard_map/ppermute | solution.py:35
  11.2 21.7 %collective-permute-start.6 = (bf16[8,16,256]{2,1,0:T(8,128)(2,1)S(1)}, bf16[8,16,256]{2,1,0:T(8,128)(2,1)S(1)}, u32[]{:S(2)}, u32[]{:S(2)}) collective-permute-start(bf16[8,16,256]{2,1,0:T(8,128)(2,1)S(1)} %get-tuple-element.32), channel_id=1, source_target_pairs={{0,2},{2,0},{1,3},{3,1},{4,6},{6,4},{5,7},{7,5},{8,10},{10,8},{9,1... | collective-permute-start | bytes 196616 | tf_op jit(solution)/shard_map/ppermute | solution.py:35
  13.2 0.8 %copy-start.3 = (s32[32,2,64]{2,1,0:T(2,128)S(1)}, s32[32,2,64]{2,1,0:T(2,128)}, u32[]{:S(2)}) copy-start(s32[32,2,64]{2,1,0:T(2,128)} %param.7) | copy-start | bytes 49156
  13.9 0.7 %copy-start.4 = (s32[64]{0:T(128)S(1)}, s32[64]{0:T(128)}, u32[]{:S(2)}) copy-start(s32[64]{0:T(128)} %param.6) | copy-start | bytes 772
  23.8 11.3 %collective-permute-start.1 = (bf16[8,16,256]{2,1,0:T(8,128)(2,1)S(1)}, bf16[8,16,256]{2,1,0:T(8,128)(2,1)S(1)}, u32[]{:S(2)}, u32[]{:S(2)}) collective-permute-start(bf16[8,16,256]{2,1,0:T(8,128)(2,1)S(1)} %get-tuple-element.23), channel_id=1, source_target_pairs={{0,2},{2,0},{1,3},{3,1},{4,6},{6,4},{5,7},{7,5},{8,10},{10,8},{9,1... | collective-permute-start | bytes 196616 | tf_op jit(solution)/shard_map/ppermute | solution.py:35
  26.1 11.2 %collective-permute-start.3 = (bf16[2,64,256]{2,1,0:T(8,128)(2,1)S(1)}, bf16[2,64,256]{2,1,0:T(8,128)(2,1)S(1)}, u32[]{:S(2)}, u32[]{:S(2)}) collective-permute-start(bf16[2,64,256]{2,1,0:T(8,128)(2,1)S(1)} %inner.5), channel_id=1, source_target_pairs={{0,4},{4,0},{8,12},{12,8},{1,5},{5,1},{9,13},{13,9},{2,6},{6,2},{1... | collective-permute-start | bytes 196616 | tf_op jit(solution)/shard_map/ppermute | solution.py:640
  30.3 7.0 %collective-permute-start.5 = (bf16[2,64,256]{2,1,0:T(8,128)(2,1)S(1)}, bf16[2,64,256]{2,1,0:T(8,128)(2,1)S(1)}, u32[]{:S(2)}, u32[]{:S(2)}) collective-permute-start(bf16[2,64,256]{2,1,0:T(8,128)(2,1)S(1)} %inner.6), channel_id=1, source_target_pairs={{0,8},{4,12},{8,0},{12,4},{1,9},{5,13},{9,1},{13,5},{2,10},{6,14},... | collective-permute-start | bytes 196616 | tf_op jit(solution)/shard_map/ppermute | solution.py:640
  35.1 6.1 %collective-permute-start.7 = (bf16[2,64,256]{2,1,0:T(8,128)(2,1)S(1)}, bf16[2,64,256]{2,1,0:T(8,128)(2,1)S(1)}, u32[]{:S(2)}, u32[]{:S(2)}) collective-permute-start(bf16[2,64,256]{2,1,0:T(8,128)(2,1)S(1)} %inner.7), channel_id=1, source_target_pairs={{0,12},{4,8},{8,4},{12,0},{1,13},{5,9},{9,5},{13,1},{2,14},{6,10},... | collective-permute-start | bytes 196616 | tf_op jit(solution)/shard_map/ppermute | solution.py:640
where the time goes:
time: 42.7 us; the launch traced here: 42.2 us
  Pallas kernels  20.9 us (49%)
  starting transfers between devices  10.4 us (24%)
  local copies, waits for them, and re-layouts  5.04 us (12%)
  waiting for transfers between devices  4.85 us (11%)
  other arithmetic  0.96 us (2%)
    pallas_call x1, Pallas kernels, fast(): pl.pallas_call(functools.partial(tables_kernel, (pulses, channels, rx_cou...  8.65 us
    pallas_call x4, Pallas kernels, fast(): pl.pallas_call(inner_kernel, out_shape=shape((2, beams, piece_width), bf1...  8.44 us
    ppermute x5, starting transfers between devices, swapped(): lax.ppermute(x, axis, [(i, i ^ 1 << distance) for i in range(lax.axis_siz...  5.6 us
    unnamed x10, local copies, waits for them, and re-layouts  5.04 us
    ppermute x3, starting transfers between devices, fast(): lax.ppermute(image, 'pulse', [(i, i ^ distance) for i in range(pulse_coun...  4.82 us
    ppermute x3, waiting for transfers between devices, fast(): lax.ppermute(image, 'pulse', [(i, i ^ distance) for i in range(pulse_coun...  3.9 us
    pallas_call x1, Pallas kernels, fast(): pl.pallas_call(functools.partial(filter_kernel, (rng_count, pulse_count,...  2.17 us
    pallas_call x1, Pallas kernels, fast(): pl.pallas_call(outer_kernel, out_shape=shape((2, beams, piece_width), f32...  1.02 us
  transfers between devices with their start and end apart: 8, of which 2 were waited for; matrix products, arithmetic and copies ran while one was open for 0% of the time, Pallas kernels for 42%

commit v1 on v0

--- a/solution.py
+++ b/solution.py
@@ -235,6 +235,14 @@
     return pl.BlockSpec(memory_space=pltpu.VMEM)
 
 
+def hbm():
+    return pl.BlockSpec(memory_space=pltpu.HBM)
+
+
+def anywhere():
+    return pl.BlockSpec(memory_space=pl.ANY)
+
+
 def rx_bands_table(receivers):
     step = np.arange(RTAPS, dtype=np.float64)
     window = 0.5 - 0.5 * np.cos(full_turn * (step + 0.5) / RTAPS)
@@ -245,7 +253,8 @@
     inside = (offset >= 0) & (offset < RTAPS)
     place = np.clip(offset, 0, RTAPS - 1)
     bands = [
-        np.where(inside, taps[:, place], 0.0) for taps in (window * np.cos(angle), window * np.sin(angle))
+        np.where(inside, taps[:, place], 0.0)
+        for taps in (window * np.cos(angle), window * np.sin(angle))
     ]
     return np.concatenate(bands, axis=-1).astype(ml_dtypes.bfloat16)
 
@@ -258,9 +267,77 @@
     inside = (offset >= 0) & (offset < CTAPS)
     place = np.clip(offset, 0, CTAPS - 1)
     bands = [
-        np.where(inside, taps[place], 0.0) for taps in (np.cos(angle) * scale, -np.sin(angle) * scale)
+        np.where(inside, taps[place], 0.0)
+        for taps in (np.cos(angle) * scale, -np.sin(angle) * scale)
     ]
     return np.concatenate(bands, axis=-1).astype(ml_dtypes.bfloat16)
+
+
+def edge_kernel(echo_hbm, edge_ref, echo_ref, arrived):
+    length = echo_hbm.shape[3]
+    start = jnp.where(lax.axis_index("rng") == 0, length - HALO, 0)
+    start = pl.multiple_of(start, LANES)
+    edge = pltpu.make_async_copy(
+        echo_hbm.at[:, :, :, pl.ds(start, HALO)], edge_ref, arrived.at[0]
+    )
+    edge.start()
+    whole = pltpu.make_async_copy(echo_hbm, echo_ref, arrived.at[1])
+    whole.start()
+    edge.wait()
+    whole.wait()
+
+
+def filter_channel(windows, bands, pulses):
+    product = jnp.dot(windows, bands, preferred_element_type=jnp.float32)
+    product = product.reshape(-1, 2, pulses, 2 * LANES)
+    real = product[:, 0, :, :LANES] - product[:, 1, :, LANES:]
+    imag = product[:, 0, :, LANES:] + product[:, 1, :, :LANES]
+    return real, imag
+
+
+def interior_kernel(echo_ref, bands_hbm, filtered_ref, rows_in, rows_out, bands_ref, arrived):
+    _, pulses, channels, length = echo_ref.shape
+    rx_place = lax.axis_index("rx")
+    fetch = pltpu.make_async_copy(
+        bands_hbm.at[pl.ds(rx_place * channels, channels)], bands_ref, arrived
+    )
+    fetch.start()
+    tiles = length // LANES
+    group = 2 * pulses
+    empty = jnp.zeros(rows_in.shape[1:], jnp.float32)
+    rows_in[0] = empty
+    rows_in[tiles + 1] = empty
+    for part in range(2):
+        for pulse in range(pulses):
+            where = pl.ds(part * pulses + pulse, channels, stride=group)
+            block = echo_ref[part, pulse].astype(jnp.float32)
+            for tile in range(tiles):
+                rows_in[tile + 1, where, :] = block[:, tile * LANES : (tile + 1) * LANES]
+    fetch.wait()
+    lane = lax.broadcasted_iota(jnp.int32, (1, LANES), 1)
+    for channel in range(channels):
+        rows = rows_in[:, channel * group : (channel + 1) * group, :].astype(jnp.bfloat16)
+        windows = jnp.concatenate(
+            [rows[:-1].reshape(-1, LANES), rows[1:].reshape(-1, LANES)], axis=1
+        )
+        real, imag = filter_channel(windows, bands_ref[channel], pulses)
+        for tile in range(tiles + 1):
+            tile_re, tile_im = real[tile], imag[tile]
+            if tile == 0:
+                tile_re = jnp.where(lane >= LANES - RTAPS // 2, tile_re, 0.0)
+                tile_im = jnp.where(lane >= LANES - RTAPS // 2, tile_im, 0.0)
+            if tile == tiles:
+                tile_re = jnp.where(lane < LANES - RTAPS // 2, tile_re, 0.0)
+                tile_im = jnp.where(lane < LANES - RTAPS // 2, tile_im, 0.0)
+            rows_out[tile, pl.ds(channel, pulses, stride=2 * channels), :] = tile_re
+            rows_out[tile, pl.ds(channels + channel, pulses, stride=2 * channels), :] = tile_im
+    rows = filtered_ref.shape[0]
+    nothing = jnp.zeros((rows, (HALO_TILES - 1) * LANES), jnp.bfloat16)
+    filtered_ref[:, : (HALO_TILES - 1) * LANES] = nothing
+    filtered_ref[:, (HALO_TILES + tiles) * LANES :] = nothing
+    for tile in range(tiles + 1):
+        spot = (HALO_TILES - 1 + tile) * LANES
+        filtered_ref[:, spot : spot + LANES] = rows_out[tile].astype(jnp.bfloat16)
 
 
 def chirp_piece(filtered_ref, chirp_ref, starts, out_ref):
@@ -280,82 +357,65 @@
         ).astype(jnp.bfloat16)
 
 
-def filter_kernel(sizes, echo_ref, edge_ref, bands_hbm, chirp_ref, *rest):
-    rng_count, piece_count, piece_tiles = sizes
-    send_refs, (filtered_ref, rows_in, rows_out, bands_ref, arrived) = (
-        rest[:piece_count],
-        rest[piece_count:],
-    )
+def chirp_half(filtered_ref, chirp_ref, owner, piece_tiles, out_refs):
+    pulse_place = lax.axis_index("pulse")
+    piece_count = sum(ref.shape[0] for ref in out_refs)
+    distance = piece_count - 1
+    for out_ref in out_refs:
+        for index in range(out_ref.shape[0]):
+            piece = jnp.bitwise_xor(pulse_place, distance)
+            first = owner * (piece_count * piece_tiles) + piece * piece_tiles
+            starts = [pl.multiple_of((first + t) * LANES, LANES) for t in range(piece_tiles)]
+            chirp_piece(filtered_ref, chirp_ref, starts, out_ref.at[index])
+            distance -= 1
+
+
+def send_kernel(piece_tiles, inner_ref, echo_ref, edge_ref, bands_hbm, chirp_hbm, *rest):
+    *send_refs, filtered_ref, chirp_ref, rows_in, rows_out, bands_ref, arrived = rest
     _, pulses, channels, length = echo_ref.shape
     rng_place = lax.axis_index("rng")
     rx_place = lax.axis_index("rx")
-    pulse_place = lax.axis_index("pulse")
     fetch = pltpu.make_async_copy(
-        bands_hbm.at[pl.ds(rx_place * channels, channels)], bands_ref, arrived
+        bands_hbm.at[pl.ds(rx_place * channels, channels)], bands_ref, arrived.at[0]
     )
     fetch.start()
+    fetch_chirp = pltpu.make_async_copy(chirp_hbm, chirp_ref, arrived.at[1])
+    fetch_chirp.start()
+    filtered_ref[...] = inner_ref[...]
     tiles = length // LANES
     group = 2 * pulses
-    has_low = jnp.where(rng_place > 0, 1.0, 0.0).astype(jnp.float32)
-    has_high = jnp.where(rng_place < rng_count - 1, 1.0, 0.0).astype(jnp.float32)
+    lowest = rng_place == 0
     for part in range(2):
         for pulse in range(pulses):
             where = pl.ds(part * pulses + pulse, channels, stride=group)
             edge = edge_ref[part, pulse].astype(jnp.float32)
-            block = echo_ref[part, pulse].astype(jnp.float32)
-            for tile in range(HALO_TILES):
-                span = edge[:, tile * LANES : (tile + 1) * LANES]
-                rows_in[tile, where, :] = span * has_low
-                rows_in[HALO_TILES + tiles + tile, where, :] = span * has_high
-            for tile in range(tiles):
-                span = block[:, tile * LANES : (tile + 1) * LANES]
-                rows_in[HALO_TILES + tile, where, :] = span
+            near_low = echo_ref[part, pulse, :, :LANES].astype(jnp.float32)
+            near_high = echo_ref[part, pulse, :, length - LANES :].astype(jnp.float32)
+            pieces = [edge[:, t * LANES : (t + 1) * LANES] for t in range(HALO_TILES)]
+            for tile in range(HALO_TILES + 1):
+                high = near_high if tile == 0 else pieces[tile - 1]
+                low = near_low if tile == HALO_TILES else pieces[tile]
+                rows_in[tile, where, :] = jnp.where(lowest, high, low)
     fetch.wait()
-    out_tiles = tiles + 2 * HALO_TILES - 1
-    lane = lax.broadcasted_iota(jnp.int32, (1, LANES), 1)
-    total = rng_count * length
     for channel in range(channels):
         rows = rows_in[:, channel * group : (channel + 1) * group, :].astype(jnp.bfloat16)
         windows = jnp.concatenate(
-            [
-                rows[:-1].reshape(out_tiles * group, LANES),
-                rows[1:].reshape(out_tiles * group, LANES),
-            ],
-            axis=1,
-        )
-        product = jnp.dot(windows, bands_ref[channel], preferred_element_type=jnp.float32)
-        product = product.reshape(out_tiles, group, 2 * LANES)
-        for tile in range(out_tiles):
-            block = product[tile]
-            real = block[:pulses, :LANES] - block[pulses:, LANES:]
-            imag = block[:pulses, LANES:] + block[pulses:, :LANES]
-            if tile <= HALO_TILES - 1 or tile >= out_tiles - HALO_TILES:
-                spot = rng_place * length + (tile - HALO_TILES) * LANES + RTAPS // 2 + lane
-                inside = (spot >= 0) & (spot < total)
-                real = jnp.where(inside, real, 0.0)
-                imag = jnp.where(inside, imag, 0.0)
-            rows_out[tile, pl.ds(channel, pulses, stride=2 * channels), :] = real
-            rows_out[tile, pl.ds(channels + channel, pulses, stride=2 * channels), :] = imag
-    for tile in range(out_tiles):
-        filtered_ref[:, tile * LANES : (tile + 1) * LANES] = rows_out[tile].astype(jnp.bfloat16)
-    base = (1 - rx_place) * (piece_count * piece_tiles)
-    for distance in range(piece_count):
-        piece = jnp.bitwise_xor(pulse_place, distance)
-        first = base + piece * piece_tiles
-        starts = [pl.multiple_of((first + t) * LANES, LANES) for t in range(piece_tiles)]
-        chirp_piece(filtered_ref, chirp_ref, starts, send_refs[distance])
-
-
-def keep_kernel(sizes, filtered_ref, chirp_ref, *keep_refs):
-    piece_count, piece_tiles = sizes
-    rx_place = lax.axis_index("rx")
-    pulse_place = lax.axis_index("pulse")
-    base = rx_place * (piece_count * piece_tiles)
-    for distance in range(piece_count):
-        piece = jnp.bitwise_xor(pulse_place, distance)
-        first = base + piece * piece_tiles
-        starts = [pl.multiple_of((first + t) * LANES, LANES) for t in range(piece_tiles)]
-        chirp_piece(filtered_ref, chirp_ref, starts, keep_refs[distance])
+            [rows[:-1].reshape(-1, LANES), rows[1:].reshape(-1, LANES)], axis=1
+        )
+        real, imag = filter_channel(windows, bands_ref[channel], pulses)
+        for tile in range(HALO_TILES):
+            rows_out[tile, pl.ds(channel, pulses, stride=2 * channels), :] = real[tile]
+            rows_out[tile, pl.ds(channels + channel, pulses, stride=2 * channels), :] = imag[tile]
+    first = jnp.where(lowest, tiles + HALO_TILES - 1, 0)
+    for tile in range(HALO_TILES):
+        start = pl.multiple_of((first + tile) * LANES, LANES)
+        filtered_ref[:, pl.ds(start, LANES)] = rows_out[tile].astype(jnp.bfloat16)
+    fetch_chirp.wait()
+    chirp_half(filtered_ref, chirp_ref, 1 - rx_place, piece_tiles, send_refs)
+
+
+def keep_kernel(piece_tiles, filtered_ref, chirp_ref, keep_ref):
+    chirp_half(filtered_ref, chirp_ref, lax.axis_index("rx"), piece_tiles, [keep_ref])
 
 
 def turn_parts(step):
@@ -382,28 +442,20 @@
 
 
 def interp_matrix(codes_ref, row):
+    beams = codes_ref.shape[1]
     code = as_column(codes_ref[pl.ds(row, 1), :])
-    beams = codes_ref.shape[1]
-    shift = jnp.right_shift(code, 2) - 1
-    part = jnp.bitwise_and(code, 3).astype(jnp.float32) * 0.25
-    weights = (
-        -part * (part - 1.0) * (part - 2.0) * (1.0 / 6.0),
-        (part + 1.0) * (part - 1.0) * (part - 2.0) * 0.5,
-        -(part + 1.0) * part * (part - 2.0) * 0.5,
-        (part + 1.0) * part * (part - 1.0) * (1.0 / 6.0),
-    )
     angle_bin = lax.broadcasted_iota(jnp.int32, (beams, beams), 0)
     column = lax.broadcasted_iota(jnp.int32, (beams, beams), 1)
-    tap = jnp.bitwise_and(column - angle_bin - shift + 1, beams - 1)
-    matrix = jnp.zeros((beams, beams), jnp.float32)
-    for index in range(4):
-        matrix = jnp.where(tap == index, weights[index], matrix)
+    half = 2 * beams
+    away = jnp.bitwise_and(4 * (column - angle_bin + 1) - code + half, 4 * beams - 1) - half
+    away = jnp.abs(away.astype(jnp.float32)) * 0.25
+    near = (1.0 - away * away) * (2.0 - away) * 0.5
+    far = (1.0 - away) * (2.0 - away) * (3.0 - away) * (1.0 / 6.0)
+    matrix = jnp.where(away < 1.0, near, jnp.where(away < 2.0, far, 0.0))
     return matrix.astype(jnp.bfloat16)
 
 
-def tables_kernel(
-    sizes, angle_ref, codes_ref, first_ref, inner_ref, outer_ref, phase_ref, outer_phase_ref
-):
+def tables_kernel(sizes, angle_ref, codes_ref, first_ref, inner_ref, phase_ref):
     pulses, channels, rx_count, width = sizes
     rng_place = lax.axis_index("rng")
     rx_place = lax.axis_index("rx")
@@ -445,7 +497,7 @@
     slot = 0
     now = pulses
     while now > 1:
-        factors.extend(now * piece_count + pulse_place * now + i + 1 for i in range(now))
+        factors.append(now * piece_count + pulse_place * now + 1)
         if now < pulses:
             for index in range(now):
                 inner_ref[slot] = interp_matrix(
@@ -455,17 +507,27 @@
         now //= 2
     lane = lax.broadcasted_iota(jnp.int32, (1, piece_width), 1)
     block = (rng_place * rx_count + rx_place) * width + 1
-
-    def one_piece(distance, carry):
-        piece = jnp.bitwise_xor(pulse_place, distance)
+    for index in range(piece_count):
+        piece = jnp.bitwise_xor(pulse_place, piece_count - 1 - index)
         base = jnp.bitwise_and(angle * (block + piece * piece_width + lane), 1023)
-        for index, factor in enumerate(factors):
+        real, imag = turn_parts(base)
+        phase_ref[index, 0, 0] = real
+        phase_ref[index, 0, 1] = imag
+        for slot, factor in enumerate(factors):
             real, imag = turn_parts(jnp.bitwise_and(base * factor, 1023))
-            phase_ref[distance, index, 0] = real * half_root
-            phase_ref[distance, index, 1] = imag * half_root
-        return carry
-
-    lax.fori_loop(0, piece_count, one_piece, 0)
+            phase_ref[index, slot + 1, 0] = real * half_root
+            phase_ref[index, slot + 1, 1] = imag * half_root
+
+
+def outer_tables_kernel(sizes, angle_ref, codes_ref, after_ref, outer_ref, phase_ref):
+    rx_count, width, piece_count = sizes
+    rng_place = lax.axis_index("rng")
+    rx_place = lax.axis_index("rx")
+    pulse_place = lax.axis_index("pulse")
+    piece_width = phase_ref.shape[3]
+    angle = as_column(angle_ref[...])
+    lane = lax.broadcasted_iota(jnp.int32, (1, piece_width), 1)
+    block = (rng_place * rx_count + rx_place) * width + 1
     base = jnp.bitwise_and(angle * (block + pulse_place * piece_width + lane), 1023)
     slot = 0
     now = piece_count
@@ -473,8 +535,8 @@
         for index in range(now):
             outer_ref[slot] = interp_matrix(codes_ref, now + index)
             real, imag = turn_parts(jnp.bitwise_and(base * (now + index + 1), 1023))
-            outer_phase_ref[slot, 0] = real * half_root
-            outer_phase_ref[slot, 1] = imag * half_root
+            phase_ref[slot, 0] = real * half_root
+            phase_ref[slot, 1] = imag * half_root
             slot += 1
         now //= 2
 
@@ -483,45 +545,77 @@
     return phase_re * real - phase_im * imag, phase_im * real + phase_re * imag
 
 
-def inner_kernel(own_ref, other_ref, first_ref, inner_ref, phase_ref, out_ref):
-    pulses = own_ref.shape[0]
+ROWS = 8
+
+
+def inner_kernel(index, keep_ref, other_ref, first_ref, inner_ref, phase_ref, *rest):
+    out_ref, moved_ref, picture_ref, level_ref = rest[-4:]
+    pulses = keep_ref.shape[1]
     beams = inner_ref.shape[1]
-    terms = []
-    for index in range(pulses):
-        rows = jnp.concatenate([own_ref[index], other_ref[index]], axis=0)
-        moved = jnp.dot(
-            first_ref[index],
+    columns = keep_ref.shape[3]
+    other = index % other_ref.shape[0]
+    for image in range(pulses):
+        rows = jnp.concatenate([keep_ref[index, image], other_ref[other, image]], axis=0)
+        moved_ref[image] = jnp.dot(
+            first_ref[image],
             jnp.concatenate([rows, rows], axis=0),
             preferred_element_type=jnp.float32,
         )
-        terms.append(
-            turned(moved[:beams], moved[beams:], phase_ref[0, index, 0], phase_ref[0, index, 1])
-        )
-        if index & 1:
-            right, left = terms.pop(), terms.pop()
-            terms.append((left[0] + right[0], left[1] + right[1]))
+
+    def merge(count, level, read, write):
+        for row in range(0, beams, ROWS):
+            span = slice(row, row + ROWS)
+            step = (phase_ref[index, 0, 0, span], phase_ref[index, 0, 1, span])
+            phase = (phase_ref[index, level, 0, span], phase_ref[index, level, 1, span])
+            for image in range(count):
+                term = turned(*read(image, row), *phase)
+                if image & 1:
+                    write(image // 2, row, left[0] + term[0], left[1] + term[1])
+                left = term
+                if image < count - 1:
+                    phase = turned(*phase, *step)
+
+    def write_picture(image, row, real, imag):
+        picture_ref[image, row : row + ROWS, :columns] = real
+        picture_ref[image, row : row + ROWS, columns:] = imag
+
+    def write_out(image, row, real, imag):
+        picture_ref[0, row : row + ROWS, :columns] = real
+        picture_ref[0, row : row + ROWS, columns:] = imag
+
+    merge(
+        pulses,
+        1,
+        lambda image, row: (
+            moved_ref[image, row : row + ROWS],
+            moved_ref[image, beams + row : beams + row + ROWS],
+        ),
+        write_picture,
+    )
     slot = 0
-    phase_slot = pulses
-    while len(terms) > 1:
-        pictures, terms = terms, []
-        for index, (real, imag) in enumerate(pictures):
-            matrix = inner_ref[slot]
-            moved_re = jnp.dot(
-                matrix, real.astype(jnp.bfloat16), preferred_element_type=jnp.float32
+    level = 2
+    count = pulses // 2
+    while count > 1:
+        for image in range(count):
+            level_ref[image] = jnp.dot(
+                inner_ref[slot],
+                picture_ref[image].astype(jnp.bfloat16),
+                preferred_element_type=jnp.float32,
             )
-            moved_im = jnp.dot(
-                matrix, imag.astype(jnp.bfloat16), preferred_element_type=jnp.float32
-            )
-            terms.append(
-                turned(moved_re, moved_im, phase_ref[0, phase_slot, 0], phase_ref[0, phase_slot, 1])
-            )
-            if index & 1:
-                right, left = terms.pop(), terms.pop()
-                terms.append((left[0] + right[0], left[1] + right[1]))
             slot += 1
-            phase_slot += 1
-    out_ref[0] = terms[0][0].astype(jnp.bfloat16)
-    out_ref[1] = terms[0][1].astype(jnp.bfloat16)
+        merge(
+            count,
+            level,
+            lambda image, row: (
+                level_ref[image, row : row + ROWS, :columns],
+                level_ref[image, row : row + ROWS, columns:],
+            ),
+            write_picture,
+        )
+        count //= 2
+        level += 1
+    out_ref[0] = picture_ref[0, :, :columns].astype(jnp.bfloat16)
+    out_ref[1] = picture_ref[0, :, columns:].astype(jnp.bfloat16)
 
 
 def outer_kernel(outer_ref, phase_ref, *rest):
@@ -554,93 +648,126 @@
     out_ref[1] = pictures[0][1]
 
 
-PARAMS = dict(compiler_params=pltpu.CompilerParams(vmem_limit_bytes=48 * 1024 * 1024))
+PARAMS = dict(compiler_params=pltpu.CompilerParams(vmem_limit_bytes=40 * 1024 * 1024))
 
 
 def fast(echoes, beam_angle, interp_table):
-    rng_count = lax.axis_size("rng")
     rx_count = lax.axis_size("rx")
     pulse_count = lax.axis_size("pulse")
-    rng_place = lax.axis_index("rng")
     _, pulses, channels, length = echoes.shape
     beams = beam_angle.shape[0]
     width = length // rx_count
     piece_width = width // pulse_count
     piece_tiles = piece_width // LANES
     rows = 2 * channels
+    group = 2 * pulses
     bands = jnp.asarray(rx_bands_table(channels * rx_count))
     chirp = jnp.asarray(chirp_bands_table())
+    angles = beam_angle.reshape(1, beams)
+    codes = interp_table.reshape(-1, beams)
     bf16 = jnp.bfloat16
     f32 = jnp.float32
-    edge = jnp.where(rng_place == 0, echoes[..., length - HALO :], echoes[..., :HALO])
+    shape = jax.ShapeDtypeStruct
+    edge, echoes = pl.pallas_call(
+        edge_kernel,
+        out_shape=[shape(echoes.shape[:3] + (HALO,), bf16), shape(echoes.shape, bf16)],
+        in_specs=[hbm()],
+        out_specs=[vmem(), vmem()],
+        scratch_shapes=[pltpu.SemaphoreType.DMA((2,))],
+        name="edge",
+        **PARAMS,
+    )(echoes)
     edge = swapped(edge, "rng", 0)
-    shape = jax.ShapeDtypeStruct
-    piece_shape = shape((pulses, rows, piece_width), bf16)
-    tiles = length // LANES + 2 * HALO_TILES
-    filtered_shape = shape((rows * pulses, (tiles - 1) * LANES), bf16)
-    *sent, filtered = pl.pallas_call(
-        functools.partial(filter_kernel, (rng_count, pulse_count, piece_tiles)),
-        out_shape=[piece_shape] * pulse_count + [filtered_shape],
-        in_specs=[vmem(), vmem(), pl.BlockSpec(memory_space=pl.ANY), vmem()],
-        out_specs=[vmem()] * (pulse_count + 1),
+    tiles = length // LANES
+    filtered_shape = shape((rows * pulses, (tiles + 2 * HALO_TILES - 1) * LANES), bf16)
+    bands_scratch = pltpu.VMEM((channels,) + bands.shape[1:], bf16)
+    filtered = pl.pallas_call(
+        interior_kernel,
+        out_shape=filtered_shape,
+        in_specs=[vmem(), hbm()],
+        out_specs=vmem(),
         scratch_shapes=[
-            pltpu.VMEM((tiles, rows * pulses, LANES), f32),
-            pltpu.VMEM((tiles - 1, rows * pulses, LANES), f32),
-            pltpu.VMEM((channels,) + bands.shape[1:], bf16),
+            pltpu.VMEM((tiles + 2, channels * group, LANES), f32),
+            pltpu.VMEM((tiles + 1, rows * pulses, LANES), f32),
+            bands_scratch,
             pltpu.SemaphoreType.DMA,
         ],
-        name="filter",
+        name="interior",
         **PARAMS,
-    )(echoes, edge, bands, chirp)
+    )(echoes, bands)
+    chunk = max(1, pulse_count // 2)
+    piece_shape = (pulses, rows, piece_width)
+    sent_shape = shape((chunk,) + piece_shape, bf16)
+    *sent, filtered, chirp = pl.pallas_call(
+        functools.partial(send_kernel, piece_tiles),
+        out_shape=[sent_shape] * (pulse_count // chunk)
+        + [filtered_shape, shape(chirp.shape, bf16)],
+        in_specs=[vmem(), vmem(), vmem(), hbm(), hbm()],
+        out_specs=[vmem()] * (pulse_count // chunk + 2),
+        scratch_shapes=[
+            pltpu.VMEM((HALO_TILES + 1, channels * group, LANES), f32),
+            pltpu.VMEM((HALO_TILES, rows * pulses, LANES), f32),
+            bands_scratch,
+            pltpu.SemaphoreType.DMA((2,)),
+        ],
+        name="send",
+        **PARAMS,
+    )(filtered, echoes, edge, bands, chirp)
     received = [swapped(piece, "rx", 0) for piece in sent]
     kept = pl.pallas_call(
-        functools.partial(keep_kernel, (pulse_count, piece_tiles)),
-        out_shape=[piece_shape] * pulse_count,
+        functools.partial(keep_kernel, piece_tiles),
+        out_shape=shape((pulse_count,) + piece_shape, bf16),
         in_specs=[vmem()] * 2,
-        out_specs=[vmem()] * pulse_count,
+        out_specs=vmem(),
         name="keep",
         **PARAMS,
     )(filtered, chirp)
-    inner_count = pulses - 2
-    outer_count = 2 * pulse_count - 2
-    first, inner, outer, phase, outer_phase = pl.pallas_call(
+    levels = pulses.bit_length() - 1
+    first, inner, phase = pl.pallas_call(
         functools.partial(tables_kernel, (pulses, channels, rx_count, width)),
         out_shape=[
             shape((pulses, 2 * beams, 8 * channels), bf16),
-            shape((inner_count, beams, beams), bf16),
+            shape((pulses - 2, beams, beams), bf16),
+            shape((pulse_count, levels + 1, 2, beams, piece_width), f32),
+        ],
+        in_specs=[vmem()] * 2,
+        out_specs=[vmem()] * 3,
+        name="tables",
+        **PARAMS,
+    )(angles, codes)
+    images = []
+    after = []
+    for index in range(pulse_count):
+        distance = pulse_count - 1 - index
+        image = pl.pallas_call(
+            functools.partial(inner_kernel, index),
+            out_shape=shape((2, beams, piece_width), bf16),
+            in_specs=[vmem()] * 5 + [anywhere()] * len(after),
+            out_specs=vmem(),
+            scratch_shapes=[
+                pltpu.VMEM((pulses, 2 * beams, piece_width), f32),
+                pltpu.VMEM((pulses // 2, beams, 2 * piece_width), f32),
+                pltpu.VMEM((pulses // 2, beams, 2 * piece_width), f32),
+            ],
+            name="inner",
+            **PARAMS,
+        )(kept, received[index // chunk], first, inner, phase, *after)
+        after = [image]
+        if distance:
+            image = lax.ppermute(image, "pulse", [(i, i ^ distance) for i in range(pulse_count)])
+        images.insert(0, image)
+    outer_count = 2 * pulse_count - 2
+    outer, outer_phase = pl.pallas_call(
+        functools.partial(outer_tables_kernel, (rx_count, width, pulse_count)),
+        out_shape=[
             shape((outer_count, beams, beams), bf16),
-            shape((pulse_count, 2 * pulses - 2, 2, beams, piece_width), f32),
             shape((outer_count, 2, beams, piece_width), f32),
         ],
-        in_specs=[vmem()] * 2,
-        out_specs=[vmem()] * 5,
-        name="tables",
+        in_specs=[vmem(), vmem(), anywhere()],
+        out_specs=[vmem()] * 2,
+        name="outer_tables",
         **PARAMS,
-    )(beam_angle.reshape(1, beams), interp_table.reshape(-1, beams))
-    images = []
-    for distance in reversed(range(pulse_count)):
-        image = pl.pallas_call(
-            inner_kernel,
-            out_shape=shape((2, beams, piece_width), bf16),
-            grid=(1,),
-            in_specs=[
-                vmem(),
-                vmem(),
-                vmem(),
-                vmem(),
-                pl.BlockSpec(
-                    (1,) + phase.shape[1:], lambda step, distance=distance: (distance, 0, 0, 0, 0)
-                ),
-            ],
-            out_specs=vmem(),
-            name="inner",
-            **PARAMS,
-        )(kept[distance], received[distance], first, inner, phase)
-        if distance:
-            image = lax.ppermute(
-                image, "pulse", [(i, i ^ distance) for i in range(pulse_count)]
-            )
-        images.insert(0, image)
+    )(angles, codes, *after)
     return pl.pallas_call(
         outer_kernel,
         out_shape=shape((2, beams, piece_width), f32),

time: 42.7 us -> 27.9 us (0.65)
  Pallas kernels: 20.9 us -> 9.88 us
  starting transfers between devices: 10.4 us -> 7.65 us
  waiting for transfers between devices: 4.85 us -> 7.41 us
  local copies, waits for them, and re-layouts: 5.04 us -> 2.65 us
  other arithmetic: 0.96 us -> 0 us
    pallas_call x1, Pallas kernels: 8.65 us -> 2.1 us  [fast(): pl.pallas_call(functools.partial(tables_kernel, (pulses, channels, rx_cou...]
    pallas_call x6 -> x9, Pallas kernels: 11.2 us -> 6.75 us  [the longest x4 2.73 us: fast(): pl.pallas_call(functools.partial(inner_kernel, index), out_shape=shape((2...]
    ppermute x5 -> x3, starting transfers between devices: 5.6 us -> 3.16 us  [swapped(): lax.ppermute(x, axis, [(i, i ^ 1 << distance) for i in range(lax.axis_siz...]
    unnamed x10, local copies, waits for them, and re-layouts: 5.04 us -> 2.65 us
    ppermute x5 -> x3, waiting for transfers between devices: 0.95 us -> 2.8 us  [swapped(): lax.ppermute(x, axis, [(i, i ^ 1 << distance) for i in range(lax.axis_siz...]
    select_n x1 -> x0, other arithmetic: 0.96 us -> none  [fast(): jnp.where(rng_place == 0, echoes[..., length - HALO:], echoes[..., :HALO])]
    ppermute x3, waiting for transfers between devices: 3.9 us -> 4.61 us  [fast(): lax.ppermute(image, 'pulse', [(i, i ^ distance) for i in range(pulse_coun...]
  transfers between devices with their start and end apart: 8 -> 6, of which waited for: 2 -> 4; matrix products, arithmetic and copies ran while one was open for 0% -> 0% of each run, Pallas kernels for 42% -> 24%
where the time goes in v1:
time: 27.9 us; the launch traced here: 27.7 us
  Pallas kernels  9.88 us (35%)
  starting transfers between devices  7.65 us (27%)
  waiting for transfers between devices  7.41 us (27%)
  local copies, waits for them, and re-layouts  2.65 us (9%)
    ppermute x3, waiting for transfers between devices, fast(): lax.ppermute(image, 'pulse', [(i, i ^ distance) for i in range(pulse_coun...  4.61 us
    ppermute x3, starting transfers between devices, fast(): lax.ppermute(image, 'pulse', [(i, i ^ distance) for i in range(pulse_coun...  4.49 us
    ppermute x3, starting transfers between devices, swapped(): lax.ppermute(x, axis, [(i, i ^ 1 << distance) for i in range(lax.axis_siz...  3.16 us
    ppermute x3, waiting for transfers between devices, swapped(): lax.ppermute(x, axis, [(i, i ^ 1 << distance) for i in range(lax.axis_siz...  2.8 us
    pallas_call x4, Pallas kernels, fast(): pl.pallas_call(functools.partial(inner_kernel, index), out_shape=shape((2...  2.73 us
    unnamed x10, local copies, waits for them, and re-layouts  2.65 us
    pallas_call x1, Pallas kernels, fast(): pl.pallas_call(functools.partial(tables_kernel, (pulses, channels, rx_cou...  2.1 us
    pallas_call x1, Pallas kernels, fast(): pl.pallas_call(functools.partial(send_kernel, piece_tiles), out_shape=[se...  1.35 us
  transfers between devices with their start and end apart: 6, of which 4 were waited for; matrix products, arithmetic and copies ran while one was open for 0% of the time, Pallas kernels for 24%

profile of v1, /device:TPU:0, one launch (start us, length us, event | category | flops | bytes accessed | tf_op | source)
XLA Modules:
  0.0 27.7 jit_solution(12341759938804976754)
XLA Ops:
  0.0 0.0 copy-start.1
  0.0 1.0 %copy-done.1 = bf16[2,8,8,2048]{3,2,1,0:T(8,128)(2,1)S(1)} copy-done((bf16[2,8,8,2048]{3,2,1,0:T(8,128)(2,1)S(1)}, bf16[2,8,8,2048]{3,2,1,0:T(8,128)(2,1)}, u32[]{:S(2)}) %copy-start.1) | copy-done | bytes 524312
  1.0 0.0 copy-start.2
  1.0 0.1 edge.1
  1.1 0.5 %collective-permute-start = (bf16[2,8,8,384]{3,2,1,0:T(8,128)(2,1)S(1)}, bf16[2,8,8,384]{3,2,1,0:T(8,128)(2,1)S(1)}, u32[]{:S(2)}, u32[]{:S(2)}) collective-permute-start(bf16[2,8,8,384]{3,2,1,0:T(8,128)(2,1)S(1)} %get-tuple-element.17), channel_id=1, source_target_pairs={{0,1},{1,0},{2,3},{3,2},{4,5},{5,4},{6,7},{7,6},{8,9},{9,8},{10,11... | collective-permute-start | bytes 294920 | tf_op jit(solution)/shard_map/ppermute | solution.py:35
  1.6 0.0 copy-start
  1.6 1.6 %copy-done = bf16[16,256,256]{2,1,0:T(8,128)(2,1)S(1)} copy-done((bf16[16,256,256]{2,1,0:T(8,128)(2,1)S(1)}, bf16[16,256,256]{2,1,0:T(8,128)(2,1)}, u32[]{:S(2)}) %copy-start) | copy-done | bytes 2097176
  3.2 1.3 %interior.1.inner_ref = bf16[128,2688]{1,0:T(8,128)(2,1)S(1)} custom-call(bf16[2,8,8,2048]{3,2,1,0:T(8,128)(2,1)S(1)} %get-tuple-element.16.echo_ref, bf16[16,256,256]{2,1,0:T(8,128)(2,1)S(1)} %copy-done), custom_call_target="tpu_custom_call" | custom-call | tf_op jit(solution)/shard_map/interior/pallas_call | solution.py:684
  4.5 0.0 copy-start.3
  4.5 0.0 copy-start.4
  4.5 0.0 collective-permute-done.edge_ref
  4.5 0.0 copy-done.2
  4.6 1.4 %send.1 = (bf16[2,8,16,256]{3,2,1,0:T(8,128)(2,1)S(1)}, bf16[2,8,16,256]{3,2,1,0:T(8,128)(2,1)S(1)}, bf16[128,2688]{1,0:T(8,128)(2,1)S(1)}, bf16[768,256]{1,0:T(8,128)(2,1)S(1)}) custom-call(bf16[128,2688]{1,0:T(8,128)(2,1)S(1)} %interior.1.inner_ref, bf16[2,8,8,2048]{3,2,1,0:T(8,128)(2,1)S(1)} %get-tuple-element.16.echo_ref, ...), custom_call_target="tpu_custom_call" | custom-call | tf_op jit(solution)/shard_map/send/pallas_call | solution.py:701
  5.9 2.6 %collective-permute-start.2 = (bf16[2,8,16,256]{3,2,1,0:T(8,128)(2,1)S(1)}, bf16[2,8,16,256]{3,2,1,0:T(8,128)(2,1)S(1)}, u32[]{:S(2)}, u32[]{:S(2)}) collective-permute-start(bf16[2,8,16,256]{3,2,1,0:T(8,128)(2,1)S(1)} %get-tuple-element.24), channel_id=1, source_target_pairs={{0,2},{2,0},{1,3},{3,1},{4,6},{6,4},{5,7},{7,5},{8,10},{10,8},{9,1... | collective-permute-start | bytes 393224 | tf_op jit(solution)/shard_map/ppermute | solution.py:35
  8.5 0.1 collective-permute-start.1
  8.6 0.0 copy-done.3
  8.6 0.0 copy-done.4
  8.6 2.1 %tables.1 = (bf16[8,128,64]{2,1,0:T(8,128)(2,1)S(1)}, bf16[6,64,64]{2,1,0:T(8,128)(2,1)S(1)}, f32[4,4,2,64,256]{4,3,2,1,0:T(8,128)S(1)}) custom-call(s32[1,64]{1,0:T(1,128)S(1)} %bitcast.4, s32[64,64]{1,0:T(8,128)S(1)} %bitcast.2), custom_call_target="tpu_custom_call" | custom-call | tf_op jit(solution)/shard_map/tables/pallas_call | solution.py:726
  10.7 0.6 %keep.1.keep_ref = bf16[4,8,16,256]{3,2,1,0:T(8,128)(2,1)S(1)} custom-call(bf16[128,2688]{1,0:T(8,128)(2,1)S(1)} %get-tuple-element.18.filtered_ref, bf16[768,256]{1,0:T(8,128)(2,1)S(1)} %get-tuple-element.19.chirp_ref), custom_call_target="tpu_custom_call" | custom-call | tf_op jit(solution)/shard_map/keep/pallas_call | solution.py:717
  11.3 1.6 %collective-permute-done.2.other_ref = bf16[2,8,16,256]{3,2,1,0:T(8,128)(2,1)S(1)} collective-permute-done((bf16[2,8,16,256]{3,2,1,0:T(8,128)(2,1)S(1)}, bf16[2,8,16,256]{3,2,1,0:T(8,128)(2,1)S(1)}, u32[]{:S(2)}, u32[]{:S(2)}) %collective-permute-start.2) | collective-permute-done | bytes 131104 | tf_op jit(solution)/shard_map/ppermute | solution.py:35
  12.8 0.7 %inner.4.rest_0_ = bf16[2,64,256]{2,1,0:T(8,128)(2,1)S(1)} custom-call(bf16[4,8,16,256]{3,2,1,0:T(8,128)(2,1)S(1)} %keep.1.keep_ref, bf16[2,8,16,256]{3,2,1,0:T(8,128)(2,1)S(1)} %collective-permute-done.2.other_ref, bf16[8,128,64]{2,1,0:T(8,128)(2,1)S(1)} %get-tuple-element.21.first_ref, bf16[6,64,64]{2,1,0:T(8,128)(2,1)S(1)} %get-tuple-element.22.inner_ref, ...), custom_call_target="tpu_custom_call" | custom-call | tf_op jit(solution)/shard_map/inner/pallas_call | solution.py:742
  13.5 0.7 %inner.5.rest_0_ = bf16[2,64,256]{2,1,0:T(8,128)(2,1)S(1)} custom-call(bf16[4,8,16,256]{3,2,1,0:T(8,128)(2,1)S(1)} %keep.1.keep_ref, bf16[2,8,16,256]{3,2,1,0:T(8,128)(2,1)S(1)} %collective-permute-done.2.other_ref, bf16[8,128,64]{2,1,0:T(8,128)(2,1)S(1)} %get-tuple-element.21.first_ref, bf16[6,64,64]{2,1,0:T(8,128)(2,1)S(1)} %get-tuple-element.22.inner_ref, ...), custom_call_target="tpu_custom_call" | custom-call | tf_op jit(solution)/shard_map/inner/pallas_call | solution.py:742
  14.2 1.2 %collective-permute-done.1.other_ref = bf16[2,8,16,256]{3,2,1,0:T(8,128)(2,1)S(1)} collective-permute-done((bf16[2,8,16,256]{3,2,1,0:T(8,128)(2,1)S(1)}, bf16[2,8,16,256]{3,2,1,0:T(8,128)(2,1)S(1)}, u32[]{:S(2)}, u32[]{:S(2)}) %collective-permute-start.1) | collective-permute-done | bytes 131104 | tf_op jit(solution)/shard_map/ppermute | solution.py:35
  15.4 0.7 %inner.6.rest_0_ = bf16[2,64,256]{2,1,0:T(8,128)(2,1)S(1)} custom-call(bf16[4,8,16,256]{3,2,1,0:T(8,128)(2,1)S(1)} %keep.1.keep_ref, bf16[2,8,16,256]{3,2,1,0:T(8,128)(2,1)S(1)} %collective-permute-done.1.other_ref, bf16[8,128,64]{2,1,0:T(8,128)(2,1)S(1)} %get-tuple-element.21.first_ref, bf16[6,64,64]{2,1,0:T(8,128)(2,1)S(1)} %get-tuple-element.22.inner_ref, ...), custom_call_target="tpu_custom_call" | custom-call | tf_op jit(solution)/shard_map/inner/pallas_call | solution.py:742
  16.1 1.9 %collective-permute-start.3 = (bf16[2,64,256]{2,1,0:T(8,128)(2,1)S(1)}, bf16[2,64,256]{2,1,0:T(8,128)(2,1)S(1)}, u32[]{:S(2)}, u32[]{:S(2)}) collective-permute-start(bf16[2,64,256]{2,1,0:T(8,128)(2,1)S(1)} %inner.6.rest_0_), channel_id=1, source_target_pairs={{0,4},{4,0},{8,12},{12,8},{1,5},{5,1},{9,13},{13,9},{2,6},{6,2},{1... | collective-permute-start | bytes 196616 | tf_op jit(solution)/shard_map/ppermute | solution.py:757
  18.0 2.6 %collective-permute-start.4 = (bf16[2,64,256]{2,1,0:T(8,128)(2,1)S(1)}, bf16[2,64,256]{2,1,0:T(8,128)(2,1)S(1)}, u32[]{:S(2)}, u32[]{:S(2)}) collective-permute-start(bf16[2,64,256]{2,1,0:T(8,128)(2,1)S(1)} %inner.5.rest_0_), channel_id=1, source_target_pairs={{0,8},{4,12},{8,0},{12,4},{1,9},{5,13},{9,1},{13,5},{2,10},{6,14},... | collective-permute-start | bytes 196616 | tf_op jit(solution)/shard_map/ppermute | solution.py:757
  20.6 0.0 collective-permute-start.5
  20.6 0.7 %inner.7.after_ref.rest_0_ = bf16[2,64,256]{2,1,0:T(8,128)(2,1)S(1)} custom-call(bf16[4,8,16,256]{3,2,1,0:T(8,128)(2,1)S(1)} %keep.1.keep_ref, bf16[2,8,16,256]{3,2,1,0:T(8,128)(2,1)S(1)} %collective-permute-done.1.other_ref, bf16[8,128,64]{2,1,0:T(8,128)(2,1)S(1)} %get-tuple-element.21.first_ref, bf16[6,64,64]{2,1,0:T(8,128)(2,1)S(1)} %get-tuple-element.22.inner_ref, ...), custom_call_target="tpu_custom_call" | custom-call | tf_op jit(solution)/shard_map/inner/pallas_call | solution.py:742
  21.3 0.7 %outer_tables.1 = (bf16[6,64,64]{2,1,0:T(8,128)(2,1)S(1)}, f32[6,2,64,256]{3,2,1,0:T(8,128)S(1)}) custom-call(s32[1,64]{1,0:T(1,128)S(1)} %bitcast.5, s32[64,64]{1,0:T(8,128)S(1)} %bitcast.3, bf16[2,64,256]{2,1,0:T(8,128)(2,1)S(1)} %inner.7.after_ref.rest_0_), custom_call_target="tpu_custom_call" | custom-call | tf_op jit(solution)/shard_map/outer_tables/pallas_call | solution.py:760
  22.1 0.0 collective-permute-done.3.rest_1_
  22.1 3.1 %collective-permute-done.4.rest_2_ = bf16[2,64,256]{2,1,0:T(8,128)(2,1)S(1)} collective-permute-done((bf16[2,64,256]{2,1,0:T(8,128)(2,1)S(1)}, bf16[2,64,256]{2,1,0:T(8,128)(2,1)S(1)}, u32[]{:S(2)}, u32[]{:S(2)}) %collective-permute-start.4) | collective-permute-done | bytes 65568 | tf_op jit(solution)/shard_map/ppermute | solution.py:757
  25.2 1.5 %collective-permute-done.5.rest_3_ = bf16[2,64,256]{2,1,0:T(8,128)(2,1)S(1)} collective-permute-done((bf16[2,64,256]{2,1,0:T(8,128)(2,1)S(1)}, bf16[2,64,256]{2,1,0:T(8,128)(2,1)S(1)}, u32[]{:S(2)}, u32[]{:S(2)}) %collective-permute-start.5) | collective-permute-done | bytes 65568 | tf_op jit(solution)/shard_map/ppermute | solution.py:757
  26.7 1.0 %outer.1 = f32[2,64,256]{2,1,0:T(8,128)} custom-call(bf16[6,64,64]{2,1,0:T(8,128)(2,1)S(1)} %get-tuple-element.25.outer_ref, f32[6,2,64,256]{3,2,1,0:T(8,128)S(1)} %get-tuple-element.26.phase_ref, bf16[2,64,256]{2,1,0:T(8,128)(2,1)S(1)} %inner.7.after_ref.rest_0_, bf16[2,64,256]{2,1,0:T(8,128)(2,1)S(1)} %collective-permute-done.3.rest_1_, ...), custom_call_target="tpu_custom_call" | custom-call | tf_op jit(solution)/shard_map/outer/pallas_call | solution.py:771
Async XLA Ops:
  0.0 1.0 %copy-start.1 = (bf16[2,8,8,2048]{3,2,1,0:T(8,128)(2,1)S(1)}, bf16[2,8,8,2048]{3,2,1,0:T(8,128)(2,1)}, u32[]{:S(2)}) copy-start(bf16[2,8,8,2048]{3,2,1,0:T(8,128)(2,1)} %echo_hbm.1) | copy-start | bytes 1572868
  1.0 3.5 %copy-start.2 = (bf16[768,256]{1,0:T(8,128)(2,1)S(1)}, bf16[768,256]{1,0:T(8,128)(2,1)}, u32[]{:S(2)}) copy-start(bf16[768,256]{1,0:T(8,128)(2,1)} %constant.5.clone.chirp_hbm) | copy-start | bytes 1179652
  1.1 3.4 %collective-permute-start = (bf16[2,8,8,384]{3,2,1,0:T(8,128)(2,1)S(1)}, bf16[2,8,8,384]{3,2,1,0:T(8,128)(2,1)S(1)}, u32[]{:S(2)}, u32[]{:S(2)}) collective-permute-start(bf16[2,8,8,384]{3,2,1,0:T(8,128)(2,1)S(1)} %get-tuple-element.17), channel_id=1, source_target_pairs={{0,1},{1,0},{2,3},{3,2},{4,5},{5,4},{6,7},{7,6},{8,9},{9,8},{10,11... | collective-permute-start | bytes 294920 | tf_op jit(solution)/shard_map/ppermute | solution.py:35
  1.6 1.6 %copy-start = (bf16[16,256,256]{2,1,0:T(8,128)(2,1)S(1)}, bf16[16,256,256]{2,1,0:T(8,128)(2,1)}, u32[]{:S(2)}) copy-start(bf16[16,256,256]{2,1,0:T(8,128)(2,1)} %constant.4.clone.bands_hbm) | copy-start | bytes 6291460
  4.5 4.1 %copy-start.3 = (s32[32,2,64]{2,1,0:T(2,128)S(1)}, s32[32,2,64]{2,1,0:T(2,128)}, u32[]{:S(2)}) copy-start(s32[32,2,64]{2,1,0:T(2,128)} %param.7) | copy-start | bytes 49156
  4.5 4.0 %copy-start.4 = (s32[64]{0:T(128)S(1)}, s32[64]{0:T(128)}, u32[]{:S(2)}) copy-start(s32[64]{0:T(128)} %param.6) | copy-start | bytes 772
  5.9 6.9 %collective-permute-start.2 = (bf16[2,8,16,256]{3,2,1,0:T(8,128)(2,1)S(1)}, bf16[2,8,16,256]{3,2,1,0:T(8,128)(2,1)S(1)}, u32[]{:S(2)}, u32[]{:S(2)}) collective-permute-start(bf16[2,8,16,256]{3,2,1,0:T(8,128)(2,1)S(1)} %get-tuple-element.24), channel_id=1, source_target_pairs={{0,2},{2,0},{1,3},{3,1},{4,6},{6,4},{5,7},{7,5},{8,10},{10,8},{9,1... | collective-permute-start | bytes 393224 | tf_op jit(solution)/shard_map/ppermute | solution.py:35
  8.5 7.0 %collective-permute-start.1 = (bf16[2,8,16,256]{3,2,1,0:T(8,128)(2,1)S(1)}, bf16[2,8,16,256]{3,2,1,0:T(8,128)(2,1)S(1)}, u32[]{:S(2)}, u32[]{:S(2)}) collective-permute-start(bf16[2,8,16,256]{3,2,1,0:T(8,128)(2,1)S(1)} %get-tuple-element.20), channel_id=1, source_target_pairs={{0,2},{2,0},{1,3},{3,1},{4,6},{6,4},{5,7},{7,5},{8,10},{10,8},{9,1... | collective-permute-start | bytes 393224 | tf_op jit(solution)/shard_map/ppermute | solution.py:35
  16.1 5.9 %collective-permute-start.3 = (bf16[2,64,256]{2,1,0:T(8,128)(2,1)S(1)}, bf16[2,64,256]{2,1,0:T(8,128)(2,1)S(1)}, u32[]{:S(2)}, u32[]{:S(2)}) collective-permute-start(bf16[2,64,256]{2,1,0:T(8,128)(2,1)S(1)} %inner.6.rest_0_), channel_id=1, source_target_pairs={{0,4},{4,0},{8,12},{12,8},{1,5},{5,1},{9,13},{13,9},{2,6},{6,2},{1... | collective-permute-start | bytes 196616 | tf_op jit(solution)/shard_map/ppermute | solution.py:757
  18.0 7.1 %collective-permute-start.4 = (bf16[2,64,256]{2,1,0:T(8,128)(2,1)S(1)}, bf16[2,64,256]{2,1,0:T(8,128)(2,1)S(1)}, u32[]{:S(2)}, u32[]{:S(2)}) collective-permute-start(bf16[2,64,256]{2,1,0:T(8,128)(2,1)S(1)} %inner.5.rest_0_), channel_id=1, source_target_pairs={{0,8},{4,12},{8,0},{12,4},{1,9},{5,13},{9,1},{13,5},{2,10},{6,14},... | collective-permute-start | bytes 196616 | tf_op jit(solution)/shard_map/ppermute | solution.py:757
  20.6 6.1 %collective-permute-start.5 = (bf16[2,64,256]{2,1,0:T(8,128)(2,1)S(1)}, bf16[2,64,256]{2,1,0:T(8,128)(2,1)S(1)}, u32[]{:S(2)}, u32[]{:S(2)}) collective-permute-start(bf16[2,64,256]{2,1,0:T(8,128)(2,1)S(1)} %inner.4.rest_0_), channel_id=1, source_target_pairs={{0,12},{4,8},{8,4},{12,0},{1,13},{5,9},{9,5},{13,1},{2,14},{6,10},... | collective-permute-start | bytes 196616 | tf_op jit(solution)/shard_map/ppermute | solution.py:757

commit v2 on v1

--- a/solution.py
+++ b/solution.py
@@ -675,6 +675,7 @@
         out_specs=[vmem(), vmem()],
         scratch_shapes=[pltpu.SemaphoreType.DMA((2,))],
         name="edge",
+        cost_estimate=pl.CostEstimate(flops=10**10, bytes_accessed=10**8, transcendentals=0),
         **PARAMS,
     )(echoes)
     edge = swapped(edge, "rng", 0)
@@ -735,14 +736,13 @@
         name="tables",
         **PARAMS,
     )(angles, codes)
-    images = []
-    after = []
-    for index in range(pulse_count):
-        distance = pulse_count - 1 - index
+    images = [None] * pulse_count
+    for distance in [*range(1, pulse_count), 0]:
+        index = pulse_count - 1 - distance
         image = pl.pallas_call(
             functools.partial(inner_kernel, index),
             out_shape=shape((2, beams, piece_width), bf16),
-            in_specs=[vmem()] * 5 + [anywhere()] * len(after),
+            in_specs=[vmem()] * 5,
             out_specs=vmem(),
             scratch_shapes=[
                 pltpu.VMEM((pulses, 2 * beams, piece_width), f32),
@@ -751,11 +751,11 @@
             ],
             name="inner",
             **PARAMS,
-        )(kept, received[index // chunk], first, inner, phase, *after)
-        after = [image]
+        )(kept, received[index // chunk], first, inner, phase)
+        images[distance] = image
         if distance:
-            image = lax.ppermute(image, "pulse", [(i, i ^ distance) for i in range(pulse_count)])
-        images.insert(0, image)
+            pairs = [(i, i ^ distance) for i in range(pulse_count)]
+            images[distance] = lax.ppermute(image, "pulse", pairs)
     outer_count = 2 * pulse_count - 2
     outer, outer_phase = pl.pallas_call(
         functools.partial(outer_tables_kernel, (rx_count, width, pulse_count)),
@@ -767,7 +767,7 @@
         out_specs=[vmem()] * 2,
         name="outer_tables",
         **PARAMS,
-    )(angles, codes, *after)
+    )(angles, codes, images[0])
     return pl.pallas_call(
         outer_kernel,
         out_shape=shape((2, beams, piece_width), f32),

time: 27.9 us -> 24.3 us (0.87)
  waiting for transfers between devices: 7.41 us -> 4.47 us
  local copies, waits for them, and re-layouts: 2.65 us -> 1.21 us
  starting transfers between devices: 7.65 us -> 8.5 us
    ppermute x3, waiting for transfers between devices: 4.61 us -> 2.96 us  [fast(): images[distance] = lax.ppermute(image, 'pulse', pairs)]
    unnamed x10, local copies, waits for them, and re-layouts: 2.65 us -> 1.21 us
    ppermute x3, waiting for transfers between devices: 2.8 us -> 1.51 us  [swapped(): lax.ppermute(x, axis, [(i, i ^ 1 << distance) for i in range(lax.axis_siz...]
    ppermute x3, starting transfers between devices: 4.49 us -> 4.95 us  [fast(): images[distance] = lax.ppermute(image, 'pulse', pairs)]
    ppermute x3, starting transfers between devices: 3.16 us -> 3.54 us  [swapped(): lax.ppermute(x, axis, [(i, i ^ 1 << distance) for i in range(lax.axis_siz...]
  transfers between devices with their start and end apart: 6 -> 6, of which waited for: 4 -> 3; matrix products, arithmetic and copies ran while one was open for 0% -> 0% of each run, Pallas kernels for 24% -> 31%
where the time goes in v2:
time: 24.3 us; the launch traced here: 24.2 us
  Pallas kernels  9.87 us (41%)
  starting transfers between devices  8.5 us (35%)
  waiting for transfers between devices  4.47 us (18%)
  local copies, waits for them, and re-layouts  1.21 us (5%)
    ppermute x3, starting transfers between devices, fast(): images[distance] = lax.ppermute(image, 'pulse', pairs)  4.95 us
    ppermute x3, starting transfers between devices, swapped(): lax.ppermute(x, axis, [(i, i ^ 1 << distance) for i in range(lax.axis_siz...  3.54 us
    ppermute x3, waiting for transfers between devices, fast(): images[distance] = lax.ppermute(image, 'pulse', pairs)  2.96 us
    pallas_call x4, Pallas kernels, fast(): pl.pallas_call(functools.partial(inner_kernel, index), out_shape=shape((2...  2.72 us
    pallas_call x1, Pallas kernels, fast(): pl.pallas_call(functools.partial(tables_kernel, (pulses, channels, rx_cou...  2.1 us
    ppermute x3, waiting for transfers between devices, swapped(): lax.ppermute(x, axis, [(i, i ^ 1 << distance) for i in range(lax.axis_siz...  1.51 us
    pallas_call x1, Pallas kernels, fast(): pl.pallas_call(functools.partial(send_kernel, piece_tiles), out_shape=[se...  1.35 us
    pallas_call x1, Pallas kernels, fast(): pl.pallas_call(interior_kernel, out_shape=filtered_shape, in_specs=[vmem(...  1.27 us
  transfers between devices with their start and end apart: 6, of which 3 were waited for; matrix products, arithmetic and copies ran while one was open for 0% of the time, Pallas kernels for 31%

profile of v2, /device:TPU:0, one launch (start us, length us, event | category | flops | bytes accessed | tf_op | source)
XLA Modules:
  0.0 24.2 jit_solution(10021361791917644463)
XLA Ops:
  0.0 0.0 copy-start
  0.0 0.0 copy-start.4
  0.0 1.2 %copy-done.4 = bf16[2,8,8,2048]{3,2,1,0:T(8,128)(2,1)S(1)} copy-done((bf16[2,8,8,2048]{3,2,1,0:T(8,128)(2,1)S(1)}, bf16[2,8,8,2048]{3,2,1,0:T(8,128)(2,1)}, u32[]{:S(2)}) %copy-start.4) | copy-done | bytes 524312
  1.2 0.1 edge.1
  1.3 0.0 copy-start.1
  1.3 0.5 %collective-permute-start = (bf16[2,8,8,384]{3,2,1,0:T(8,128)(2,1)S(1)}, bf16[2,8,8,384]{3,2,1,0:T(8,128)(2,1)S(1)}, u32[]{:S(2)}, u32[]{:S(2)}) collective-permute-start(bf16[2,8,8,384]{3,2,1,0:T(8,128)(2,1)S(1)} %get-tuple-element.17), channel_id=1, source_target_pairs={{0,1},{1,0},{2,3},{3,2},{4,5},{5,4},{6,7},{7,6},{8,9},{9,8},{10,11... | collective-permute-start | bytes 294920 | tf_op jit(solution)/shard_map/ppermute | solution.py:35
  1.8 0.0 copy-done
  1.8 1.3 %interior.1.inner_ref = bf16[128,2688]{1,0:T(8,128)(2,1)S(1)} custom-call(bf16[2,8,8,2048]{3,2,1,0:T(8,128)(2,1)S(1)} %get-tuple-element.16.echo_ref, bf16[16,256,256]{2,1,0:T(8,128)(2,1)S(1)} %copy-done), custom_call_target="tpu_custom_call" | custom-call | tf_op jit(solution)/shard_map/interior/pallas_call | solution.py:685
  3.1 0.0 copy-start.2
  3.1 0.0 copy-start.3
  3.1 0.0 collective-permute-done.edge_ref
  3.1 0.0 copy-done.1
  3.1 1.4 %send.1 = (bf16[2,8,16,256]{3,2,1,0:T(8,128)(2,1)S(1)}, bf16[2,8,16,256]{3,2,1,0:T(8,128)(2,1)S(1)}, bf16[128,2688]{1,0:T(8,128)(2,1)S(1)}, bf16[768,256]{1,0:T(8,128)(2,1)S(1)}) custom-call(bf16[128,2688]{1,0:T(8,128)(2,1)S(1)} %interior.1.inner_ref, bf16[2,8,8,2048]{3,2,1,0:T(8,128)(2,1)S(1)} %get-tuple-element.16.echo_ref, ...), custom_call_target="tpu_custom_call" | custom-call | tf_op jit(solution)/shard_map/send/pallas_call | solution.py:702
  4.5 2.9 %collective-permute-start.3 = (bf16[2,8,16,256]{3,2,1,0:T(8,128)(2,1)S(1)}, bf16[2,8,16,256]{3,2,1,0:T(8,128)(2,1)S(1)}, u32[]{:S(2)}, u32[]{:S(2)}) collective-permute-start(bf16[2,8,16,256]{3,2,1,0:T(8,128)(2,1)S(1)} %get-tuple-element.26), channel_id=1, source_target_pairs={{0,2},{2,0},{1,3},{3,1},{4,6},{6,4},{5,7},{7,5},{8,10},{10,8},{9,1... | collective-permute-start | bytes 393224 | tf_op jit(solution)/shard_map/ppermute | solution.py:35
  7.4 0.1 collective-permute-start.1
  7.5 0.0 copy-done.2
  7.5 0.0 copy-done.3
  7.5 2.1 %tables.1 = (bf16[8,128,64]{2,1,0:T(8,128)(2,1)S(1)}, bf16[6,64,64]{2,1,0:T(8,128)(2,1)S(1)}, f32[4,4,2,64,256]{4,3,2,1,0:T(8,128)S(1)}) custom-call(s32[1,64]{1,0:T(1,128)S(1)} %bitcast.4, s32[64,64]{1,0:T(8,128)S(1)} %bitcast.2), custom_call_target="tpu_custom_call" | custom-call | tf_op jit(solution)/shard_map/tables/pallas_call | solution.py:727
  9.6 0.6 %keep.1.keep_ref = bf16[4,8,16,256]{3,2,1,0:T(8,128)(2,1)S(1)} custom-call(bf16[128,2688]{1,0:T(8,128)(2,1)S(1)} %get-tuple-element.18.filtered_ref, bf16[768,256]{1,0:T(8,128)(2,1)S(1)} %get-tuple-element.19.chirp_ref), custom_call_target="tpu_custom_call" | custom-call | tf_op jit(solution)/shard_map/keep/pallas_call | solution.py:718
  10.2 1.5 %collective-permute-done.3.other_ref = bf16[2,8,16,256]{3,2,1,0:T(8,128)(2,1)S(1)} collective-permute-done((bf16[2,8,16,256]{3,2,1,0:T(8,128)(2,1)S(1)}, bf16[2,8,16,256]{3,2,1,0:T(8,128)(2,1)S(1)}, u32[]{:S(2)}, u32[]{:S(2)}) %collective-permute-start.3) | collective-permute-done | bytes 131104 | tf_op jit(solution)/shard_map/ppermute | solution.py:35
  11.7 0.7 %inner.6 = bf16[2,64,256]{2,1,0:T(8,128)(2,1)S(1)} custom-call(bf16[4,8,16,256]{3,2,1,0:T(8,128)(2,1)S(1)} %keep.1.keep_ref, bf16[2,8,16,256]{3,2,1,0:T(8,128)(2,1)S(1)} %collective-permute-done.3.other_ref, bf16[8,128,64]{2,1,0:T(8,128)(2,1)S(1)} %get-tuple-element.21.first_ref, bf16[6,64,64]{2,1,0:T(8,128)(2,1)S(1)} %get-tuple-element.22.inner_ref, ...), custom_call_target="tpu_custom_call" | custom-call | tf_op jit(solution)/shard_map/inner/pallas_call | solution.py:742
  12.4 3.2 %collective-permute-start.4 = (bf16[2,64,256]{2,1,0:T(8,128)(2,1)S(1)}, bf16[2,64,256]{2,1,0:T(8,128)(2,1)S(1)}, u32[]{:S(2)}, u32[]{:S(2)}) collective-permute-start(bf16[2,64,256]{2,1,0:T(8,128)(2,1)S(1)} %inner.6), channel_id=1, source_target_pairs={{0,8},{4,12},{8,0},{12,4},{1,9},{5,13},{9,1},{13,5},{2,10},{6,14},... | collective-permute-start | bytes 196616 | tf_op jit(solution)/shard_map/ppermute | solution.py:758
  15.6 0.7 %inner.7 = bf16[2,64,256]{2,1,0:T(8,128)(2,1)S(1)} custom-call(bf16[4,8,16,256]{3,2,1,0:T(8,128)(2,1)S(1)} %keep.1.keep_ref, bf16[2,8,16,256]{3,2,1,0:T(8,128)(2,1)S(1)} %collective-permute-done.3.other_ref, bf16[8,128,64]{2,1,0:T(8,128)(2,1)S(1)} %get-tuple-element.21.first_ref, bf16[6,64,64]{2,1,0:T(8,128)(2,1)S(1)} %get-tuple-element.22.inner_ref, ...), custom_call_target="tpu_custom_call" | custom-call | tf_op jit(solution)/shard_map/inner/pallas_call | solution.py:742
  16.3 1.4 %collective-permute-start.5 = (bf16[2,64,256]{2,1,0:T(8,128)(2,1)S(1)}, bf16[2,64,256]{2,1,0:T(8,128)(2,1)S(1)}, u32[]{:S(2)}, u32[]{:S(2)}) collective-permute-start(bf16[2,64,256]{2,1,0:T(8,128)(2,1)S(1)} %inner.7), channel_id=1, source_target_pairs={{0,12},{4,8},{8,4},{12,0},{1,13},{5,9},{9,5},{13,1},{2,14},{6,10},... | collective-permute-start | bytes 196616 | tf_op jit(solution)/shard_map/ppermute | solution.py:758
  17.7 0.0 collective-permute-done.1.other_ref
  17.7 0.7 %inner.5 = bf16[2,64,256]{2,1,0:T(8,128)(2,1)S(1)} custom-call(bf16[4,8,16,256]{3,2,1,0:T(8,128)(2,1)S(1)} %keep.1.keep_ref, bf16[2,8,16,256]{3,2,1,0:T(8,128)(2,1)S(1)} %collective-permute-done.1.other_ref, bf16[8,128,64]{2,1,0:T(8,128)(2,1)S(1)} %get-tuple-element.21.first_ref, bf16[6,64,64]{2,1,0:T(8,128)(2,1)S(1)} %get-tuple-element.22.inner_ref, ...), custom_call_target="tpu_custom_call" | custom-call | tf_op jit(solution)/shard_map/inner/pallas_call | solution.py:742
  18.4 0.3 %collective-permute-start.2 = (bf16[2,64,256]{2,1,0:T(8,128)(2,1)S(1)}, bf16[2,64,256]{2,1,0:T(8,128)(2,1)S(1)}, u32[]{:S(2)}, u32[]{:S(2)}) collective-permute-start(bf16[2,64,256]{2,1,0:T(8,128)(2,1)S(1)} %inner.5), channel_id=1, source_target_pairs={{0,4},{4,0},{8,12},{12,8},{1,5},{5,1},{9,13},{13,9},{2,6},{6,2},{1... | collective-permute-start | bytes 196616 | tf_op jit(solution)/shard_map/ppermute | solution.py:758
  18.7 0.7 %inner.4.after_ref.rest_0_ = bf16[2,64,256]{2,1,0:T(8,128)(2,1)S(1)} custom-call(bf16[4,8,16,256]{3,2,1,0:T(8,128)(2,1)S(1)} %keep.1.keep_ref, bf16[2,8,16,256]{3,2,1,0:T(8,128)(2,1)S(1)} %collective-permute-done.1.other_ref, bf16[8,128,64]{2,1,0:T(8,128)(2,1)S(1)} %get-tuple-element.21.first_ref, bf16[6,64,64]{2,1,0:T(8,128)(2,1)S(1)} %get-tuple-element.22.inner_ref, ...), custom_call_target="tpu_custom_call" | custom-call | tf_op jit(solution)/shard_map/inner/pallas_call | solution.py:742
  19.4 0.7 %outer_tables.1 = (bf16[6,64,64]{2,1,0:T(8,128)(2,1)S(1)}, f32[6,2,64,256]{3,2,1,0:T(8,128)S(1)}) custom-call(s32[1,64]{1,0:T(1,128)S(1)} %bitcast.5, s32[64,64]{1,0:T(8,128)S(1)} %bitcast.3, bf16[2,64,256]{2,1,0:T(8,128)(2,1)S(1)} %inner.4.after_ref.rest_0_), custom_call_target="tpu_custom_call" | custom-call | tf_op jit(solution)/shard_map/outer_tables/pallas_call | solution.py:760
  20.2 0.0 collective-permute-done.4.rest_2_
  20.2 2.3 %collective-permute-done.5.rest_3_ = bf16[2,64,256]{2,1,0:T(8,128)(2,1)S(1)} collective-permute-done((bf16[2,64,256]{2,1,0:T(8,128)(2,1)S(1)}, bf16[2,64,256]{2,1,0:T(8,128)(2,1)S(1)}, u32[]{:S(2)}, u32[]{:S(2)}) %collective-permute-start.5) | collective-permute-done | bytes 65568 | tf_op jit(solution)/shard_map/ppermute | solution.py:758
  22.5 0.7 %collective-permute-done.2.rest_1_ = bf16[2,64,256]{2,1,0:T(8,128)(2,1)S(1)} collective-permute-done((bf16[2,64,256]{2,1,0:T(8,128)(2,1)S(1)}, bf16[2,64,256]{2,1,0:T(8,128)(2,1)S(1)}, u32[]{:S(2)}, u32[]{:S(2)}) %collective-permute-start.2) | collective-permute-done | bytes 65568 | tf_op jit(solution)/shard_map/ppermute | solution.py:758
  23.2 1.0 %outer.1 = f32[2,64,256]{2,1,0:T(8,128)} custom-call(bf16[6,64,64]{2,1,0:T(8,128)(2,1)S(1)} %get-tuple-element.24.outer_ref, f32[6,2,64,256]{3,2,1,0:T(8,128)S(1)} %get-tuple-element.25.phase_ref, bf16[2,64,256]{2,1,0:T(8,128)(2,1)S(1)} %inner.4.after_ref.rest_0_, bf16[2,64,256]{2,1,0:T(8,128)(2,1)S(1)} %collective-permute-done.2.rest_1_, ...), custom_call_target="tpu_custom_call" | custom-call | tf_op jit(solution)/shard_map/outer/pallas_call | solution.py:771
Async XLA Ops:
  0.0 1.8 %copy-start = (bf16[16,256,256]{2,1,0:T(8,128)(2,1)S(1)}, bf16[16,256,256]{2,1,0:T(8,128)(2,1)}, u32[]{:S(2)}) copy-start(bf16[16,256,256]{2,1,0:T(8,128)(2,1)} %constant.4.clone.bands_hbm) | copy-start | bytes 6291460
  0.0 1.2 %copy-start.4 = (bf16[2,8,8,2048]{3,2,1,0:T(8,128)(2,1)S(1)}, bf16[2,8,8,2048]{3,2,1,0:T(8,128)(2,1)}, u32[]{:S(2)}) copy-start(bf16[2,8,8,2048]{3,2,1,0:T(8,128)(2,1)} %echo_hbm.1) | copy-start | bytes 1572868
  1.3 1.9 %copy-start.1 = (bf16[768,256]{1,0:T(8,128)(2,1)S(1)}, bf16[768,256]{1,0:T(8,128)(2,1)}, u32[]{:S(2)}) copy-start(bf16[768,256]{1,0:T(8,128)(2,1)} %constant.5.clone.chirp_hbm) | copy-start | bytes 1179652
  1.3 1.8 %collective-permute-start = (bf16[2,8,8,384]{3,2,1,0:T(8,128)(2,1)S(1)}, bf16[2,8,8,384]{3,2,1,0:T(8,128)(2,1)S(1)}, u32[]{:S(2)}, u32[]{:S(2)}) collective-permute-start(bf16[2,8,8,384]{3,2,1,0:T(8,128)(2,1)S(1)} %get-tuple-element.17), channel_id=1, source_target_pairs={{0,1},{1,0},{2,3},{3,2},{4,5},{5,4},{6,7},{7,6},{8,9},{9,8},{10,11... | collective-permute-start | bytes 294920 | tf_op jit(solution)/shard_map/ppermute | solution.py:35
  3.1 4.4 %copy-start.2 = (s32[32,2,64]{2,1,0:T(2,128)S(1)}, s32[32,2,64]{2,1,0:T(2,128)}, u32[]{:S(2)}) copy-start(s32[32,2,64]{2,1,0:T(2,128)} %param.7) | copy-start | bytes 49156
  3.1 4.4 %copy-start.3 = (s32[64]{0:T(128)S(1)}, s32[64]{0:T(128)}, u32[]{:S(2)}) copy-start(s32[64]{0:T(128)} %param.6) | copy-start | bytes 772
  4.5 7.2 %collective-permute-start.3 = (bf16[2,8,16,256]{3,2,1,0:T(8,128)(2,1)S(1)}, bf16[2,8,16,256]{3,2,1,0:T(8,128)(2,1)S(1)}, u32[]{:S(2)}, u32[]{:S(2)}) collective-permute-start(bf16[2,8,16,256]{3,2,1,0:T(8,128)(2,1)S(1)} %get-tuple-element.26), channel_id=1, source_target_pairs={{0,2},{2,0},{1,3},{3,1},{4,6},{6,4},{5,7},{7,5},{8,10},{10,8},{9,1... | collective-permute-start | bytes 393224 | tf_op jit(solution)/shard_map/ppermute | solution.py:35
  7.4 10.3 %collective-permute-start.1 = (bf16[2,8,16,256]{3,2,1,0:T(8,128)(2,1)S(1)}, bf16[2,8,16,256]{3,2,1,0:T(8,128)(2,1)S(1)}, u32[]{:S(2)}, u32[]{:S(2)}) collective-permute-start(bf16[2,8,16,256]{3,2,1,0:T(8,128)(2,1)S(1)} %get-tuple-element.20), channel_id=1, source_target_pairs={{0,2},{2,0},{1,3},{3,1},{4,6},{6,4},{5,7},{7,5},{8,10},{10,8},{9,1... | collective-permute-start | bytes 393224 | tf_op jit(solution)/shard_map/ppermute | solution.py:35
  12.4 7.8 %collective-permute-start.4 = (bf16[2,64,256]{2,1,0:T(8,128)(2,1)S(1)}, bf16[2,64,256]{2,1,0:T(8,128)(2,1)S(1)}, u32[]{:S(2)}, u32[]{:S(2)}) collective-permute-start(bf16[2,64,256]{2,1,0:T(8,128)(2,1)S(1)} %inner.6), channel_id=1, source_target_pairs={{0,8},{4,12},{8,0},{12,4},{1,9},{5,13},{9,1},{13,5},{2,10},{6,14},... | collective-permute-start | bytes 196616 | tf_op jit(solution)/shard_map/ppermute | solution.py:758
  16.3 6.2 %collective-permute-start.5 = (bf16[2,64,256]{2,1,0:T(8,128)(2,1)S(1)}, bf16[2,64,256]{2,1,0:T(8,128)(2,1)S(1)}, u32[]{:S(2)}, u32[]{:S(2)}) collective-permute-start(bf16[2,64,256]{2,1,0:T(8,128)(2,1)S(1)} %inner.7), channel_id=1, source_target_pairs={{0,12},{4,8},{8,4},{12,0},{1,13},{5,9},{9,5},{13,1},{2,14},{6,10},... | collective-permute-start | bytes 196616 | tf_op jit(solution)/shard_map/ppermute | solution.py:758
  18.4 4.7 %collective-permute-start.2 = (bf16[2,64,256]{2,1,0:T(8,128)(2,1)S(1)}, bf16[2,64,256]{2,1,0:T(8,128)(2,1)S(1)}, u32[]{:S(2)}, u32[]{:S(2)}) collective-permute-start(bf16[2,64,256]{2,1,0:T(8,128)(2,1)S(1)} %inner.5), channel_id=1, source_target_pairs={{0,4},{4,0},{8,12},{12,8},{1,5},{5,1},{9,13},{13,9},{2,6},{6,2},{1... | collective-permute-start | bytes 196616 | tf_op jit(solution)/shard_map/ppermute | solution.py:758

commit v3 on v2

--- a/solution.py
+++ b/solution.py
@@ -295,13 +295,9 @@
     return real, imag
 
 
-def interior_kernel(echo_ref, bands_hbm, filtered_ref, rows_in, rows_out, bands_ref, arrived):
+def interior_kernel(echo_ref, bands_ref, filtered_ref, rows_in, rows_out):
     _, pulses, channels, length = echo_ref.shape
-    rx_place = lax.axis_index("rx")
-    fetch = pltpu.make_async_copy(
-        bands_hbm.at[pl.ds(rx_place * channels, channels)], bands_ref, arrived
-    )
-    fetch.start()
+    first_channel = lax.axis_index("rx") * channels
     tiles = length // LANES
     group = 2 * pulses
     empty = jnp.zeros(rows_in.shape[1:], jnp.float32)
@@ -313,14 +309,13 @@
             block = echo_ref[part, pulse].astype(jnp.float32)
             for tile in range(tiles):
                 rows_in[tile + 1, where, :] = block[:, tile * LANES : (tile + 1) * LANES]
-    fetch.wait()
     lane = lax.broadcasted_iota(jnp.int32, (1, LANES), 1)
     for channel in range(channels):
         rows = rows_in[:, channel * group : (channel + 1) * group, :].astype(jnp.bfloat16)
         windows = jnp.concatenate(
             [rows[:-1].reshape(-1, LANES), rows[1:].reshape(-1, LANES)], axis=1
         )
-        real, imag = filter_channel(windows, bands_ref[channel], pulses)
+        real, imag = filter_channel(windows, bands_ref[first_channel + channel], pulses)
         for tile in range(tiles + 1):
             tile_re, tile_im = real[tile], imag[tile]
             if tile == 0:
@@ -357,34 +352,26 @@
         ).astype(jnp.bfloat16)
 
 
-def chirp_half(filtered_ref, chirp_ref, owner, piece_tiles, out_refs):
+def chirp_pieces(filtered_ref, chirp_ref, owner, piece_count, distances, out_ref):
     pulse_place = lax.axis_index("pulse")
-    piece_count = sum(ref.shape[0] for ref in out_refs)
-    distance = piece_count - 1
-    for out_ref in out_refs:
-        for index in range(out_ref.shape[0]):
-            piece = jnp.bitwise_xor(pulse_place, distance)
-            first = owner * (piece_count * piece_tiles) + piece * piece_tiles
-            starts = [pl.multiple_of((first + t) * LANES, LANES) for t in range(piece_tiles)]
-            chirp_piece(filtered_ref, chirp_ref, starts, out_ref.at[index])
-            distance -= 1
-
-
-def send_kernel(piece_tiles, inner_ref, echo_ref, edge_ref, bands_hbm, chirp_hbm, *rest):
-    *send_refs, filtered_ref, chirp_ref, rows_in, rows_out, bands_ref, arrived = rest
+    piece_tiles = out_ref.shape[3] // LANES
+    for index, distance in enumerate(distances):
+        piece = jnp.bitwise_xor(pulse_place, distance)
+        first = (owner * piece_count + piece) * piece_tiles
+        starts = [pl.multiple_of((first + t) * LANES, LANES) for t in range(piece_tiles)]
+        chirp_piece(filtered_ref, chirp_ref, starts, out_ref.at[index])
+
+
+def edges_kernel(
+    plan, inner_ref, echo_ref, edge_ref, bands_ref, chirp_ref, filtered_ref, *rest
+):
+    *send_refs, rows_in, rows_out = rest
+    del inner_ref
     _, pulses, channels, length = echo_ref.shape
-    rng_place = lax.axis_index("rng")
-    rx_place = lax.axis_index("rx")
-    fetch = pltpu.make_async_copy(
-        bands_hbm.at[pl.ds(rx_place * channels, channels)], bands_ref, arrived.at[0]
-    )
-    fetch.start()
-    fetch_chirp = pltpu.make_async_copy(chirp_hbm, chirp_ref, arrived.at[1])
-    fetch_chirp.start()
-    filtered_ref[...] = inner_ref[...]
+    first_channel = lax.axis_index("rx") * channels
     tiles = length // LANES
     group = 2 * pulses
-    lowest = rng_place == 0
+    lowest = lax.axis_index("rng") == 0
     for part in range(2):
         for pulse in range(pulses):
             where = pl.ds(part * pulses + pulse, channels, stride=group)
@@ -396,13 +383,12 @@
                 high = near_high if tile == 0 else pieces[tile - 1]
                 low = near_low if tile == HALO_TILES else pieces[tile]
                 rows_in[tile, where, :] = jnp.where(lowest, high, low)
-    fetch.wait()
     for channel in range(channels):
         rows = rows_in[:, channel * group : (channel + 1) * group, :].astype(jnp.bfloat16)
         windows = jnp.concatenate(
             [rows[:-1].reshape(-1, LANES), rows[1:].reshape(-1, LANES)], axis=1
         )
-        real, imag = filter_channel(windows, bands_ref[channel], pulses)
+        real, imag = filter_channel(windows, bands_ref[first_channel + channel], pulses)
         for tile in range(HALO_TILES):
             rows_out[tile, pl.ds(channel, pulses, stride=2 * channels), :] = real[tile]
             rows_out[tile, pl.ds(channels + channel, pulses, stride=2 * channels), :] = imag[tile]
@@ -410,12 +396,19 @@
     for tile in range(HALO_TILES):
         start = pl.multiple_of((first + tile) * LANES, LANES)
         filtered_ref[:, pl.ds(start, LANES)] = rows_out[tile].astype(jnp.bfloat16)
-    fetch_chirp.wait()
-    chirp_half(filtered_ref, chirp_ref, 1 - rx_place, piece_tiles, send_refs)
-
-
-def keep_kernel(piece_tiles, filtered_ref, chirp_ref, keep_ref):
-    chirp_half(filtered_ref, chirp_ref, lax.axis_index("rx"), piece_tiles, [keep_ref])
+    piece_count, groups = plan
+    for distances, send_ref in zip(groups, send_refs):
+        chirp_pieces(
+            filtered_ref, chirp_ref, 1 - lax.axis_index("rx"), piece_count, distances, send_ref
+        )
+
+
+def chirp_kernel(partner, piece_count, groups, filtered_ref, chirp_ref, *out_refs):
+    out_refs = out_refs[len(out_refs) - len(groups) :]
+    rx_place = lax.axis_index("rx")
+    owner = 1 - rx_place if partner else rx_place
+    for distances, out_ref in zip(groups, out_refs):
+        chirp_pieces(filtered_ref, chirp_ref, owner, piece_count, distances, out_ref)
 
 
 def turn_parts(step):
@@ -433,6 +426,10 @@
     return real, imag
 
 
+def turned(real, imag, phase_re, phase_im):
+    return phase_re * real - phase_im * imag, phase_im * real + phase_re * imag
+
+
 def as_column(row):
     count = row.shape[1]
     first = lax.broadcasted_iota(jnp.int32, (count, count), 0)
@@ -441,9 +438,8 @@
     return jnp.sum(spread, axis=1, keepdims=True).astype(jnp.int32)
 
 
-def interp_matrix(codes_ref, row):
-    beams = codes_ref.shape[1]
-    code = as_column(codes_ref[pl.ds(row, 1), :])
+def interp_matrix(code):
+    beams = code.shape[0]
     angle_bin = lax.broadcasted_iota(jnp.int32, (beams, beams), 0)
     column = lax.broadcasted_iota(jnp.int32, (beams, beams), 1)
     half = 2 * beams
@@ -455,6 +451,15 @@
     return matrix.astype(jnp.bfloat16)
 
 
+def code_columns(codes_ref, rows):
+    picked = [codes_ref[pl.ds(row, 1), :] for row in rows]
+    picked = jnp.concatenate(picked, axis=0).astype(jnp.float32)
+    spare = -len(rows) % 8
+    if spare:
+        picked = jnp.concatenate([picked, jnp.zeros((spare, picked.shape[1]), jnp.float32)], axis=0)
+    return picked.T.astype(jnp.int32)
+
+
 def tables_kernel(sizes, angle_ref, codes_ref, first_ref, inner_ref, phase_ref):
     pulses, channels, rx_count, width = sizes
     rng_place = lax.axis_index("rng")
@@ -462,9 +467,17 @@
     pulse_place = lax.axis_index("pulse")
     beams = angle_ref.shape[1]
     piece_count = phase_ref.shape[0]
-    piece_width = phase_ref.shape[4]
-    images = pulses * piece_count
+    piece_tiles = phase_ref.shape[4] // LANES
     angle = as_column(angle_ref[...])
+    factors = []
+    rows = []
+    now = pulses
+    while now > 1:
+        base = now * piece_count + pulse_place * now
+        factors.append(base + 1)
+        rows.extend(base + index for index in range(now))
+        now //= 2
+    codes = code_columns(codes_ref, rows)
     column = lax.broadcasted_iota(jnp.int32, (1, 4 * channels * 2), 1)
     within = jnp.bitwise_and(column, 4 * channels - 1)
     owner = jnp.bitwise_xor(rx_place, jnp.where(within >= 2 * channels, 1, 0))
@@ -483,40 +496,39 @@
     )
     low_half = column >= 4 * channels
     entries = 8 * channels
+    matrices = [interp_matrix(codes[:, index : index + 1]) for index in range(len(rows))]
+    composed = jnp.dot(
+        jnp.concatenate(matrices[:pulses], axis=0), steer, preferred_element_type=jnp.float32
+    )
     for index in range(pulses):
-        matrix = interp_matrix(codes_ref, images + pulse_place * pulses + index)
-        composed = jnp.dot(matrix, steer, preferred_element_type=jnp.float32)
         for part in range(2):
-            value = composed[:, part * entries : (part + 1) * entries]
-            high = value.astype(jnp.bfloat16)
-            low = (value - high.astype(jnp.float32)).astype(jnp.bfloat16)
+            value = composed[
+                index * beams : (index + 1) * beams, part * entries : (part + 1) * entries
+            ]
+            high = value.astype(jnp.bfloat16).astype(jnp.float32)
             first_ref[index, part * beams : (part + 1) * beams, :] = jnp.where(
-                low_half, low.astype(jnp.float32), high.astype(jnp.float32)
+                low_half, value - high, high
             ).astype(jnp.bfloat16)
-    factors = []
-    slot = 0
-    now = pulses
-    while now > 1:
-        factors.append(now * piece_count + pulse_place * now + 1)
-        if now < pulses:
-            for index in range(now):
-                inner_ref[slot] = interp_matrix(
-                    codes_ref, now * piece_count + pulse_place * now + index
-                )
-                slot += 1
-        now //= 2
-    lane = lax.broadcasted_iota(jnp.int32, (1, piece_width), 1)
+    for index, matrix in enumerate(matrices[pulses:]):
+        inner_ref[index] = matrix
+    lane = lax.broadcasted_iota(jnp.int32, (1, LANES), 1)
     block = (rng_place * rx_count + rx_place) * width + 1
-    for index in range(piece_count):
-        piece = jnp.bitwise_xor(pulse_place, piece_count - 1 - index)
-        base = jnp.bitwise_and(angle * (block + piece * piece_width + lane), 1023)
-        real, imag = turn_parts(base)
-        phase_ref[index, 0, 0] = real
-        phase_ref[index, 0, 1] = imag
-        for slot, factor in enumerate(factors):
-            real, imag = turn_parts(jnp.bitwise_and(base * factor, 1023))
-            phase_ref[index, slot + 1, 0] = real * half_root
-            phase_ref[index, slot + 1, 1] = imag * half_root
+    base = jnp.bitwise_and(angle * (block + lane), 1023)
+    for slot, factor in enumerate([1, *factors]):
+        scale = half_root if slot else 1.0
+        real, imag = turn_parts(jnp.bitwise_and(base * factor, 1023))
+        real, imag = real * scale, imag * scale
+        step = turn_parts(jnp.bitwise_and(angle * (factor * LANES), 1023))
+        for tile in range(piece_count * piece_tiles):
+            index = piece_count - 1 - jnp.bitwise_xor(pulse_place, tile // piece_tiles)
+            start = tile % piece_tiles * LANES
+            phase_ref[index, slot, 0, :, start : start + LANES] = real
+            phase_ref[index, slot, 1, :, start : start + LANES] = imag
+            real, imag = turned(real, imag, *step)
+
+
+def outer_levels(piece_count):
+    return [piece_count >> level for level in range(piece_count.bit_length() - 1)]
 
 
 def outer_tables_kernel(sizes, angle_ref, codes_ref, after_ref, outer_ref, phase_ref):
@@ -529,11 +541,13 @@
     lane = lax.broadcasted_iota(jnp.int32, (1, piece_width), 1)
     block = (rng_place * rx_count + rx_place) * width + 1
     base = jnp.bitwise_and(angle * (block + pulse_place * piece_width + lane), 1023)
+    rows = [row + level for level in outer_levels(piece_count) for row in range(level)]
+    codes = code_columns(codes_ref, rows)
     slot = 0
     now = piece_count
     while now > 1:
         for index in range(now):
-            outer_ref[slot] = interp_matrix(codes_ref, now + index)
+            outer_ref[slot] = interp_matrix(codes[:, slot : slot + 1])
             real, imag = turn_parts(jnp.bitwise_and(base * (now + index + 1), 1023))
             phase_ref[slot, 0] = real * half_root
             phase_ref[slot, 1] = imag * half_root
@@ -541,19 +555,14 @@
         now //= 2
 
 
-def turned(real, imag, phase_re, phase_im):
-    return phase_re * real - phase_im * imag, phase_im * real + phase_re * imag
-
-
 ROWS = 8
 
 
-def inner_kernel(index, keep_ref, other_ref, first_ref, inner_ref, phase_ref, *rest):
+def inner_kernel(index, other, keep_ref, other_ref, first_ref, inner_ref, phase_ref, *rest):
     out_ref, moved_ref, picture_ref, level_ref = rest[-4:]
     pulses = keep_ref.shape[1]
     beams = inner_ref.shape[1]
     columns = keep_ref.shape[3]
-    other = index % other_ref.shape[0]
     for image in range(pulses):
         rows = jnp.concatenate([keep_ref[index, image], other_ref[other, image]], axis=0)
         moved_ref[image] = jnp.dot(
@@ -619,7 +628,7 @@
 
 
 def outer_kernel(outer_ref, phase_ref, *rest):
-    image_refs, out_ref = rest[:-1], rest[-1]
+    image_refs, out_ref = rest[-2::-1], rest[-1]
     pulse_place = lax.axis_index("pulse")
     pictures = [(ref[0], ref[1]) for ref in image_refs]
     base = 0
@@ -649,6 +658,13 @@
 
 
 PARAMS = dict(compiler_params=pltpu.CompilerParams(vmem_limit_bytes=40 * 1024 * 1024))
+
+
+def send_groups(pulse_count):
+    last = pulse_count - 1
+    if pulse_count < 4:
+        return [[distance] for distance in range(last, -1, -1)]
+    return [[distance] for distance in range(last, -1, -1)]
 
 
 def fast(echoes, beam_angle, interp_table):
@@ -681,48 +697,56 @@
     edge = swapped(edge, "rng", 0)
     tiles = length // LANES
     filtered_shape = shape((rows * pulses, (tiles + 2 * HALO_TILES - 1) * LANES), bf16)
-    bands_scratch = pltpu.VMEM((channels,) + bands.shape[1:], bf16)
     filtered = pl.pallas_call(
         interior_kernel,
         out_shape=filtered_shape,
-        in_specs=[vmem(), hbm()],
+        in_specs=[vmem()] * 2,
         out_specs=vmem(),
         scratch_shapes=[
             pltpu.VMEM((tiles + 2, channels * group, LANES), f32),
             pltpu.VMEM((tiles + 1, rows * pulses, LANES), f32),
-            bands_scratch,
-            pltpu.SemaphoreType.DMA,
         ],
         name="interior",
         **PARAMS,
     )(echoes, bands)
-    chunk = max(1, pulse_count // 2)
-    piece_shape = (pulses, rows, piece_width)
-    sent_shape = shape((chunk,) + piece_shape, bf16)
-    *sent, filtered, chirp = pl.pallas_call(
-        functools.partial(send_kernel, piece_tiles),
-        out_shape=[sent_shape] * (pulse_count // chunk)
-        + [filtered_shape, shape(chirp.shape, bf16)],
-        in_specs=[vmem(), vmem(), vmem(), hbm(), hbm()],
-        out_specs=[vmem()] * (pulse_count // chunk + 2),
+
+    def pieces(count):
+        return shape((count, pulses, rows, piece_width), bf16)
+
+    last = pulse_count - 1
+    groups = send_groups(pulse_count)
+    filtered, *sent = pl.pallas_call(
+        functools.partial(edges_kernel, (pulse_count, groups)),
+        out_shape=[filtered_shape] + [pieces(len(members)) for members in groups],
+        in_specs=[vmem()] * 5,
+        out_specs=[vmem()] * (1 + len(groups)),
         scratch_shapes=[
             pltpu.VMEM((HALO_TILES + 1, channels * group, LANES), f32),
             pltpu.VMEM((HALO_TILES, rows * pulses, LANES), f32),
-            bands_scratch,
-            pltpu.SemaphoreType.DMA((2,)),
         ],
-        name="send",
+        input_output_aliases={0: 0},
+        name="edges",
         **PARAMS,
     )(filtered, echoes, edge, bands, chirp)
-    received = [swapped(piece, "rx", 0) for piece in sent]
+    received = {}
+
+    def receive(members, piece):
+        piece = swapped(piece, "rx", 0)
+        for index, distance in enumerate(members):
+            received[distance] = (piece, index)
+
+    for index in [*range(len(groups) - 2, -1, -1), len(groups) - 1]:
+        receive(groups[index], sent[index])
     kept = pl.pallas_call(
-        functools.partial(keep_kernel, piece_tiles),
-        out_shape=shape((pulse_count,) + piece_shape, bf16),
+        functools.partial(
+            chirp_kernel, False, pulse_count, [[last - index for index in range(pulse_count)]]
+        ),
+        out_shape=[pieces(pulse_count)],
         in_specs=[vmem()] * 2,
-        out_specs=vmem(),
+        out_specs=[vmem()],
         name="keep",
         **PARAMS,
-    )(filtered, chirp)
+    )(filtered, chirp)[0]
     levels = pulses.bit_length() - 1
     first, inner, phase = pl.pallas_call(
         functools.partial(tables_kernel, (pulses, channels, rx_count, width)),
@@ -737,10 +761,11 @@
         **PARAMS,
     )(angles, codes)
     images = [None] * pulse_count
-    for distance in [*range(1, pulse_count), 0]:
-        index = pulse_count - 1 - distance
-        image = pl.pallas_call(
-            functools.partial(inner_kernel, index),
+
+    def merge(distance):
+        other, place = received[distance]
+        return pl.pallas_call(
+            functools.partial(inner_kernel, last - distance, place),
             out_shape=shape((2, beams, piece_width), bf16),
             in_specs=[vmem()] * 5,
             out_specs=vmem(),
@@ -751,11 +776,13 @@
             ],
             name="inner",
             **PARAMS,
-        )(kept, received[index // chunk], first, inner, phase)
-        images[distance] = image
-        if distance:
-            pairs = [(i, i ^ distance) for i in range(pulse_count)]
-            images[distance] = lax.ppermute(image, "pulse", pairs)
+        )(kept, other, first, inner, phase)
+
+    for distance in [*range(1, pulse_count), 0]:
+        images[distance] = merge(distance)
+    for distance in range(1, pulse_count):
+        pairs = [(i, i ^ distance) for i in range(pulse_count)]
+        images[distance] = lax.ppermute(images[distance], "pulse", pairs)
     outer_count = 2 * pulse_count - 2
     outer, outer_phase = pl.pallas_call(
         functools.partial(outer_tables_kernel, (rx_count, width, pulse_count)),
@@ -775,7 +802,7 @@
         out_specs=vmem(),
         name="outer",
         **PARAMS,
-    )(outer, outer_phase, *images)
+    )(outer, outer_phase, *images[::-1])
 
 
 def power_of_two(count):

time: 24.3 us -> 23.2 us (0.955)
  starting transfers between devices: 8.5 us -> 10.4 us
  Pallas kernels: 9.87 us -> 8.24 us
  waiting for transfers between devices: 4.47 us -> 3.01 us
    ppermute x3 -> x5, starting transfers between devices: 3.54 us -> 5.63 us  [swapped(): lax.ppermute(x, axis, [(i, i ^ 1 << distance) for i in range(lax.axis_siz...]
    ppermute x3 -> x5, waiting for transfers between devices: 1.51 us -> 0.03 us  [swapped(): lax.ppermute(x, axis, [(i, i ^ 1 << distance) for i in range(lax.axis_siz...]
    pallas_call x1, Pallas kernels: 2.1 us -> 1.24 us  [fast(): pl.pallas_call(functools.partial(tables_kernel, (pulses, channels, rx_cou...]
    pallas_call x6, Pallas kernels: 4.66 us -> 4.27 us  [the longest x4 2.75 us: merge(): pl.pallas_call(functools.partial(inner_kernel, last - distance, place), o...]
    pallas_call x1, Pallas kernels: 1.27 us -> 0.9 us  [fast(): pl.pallas_call(interior_kernel, out_shape=filtered_shape, in_specs=[vmem(...]
  transfers between devices with their start and end apart: 6 -> 8, of which waited for: 3 -> 2; matrix products, arithmetic and copies ran while one was open for 0% -> 0% of each run, Pallas kernels for 31% -> 27%
where the time goes in v3:
time: 23.2 us; the launch traced here: 23 us
  starting transfers between devices  10.4 us (45%)
  Pallas kernels  8.24 us (36%)
  waiting for transfers between devices  3.01 us (13%)
  local copies, waits for them, and re-layouts  1.21 us (5%)
    ppermute x5, starting transfers between devices, swapped(): lax.ppermute(x, axis, [(i, i ^ 1 << distance) for i in range(lax.axis_siz...  5.63 us
    ppermute x3, starting transfers between devices, fast(): images[distance] = lax.ppermute(images[distance], 'pulse', pairs)  4.81 us
    ppermute x3, waiting for transfers between devices, fast(): images[distance] = lax.ppermute(images[distance], 'pulse', pairs)  2.98 us
    pallas_call x4, Pallas kernels, merge(): pl.pallas_call(functools.partial(inner_kernel, last - distance, place), o...  2.75 us
    pallas_call x1, Pallas kernels, fast(): pl.pallas_call(functools.partial(tables_kernel, (pulses, channels, rx_cou...  1.24 us
    unnamed x10, local copies, waits for them, and re-layouts  1.21 us
    pallas_call x1, Pallas kernels, fast(): pl.pallas_call(outer_kernel, out_shape=shape((2, beams, piece_width), f32...  1.02 us
    pallas_call x1, Pallas kernels, fast(): pl.pallas_call(functools.partial(edges_kernel, (pulse_count, groups)), ou...  0.94 us
  transfers between devices with their start and end apart: 8, of which 2 were waited for; matrix products, arithmetic and copies ran while one was open for 0% of the time, Pallas kernels for 27%

profile of v3, /device:TPU:0, one launch (start us, length us, event | category | flops | bytes accessed | tf_op | source)
XLA Modules:
  0.0 23.0 jit_solution(8908287816768546718)
XLA Ops:
  0.0 0.0 copy-start
  0.0 0.0 copy-start.4
  0.0 1.2 %copy-done.4 = bf16[2,8,8,2048]{3,2,1,0:T(8,128)(2,1)S(1)} copy-done((bf16[2,8,8,2048]{3,2,1,0:T(8,128)(2,1)S(1)}, bf16[2,8,8,2048]{3,2,1,0:T(8,128)(2,1)}, u32[]{:S(2)}) %copy-start.4) | copy-done | bytes 524312
  1.2 0.1 edge.1
  1.3 0.0 copy-start.1
  1.3 0.5 %collective-permute-start = (bf16[2,8,8,384]{3,2,1,0:T(8,128)(2,1)S(1)}, bf16[2,8,8,384]{3,2,1,0:T(8,128)(2,1)S(1)}, u32[]{:S(2)}, u32[]{:S(2)}) collective-permute-start(bf16[2,8,8,384]{3,2,1,0:T(8,128)(2,1)S(1)} %get-tuple-element.18), channel_id=1, source_target_pairs={{0,1},{1,0},{2,3},{3,2},{4,5},{5,4},{6,7},{7,6},{8,9},{9,8},{10,11... | collective-permute-start | bytes 294920 | tf_op jit(solution)/shard_map/ppermute | solution.py:35
  1.8 0.0 copy-done
  1.8 0.9 %interior.1.inner_ref = bf16[128,2688]{1,0:T(8,128)(2,1)S(1)} custom-call(bf16[2,8,8,2048]{3,2,1,0:T(8,128)(2,1)S(1)} %get-tuple-element.17.echo_ref, bf16[16,256,256]{2,1,0:T(8,128)(2,1)S(1)} %copy-done), custom_call_target="tpu_custom_call" | custom-call | tf_op jit(solution)/shard_map/interior/pallas_call | solution.py:700
  2.7 0.0 copy-start.2
  2.7 0.0 copy-start.3
  2.7 0.0 collective-permute-done.edge_ref
  2.7 0.0 copy-done.1
  2.8 0.9 %edges.1 = (bf16[128,2688]{1,0:T(8,128)(2,1)S(1)}, bf16[1,8,16,256]{3,2,1,0:T(8,128)(2,1)S(1)}, bf16[1,8,16,256]{3,2,1,0:T(8,128)(2,1)S(1)}, bf16[1,8,16,256]{3,...) custom-call(bf16[128,2688]{1,0:T(8,128)(2,1)S(1)} %interior.1.inner_ref, ...), custom_call_target="tpu_custom_call", output_to_operand_aliasing={{0}: (0, {})} | custom-call | tf_op jit(solution)/shard_map/edges/pallas_call | solution.py:718
  3.7 2.9 %collective-permute-start.2 = (bf16[1,8,16,256]{3,2,1,0:T(8,128)(2,1)S(1)}, bf16[1,8,16,256]{3,2,1,0:T(8,128)(2,1)S(1)}, u32[]{:S(2)}, u32[]{:S(2)}) collective-permute-start(bf16[1,8,16,256]{3,2,1,0:T(8,128)(2,1)S(1)} %get-tuple-element.26), channel_id=1, source_target_pairs={{0,2},{2,0},{1,3},{3,1},{4,6},{6,4},{5,7},{7,5},{8,10},{10,8},{9,1... | collective-permute-start | bytes 196616 | tf_op jit(solution)/shard_map/ppermute | solution.py:35
  6.6 0.1 collective-permute-start.4
  6.7 1.9 %collective-permute-start.6 = (bf16[1,8,16,256]{3,2,1,0:T(8,128)(2,1)S(1)}, bf16[1,8,16,256]{3,2,1,0:T(8,128)(2,1)S(1)}, u32[]{:S(2)}, u32[]{:S(2)}) collective-permute-start(bf16[1,8,16,256]{3,2,1,0:T(8,128)(2,1)S(1)} %get-tuple-element.28), channel_id=1, source_target_pairs={{0,2},{2,0},{1,3},{3,1},{4,6},{6,4},{5,7},{7,5},{8,10},{10,8},{9,1... | collective-permute-start | bytes 196616 | tf_op jit(solution)/shard_map/ppermute | solution.py:35
  8.7 0.0 copy-done.2
  8.7 0.0 copy-done.3
  8.7 1.2 %tables.1 = (bf16[8,128,64]{2,1,0:T(8,128)(2,1)S(1)}, bf16[6,64,64]{2,1,0:T(8,128)(2,1)S(1)}, f32[4,4,2,64,256]{4,3,2,1,0:T(8,128)S(1)}) custom-call(s32[1,64]{1,0:T(1,128)S(1)} %bitcast.4, s32[64,64]{1,0:T(8,128)S(1)} %bitcast.2), custom_call_target="tpu_custom_call" | custom-call | tf_op jit(solution)/shard_map/tables/pallas_call | solution.py:751
  9.9 0.6 %keep.1.keep_ref = bf16[4,8,16,256]{3,2,1,0:T(8,128)(2,1)S(1)} custom-call(bf16[128,2688]{1,0:T(8,128)(2,1)S(1)} %get-tuple-element.19.filtered_ref, bf16[768,256]{1,0:T(8,128)(2,1)S(1)} %copy-done.1), custom_call_target="tpu_custom_call" | custom-call | tf_op jit(solution)/shard_map/keep/pallas_call | solution.py:740
  10.5 0.1 collective-permute-start.1
  10.7 0.0 collective-permute-done.2.other_ref
  10.7 0.7 %inner.5 = bf16[2,64,256]{2,1,0:T(8,128)(2,1)S(1)} custom-call(bf16[4,8,16,256]{3,2,1,0:T(8,128)(2,1)S(1)} %keep.1.keep_ref, bf16[1,8,16,256]{3,2,1,0:T(8,128)(2,1)S(1)} %collective-permute-done.2.other_ref, bf16[8,128,64]{2,1,0:T(8,128)(2,1)S(1)} %get-tuple-element.21.first_ref, bf16[6,64,64]{2,1,0:T(8,128)(2,1)S(1)} %get-tuple-element.22.inner_ref, ...), custom_call_target="tpu_custom_call" | custom-call | tf_op jit(solution)/shard_map/inner/pallas_call | solution.py:767
  11.4 4.1 %collective-permute-start.3 = (bf16[2,64,256]{2,1,0:T(8,128)(2,1)S(1)}, bf16[2,64,256]{2,1,0:T(8,128)(2,1)S(1)}, u32[]{:S(2)}, u32[]{:S(2)}) collective-permute-start(bf16[2,64,256]{2,1,0:T(8,128)(2,1)S(1)} %inner.5), channel_id=1, source_target_pairs={{0,12},{4,8},{8,4},{12,0},{1,13},{5,9},{9,5},{13,1},{2,14},{6,10},... | collective-permute-start | bytes 196616 | tf_op jit(solution)/shard_map/ppermute | solution.py:785
  15.5 0.0 collective-permute-done.4.other_ref
  15.5 0.7 %inner.6 = bf16[2,64,256]{2,1,0:T(8,128)(2,1)S(1)} custom-call(bf16[4,8,16,256]{3,2,1,0:T(8,128)(2,1)S(1)} %keep.1.keep_ref, bf16[1,8,16,256]{3,2,1,0:T(8,128)(2,1)S(1)} %collective-permute-done.4.other_ref, bf16[8,128,64]{2,1,0:T(8,128)(2,1)S(1)} %get-tuple-element.21.first_ref, bf16[6,64,64]{2,1,0:T(8,128)(2,1)S(1)} %get-tuple-element.22.inner_ref, ...), custom_call_target="tpu_custom_call" | custom-call | tf_op jit(solution)/shard_map/inner/pallas_call | solution.py:767
  16.2 0.1 collective-permute-start.5
  16.3 0.0 collective-permute-done.6.other_ref
  16.3 0.7 %inner.7 = bf16[2,64,256]{2,1,0:T(8,128)(2,1)S(1)} custom-call(bf16[4,8,16,256]{3,2,1,0:T(8,128)(2,1)S(1)} %keep.1.keep_ref, bf16[1,8,16,256]{3,2,1,0:T(8,128)(2,1)S(1)} %collective-permute-done.6.other_ref, bf16[8,128,64]{2,1,0:T(8,128)(2,1)S(1)} %get-tuple-element.21.first_ref, bf16[6,64,64]{2,1,0:T(8,128)(2,1)S(1)} %get-tuple-element.22.inner_ref, ...), custom_call_target="tpu_custom_call" | custom-call | tf_op jit(solution)/shard_map/inner/pallas_call | solution.py:767
  17.0 0.6 %collective-permute-start.7 = (bf16[2,64,256]{2,1,0:T(8,128)(2,1)S(1)}, bf16[2,64,256]{2,1,0:T(8,128)(2,1)S(1)}, u32[]{:S(2)}, u32[]{:S(2)}) collective-permute-start(bf16[2,64,256]{2,1,0:T(8,128)(2,1)S(1)} %inner.7), channel_id=1, source_target_pairs={{0,4},{4,0},{8,12},{12,8},{1,5},{5,1},{9,13},{13,9},{2,6},{6,2},{1... | collective-permute-start | bytes 196616 | tf_op jit(solution)/shard_map/ppermute | solution.py:785
  17.6 0.0 collective-permute-done.1.other_ref
  17.6 0.7 %inner.4.after_ref.rest_3_ = bf16[2,64,256]{2,1,0:T(8,128)(2,1)S(1)} custom-call(bf16[4,8,16,256]{3,2,1,0:T(8,128)(2,1)S(1)} %keep.1.keep_ref, bf16[1,8,16,256]{3,2,1,0:T(8,128)(2,1)S(1)} %collective-permute-done.1.other_ref, bf16[8,128,64]{2,1,0:T(8,128)(2,1)S(1)} %get-tuple-element.21.first_ref, bf16[6,64,64]{2,1,0:T(8,128)(2,1)S(1)} %get-tuple-element.22.inner_ref, ...), custom_call_target="tpu_custom_call" | custom-call | tf_op jit(solution)/shard_map/inner/pallas_call | solution.py:767
  18.3 0.7 %outer_tables.1 = (bf16[6,64,64]{2,1,0:T(8,128)(2,1)S(1)}, f32[6,2,64,256]{3,2,1,0:T(8,128)S(1)}) custom-call(s32[1,64]{1,0:T(1,128)S(1)} %bitcast.5, s32[64,64]{1,0:T(8,128)S(1)} %bitcast.3, bf16[2,64,256]{2,1,0:T(8,128)(2,1)S(1)} %inner.4.after_ref.rest_3_), custom_call_target="tpu_custom_call" | custom-call | tf_op jit(solution)/shard_map/outer_tables/pallas_call | solution.py:787
  19.0 0.0 collective-permute-done.3.rest_0_
  19.0 2.5 %collective-permute-done.5.rest_1_ = bf16[2,64,256]{2,1,0:T(8,128)(2,1)S(1)} collective-permute-done((bf16[2,64,256]{2,1,0:T(8,128)(2,1)S(1)}, bf16[2,64,256]{2,1,0:T(8,128)(2,1)S(1)}, u32[]{:S(2)}, u32[]{:S(2)}) %collective-permute-start.5) | collective-permute-done | bytes 65568 | tf_op jit(solution)/shard_map/ppermute | solution.py:785
  21.5 0.5 %collective-permute-done.7.rest_2_ = bf16[2,64,256]{2,1,0:T(8,128)(2,1)S(1)} collective-permute-done((bf16[2,64,256]{2,1,0:T(8,128)(2,1)S(1)}, bf16[2,64,256]{2,1,0:T(8,128)(2,1)S(1)}, u32[]{:S(2)}, u32[]{:S(2)}) %collective-permute-start.7) | collective-permute-done | bytes 65568 | tf_op jit(solution)/shard_map/ppermute | solution.py:785
  22.0 1.0 %outer.1 = f32[2,64,256]{2,1,0:T(8,128)} custom-call(bf16[6,64,64]{2,1,0:T(8,128)(2,1)S(1)} %get-tuple-element.24.outer_ref, f32[6,2,64,256]{3,2,1,0:T(8,128)S(1)} %get-tuple-element.25.phase_ref, bf16[2,64,256]{2,1,0:T(8,128)(2,1)S(1)} %collective-permute-done.3.rest_0_, bf16[2,64,256]{2,1,0:T(8,128)(2,1)S(1)} %collective-permute-done.5.rest_1_, ...), custom_call_target="tpu_custom_call" | custom-call | tf_op jit(solution)/shard_map/outer/pallas_call | solution.py:798
Async XLA Ops:
  0.0 1.8 %copy-start = (bf16[16,256,256]{2,1,0:T(8,128)(2,1)S(1)}, bf16[16,256,256]{2,1,0:T(8,128)(2,1)}, u32[]{:S(2)}) copy-start(bf16[16,256,256]{2,1,0:T(8,128)(2,1)} %constant.4.clone.bands_ref) | copy-start | bytes 6291460
  0.0 1.2 %copy-start.4 = (bf16[2,8,8,2048]{3,2,1,0:T(8,128)(2,1)S(1)}, bf16[2,8,8,2048]{3,2,1,0:T(8,128)(2,1)}, u32[]{:S(2)}) copy-start(bf16[2,8,8,2048]{3,2,1,0:T(8,128)(2,1)} %echo_hbm.1) | copy-start | bytes 1572868
  1.3 1.5 %copy-start.1 = (bf16[768,256]{1,0:T(8,128)(2,1)S(1)}, bf16[768,256]{1,0:T(8,128)(2,1)}, u32[]{:S(2)}) copy-start(bf16[768,256]{1,0:T(8,128)(2,1)} %constant.5.clone.chirp_ref) | copy-start | bytes 1179652
  1.3 1.5 %collective-permute-start = (bf16[2,8,8,384]{3,2,1,0:T(8,128)(2,1)S(1)}, bf16[2,8,8,384]{3,2,1,0:T(8,128)(2,1)S(1)}, u32[]{:S(2)}, u32[]{:S(2)}) collective-permute-start(bf16[2,8,8,384]{3,2,1,0:T(8,128)(2,1)S(1)} %get-tuple-element.18), channel_id=1, source_target_pairs={{0,1},{1,0},{2,3},{3,2},{4,5},{5,4},{6,7},{7,6},{8,9},{9,8},{10,11... | collective-permute-start | bytes 294920 | tf_op jit(solution)/shard_map/ppermute | solution.py:35
  2.7 6.0 %copy-start.2 = (s32[32,2,64]{2,1,0:T(2,128)S(1)}, s32[32,2,64]{2,1,0:T(2,128)}, u32[]{:S(2)}) copy-start(s32[32,2,64]{2,1,0:T(2,128)} %param.7) | copy-start | bytes 49156
  2.7 6.0 %copy-start.3 = (s32[64]{0:T(128)S(1)}, s32[64]{0:T(128)}, u32[]{:S(2)}) copy-start(s32[64]{0:T(128)} %param.6) | copy-start | bytes 772
  3.7 7.0 %collective-permute-start.2 = (bf16[1,8,16,256]{3,2,1,0:T(8,128)(2,1)S(1)}, bf16[1,8,16,256]{3,2,1,0:T(8,128)(2,1)S(1)}, u32[]{:S(2)}, u32[]{:S(2)}) collective-permute-start(bf16[1,8,16,256]{3,2,1,0:T(8,128)(2,1)S(1)} %get-tuple-element.26), channel_id=1, source_target_pairs={{0,2},{2,0},{1,3},{3,1},{4,6},{6,4},{5,7},{7,5},{8,10},{10,8},{9,1... | collective-permute-start | bytes 196616 | tf_op jit(solution)/shard_map/ppermute | solution.py:35
  6.6 8.8 %collective-permute-start.4 = (bf16[1,8,16,256]{3,2,1,0:T(8,128)(2,1)S(1)}, bf16[1,8,16,256]{3,2,1,0:T(8,128)(2,1)S(1)}, u32[]{:S(2)}, u32[]{:S(2)}) collective-permute-start(bf16[1,8,16,256]{3,2,1,0:T(8,128)(2,1)S(1)} %get-tuple-element.27), channel_id=1, source_target_pairs={{0,2},{2,0},{1,3},{3,1},{4,6},{6,4},{5,7},{7,5},{8,10},{10,8},{9,1... | collective-permute-start | bytes 196616 | tf_op jit(solution)/shard_map/ppermute | solution.py:35
  6.7 9.6 %collective-permute-start.6 = (bf16[1,8,16,256]{3,2,1,0:T(8,128)(2,1)S(1)}, bf16[1,8,16,256]{3,2,1,0:T(8,128)(2,1)S(1)}, u32[]{:S(2)}, u32[]{:S(2)}) collective-permute-start(bf16[1,8,16,256]{3,2,1,0:T(8,128)(2,1)S(1)} %get-tuple-element.28), channel_id=1, source_target_pairs={{0,2},{2,0},{1,3},{3,1},{4,6},{6,4},{5,7},{7,5},{8,10},{10,8},{9,1... | collective-permute-start | bytes 196616 | tf_op jit(solution)/shard_map/ppermute | solution.py:35
  10.5 7.1 %collective-permute-start.1 = (bf16[1,8,16,256]{3,2,1,0:T(8,128)(2,1)S(1)}, bf16[1,8,16,256]{3,2,1,0:T(8,128)(2,1)S(1)}, u32[]{:S(2)}, u32[]{:S(2)}) collective-permute-start(bf16[1,8,16,256]{3,2,1,0:T(8,128)(2,1)S(1)} %get-tuple-element.20), channel_id=1, source_target_pairs={{0,2},{2,0},{1,3},{3,1},{4,6},{6,4},{5,7},{7,5},{8,10},{10,8},{9,1... | collective-permute-start | bytes 196616 | tf_op jit(solution)/shard_map/ppermute | solution.py:35
  11.4 7.7 %collective-permute-start.3 = (bf16[2,64,256]{2,1,0:T(8,128)(2,1)S(1)}, bf16[2,64,256]{2,1,0:T(8,128)(2,1)S(1)}, u32[]{:S(2)}, u32[]{:S(2)}) collective-permute-start(bf16[2,64,256]{2,1,0:T(8,128)(2,1)S(1)} %inner.5), channel_id=1, source_target_pairs={{0,12},{4,8},{8,4},{12,0},{1,13},{5,9},{9,5},{13,1},{2,14},{6,10},... | collective-permute-start | bytes 196616 | tf_op jit(solution)/shard_map/ppermute | solution.py:785
  16.2 5.3 %collective-permute-start.5 = (bf16[2,64,256]{2,1,0:T(8,128)(2,1)S(1)}, bf16[2,64,256]{2,1,0:T(8,128)(2,1)S(1)}, u32[]{:S(2)}, u32[]{:S(2)}) collective-permute-start(bf16[2,64,256]{2,1,0:T(8,128)(2,1)S(1)} %inner.6), channel_id=1, source_target_pairs={{0,8},{4,12},{8,0},{12,4},{1,9},{5,13},{9,1},{13,5},{2,10},{6,14},... | collective-permute-start | bytes 196616 | tf_op jit(solution)/shard_map/ppermute | solution.py:785
  17.0 5.0 %collective-permute-start.7 = (bf16[2,64,256]{2,1,0:T(8,128)(2,1)S(1)}, bf16[2,64,256]{2,1,0:T(8,128)(2,1)S(1)}, u32[]{:S(2)}, u32[]{:S(2)}) collective-permute-start(bf16[2,64,256]{2,1,0:T(8,128)(2,1)S(1)} %inner.7), channel_id=1, source_target_pairs={{0,4},{4,0},{8,12},{12,8},{1,5},{5,1},{9,13},{13,9},{2,6},{6,2},{1... | collective-permute-start | bytes 196616 | tf_op jit(solution)/shard_map/ppermute | solution.py:785

commit v4 on v3

--- a/solution.py
+++ b/solution.py
@@ -273,20 +273,6 @@
     return np.concatenate(bands, axis=-1).astype(ml_dtypes.bfloat16)
 
 
-def edge_kernel(echo_hbm, edge_ref, echo_ref, arrived):
-    length = echo_hbm.shape[3]
-    start = jnp.where(lax.axis_index("rng") == 0, length - HALO, 0)
-    start = pl.multiple_of(start, LANES)
-    edge = pltpu.make_async_copy(
-        echo_hbm.at[:, :, :, pl.ds(start, HALO)], edge_ref, arrived.at[0]
-    )
-    edge.start()
-    whole = pltpu.make_async_copy(echo_hbm, echo_ref, arrived.at[1])
-    whole.start()
-    edge.wait()
-    whole.wait()
-
-
 def filter_channel(windows, bands, pulses):
     product = jnp.dot(windows, bands, preferred_element_type=jnp.float32)
     product = product.reshape(-1, 2, pulses, 2 * LANES)
@@ -295,7 +281,12 @@
     return real, imag
 
 
-def interior_kernel(echo_ref, bands_ref, filtered_ref, rows_in, rows_out):
+def mask_kernel(mask_ref):
+    lane = lax.broadcasted_iota(jnp.int32, mask_ref.shape, 1)
+    mask_ref[...] = jnp.where(lane >= LANES - RTAPS // 2, 1.0, 0.0)
+
+
+def interior_kernel(echo_ref, bands_ref, mask_ref, filtered_ref, rows_in, rows_out):
     _, pulses, channels, length = echo_ref.shape
     first_channel = lax.axis_index("rx") * channels
     tiles = length // LANES
@@ -309,7 +300,7 @@
             block = echo_ref[part, pulse].astype(jnp.float32)
             for tile in range(tiles):
                 rows_in[tile + 1, where, :] = block[:, tile * LANES : (tile + 1) * LANES]
-    lane = lax.broadcasted_iota(jnp.int32, (1, LANES), 1)
+    mask = mask_ref[...]
     for channel in range(channels):
         rows = rows_in[:, channel * group : (channel + 1) * group, :].astype(jnp.bfloat16)
         windows = jnp.concatenate(
@@ -319,11 +310,9 @@
         for tile in range(tiles + 1):
             tile_re, tile_im = real[tile], imag[tile]
             if tile == 0:
-                tile_re = jnp.where(lane >= LANES - RTAPS // 2, tile_re, 0.0)
-                tile_im = jnp.where(lane >= LANES - RTAPS // 2, tile_im, 0.0)
+                tile_re, tile_im = tile_re * mask, tile_im * mask
             if tile == tiles:
-                tile_re = jnp.where(lane < LANES - RTAPS // 2, tile_re, 0.0)
-                tile_im = jnp.where(lane < LANES - RTAPS // 2, tile_im, 0.0)
+                tile_re, tile_im = tile_re * (1.0 - mask), tile_im * (1.0 - mask)
             rows_out[tile, pl.ds(channel, pulses, stride=2 * channels), :] = tile_re
             rows_out[tile, pl.ds(channels + channel, pulses, stride=2 * channels), :] = tile_im
     rows = filtered_ref.shape[0]
@@ -363,7 +352,7 @@
 
 
 def edges_kernel(
-    plan, inner_ref, echo_ref, edge_ref, bands_ref, chirp_ref, filtered_ref, *rest
+    plan, inner_ref, echo_ref, across_ref, bands_ref, chirp_ref, filtered_ref, *rest
 ):
     *send_refs, rows_in, rows_out = rest
     del inner_ref
@@ -372,10 +361,11 @@
     tiles = length // LANES
     group = 2 * pulses
     lowest = lax.axis_index("rng") == 0
+    far = pl.ds(pl.multiple_of(jnp.where(lowest, 0, length - HALO), LANES), HALO)
     for part in range(2):
         for pulse in range(pulses):
             where = pl.ds(part * pulses + pulse, channels, stride=group)
-            edge = edge_ref[part, pulse].astype(jnp.float32)
+            edge = across_ref[part, pulse, :, far].astype(jnp.float32)
             near_low = echo_ref[part, pulse, :, :LANES].astype(jnp.float32)
             near_high = echo_ref[part, pulse, :, length - LANES :].astype(jnp.float32)
             pieces = [edge[:, t * LANES : (t + 1) * LANES] for t in range(HALO_TILES)]
@@ -403,12 +393,12 @@
         )
 
 
-def chirp_kernel(partner, piece_count, groups, filtered_ref, chirp_ref, *out_refs):
-    out_refs = out_refs[len(out_refs) - len(groups) :]
+def rest_kernel(piece_count, groups, filtered_ref, chirp_ref, after_ref, keep_ref, *send_refs):
     rx_place = lax.axis_index("rx")
-    owner = 1 - rx_place if partner else rx_place
-    for distances, out_ref in zip(groups, out_refs):
-        chirp_pieces(filtered_ref, chirp_ref, owner, piece_count, distances, out_ref)
+    own = list(range(piece_count - 1, -1, -1))
+    chirp_pieces(filtered_ref, chirp_ref, rx_place, piece_count, own, keep_ref)
+    for distances, send_ref in zip(groups, send_refs):
+        chirp_pieces(filtered_ref, chirp_ref, 1 - rx_place, piece_count, distances, send_ref)
 
 
 def turn_parts(step):
@@ -657,6 +647,12 @@
     out_ref[1] = pictures[0][1]
 
 
+def cost(micros):
+    return pl.CostEstimate(
+        flops=int(micros * 1.1e9), bytes_accessed=int(micros * 3.6e6), transcendentals=0
+    )
+
+
 PARAMS = dict(compiler_params=pltpu.CompilerParams(vmem_limit_bytes=40 * 1024 * 1024))
 
 
@@ -664,7 +660,7 @@
     last = pulse_count - 1
     if pulse_count < 4:
         return [[distance] for distance in range(last, -1, -1)]
-    return [[distance] for distance in range(last, -1, -1)]
+    return [[last, last - 1], list(range(last - 2, -1, -1))]
 
 
 def fast(echoes, beam_angle, interp_table):
@@ -684,23 +680,21 @@
     bf16 = jnp.bfloat16
     f32 = jnp.float32
     shape = jax.ShapeDtypeStruct
-    edge, echoes = pl.pallas_call(
-        edge_kernel,
-        out_shape=[shape(echoes.shape[:3] + (HALO,), bf16), shape(echoes.shape, bf16)],
-        in_specs=[hbm()],
-        out_specs=[vmem(), vmem()],
-        scratch_shapes=[pltpu.SemaphoreType.DMA((2,))],
-        name="edge",
-        cost_estimate=pl.CostEstimate(flops=10**10, bytes_accessed=10**8, transcendentals=0),
+    across = swapped(echoes, "rng", 0)
+    mask = pl.pallas_call(
+        mask_kernel,
+        out_shape=shape((pulses, LANES), f32),
+        out_specs=vmem(),
+        name="mask",
+        cost_estimate=cost(10.0),
         **PARAMS,
-    )(echoes)
-    edge = swapped(edge, "rng", 0)
+    )()
     tiles = length // LANES
     filtered_shape = shape((rows * pulses, (tiles + 2 * HALO_TILES - 1) * LANES), bf16)
     filtered = pl.pallas_call(
         interior_kernel,
         out_shape=filtered_shape,
-        in_specs=[vmem()] * 2,
+        in_specs=[vmem()] * 3,
         out_specs=vmem(),
         scratch_shapes=[
             pltpu.VMEM((tiles + 2, channels * group, LANES), f32),
@@ -708,18 +702,18 @@
         ],
         name="interior",
         **PARAMS,
-    )(echoes, bands)
+    )(echoes, bands, mask)
 
     def pieces(count):
         return shape((count, pulses, rows, piece_width), bf16)
 
     last = pulse_count - 1
     groups = send_groups(pulse_count)
-    filtered, *sent = pl.pallas_call(
-        functools.partial(edges_kernel, (pulse_count, groups)),
-        out_shape=[filtered_shape] + [pieces(len(members)) for members in groups],
+    filtered, first_sent = pl.pallas_call(
+        functools.partial(edges_kernel, (pulse_count, groups[:1])),
+        out_shape=[filtered_shape, pieces(len(groups[0]))],
         in_specs=[vmem()] * 5,
-        out_specs=[vmem()] * (1 + len(groups)),
+        out_specs=[vmem()] * 2,
         scratch_shapes=[
             pltpu.VMEM((HALO_TILES + 1, channels * group, LANES), f32),
             pltpu.VMEM((HALO_TILES, rows * pulses, LANES), f32),
@@ -727,26 +721,7 @@
         input_output_aliases={0: 0},
         name="edges",
         **PARAMS,
-    )(filtered, echoes, edge, bands, chirp)
-    received = {}
-
-    def receive(members, piece):
-        piece = swapped(piece, "rx", 0)
-        for index, distance in enumerate(members):
-            received[distance] = (piece, index)
-
-    for index in [*range(len(groups) - 2, -1, -1), len(groups) - 1]:
-        receive(groups[index], sent[index])
-    kept = pl.pallas_call(
-        functools.partial(
-            chirp_kernel, False, pulse_count, [[last - index for index in range(pulse_count)]]
-        ),
-        out_shape=[pieces(pulse_count)],
-        in_specs=[vmem()] * 2,
-        out_specs=[vmem()],
-        name="keep",
-        **PARAMS,
-    )(filtered, chirp)[0]
+    )(filtered, echoes, across, bands, chirp)
     levels = pulses.bit_length() - 1
     first, inner, phase = pl.pallas_call(
         functools.partial(tables_kernel, (pulses, channels, rx_count, width)),
@@ -760,6 +735,19 @@
         name="tables",
         **PARAMS,
     )(angles, codes)
+    kept, *sent = pl.pallas_call(
+        functools.partial(rest_kernel, pulse_count, groups[1:]),
+        out_shape=[pieces(pulse_count)] + [pieces(len(members)) for members in groups[1:]],
+        in_specs=[vmem()] * 2 + [anywhere()],
+        out_specs=[vmem()] * len(groups),
+        name="rest",
+        **PARAMS,
+    )(filtered, chirp, first)
+    received = {}
+    for members, piece in zip(groups, [first_sent, *sent]):
+        piece = swapped(piece, "rx", 0)
+        for index, distance in enumerate(members):
+            received[distance] = (piece, index)
     images = [None] * pulse_count
 
     def merge(distance):

time: 23.2 us -> 22.2 us (0.957)
  starting transfers between devices: 10.4 us -> 8.16 us
  waiting for transfers between devices: 3.01 us -> 4.33 us
    ppermute x5 -> x3, starting transfers between devices: 5.63 us -> 3.55 us  [swapped(): lax.ppermute(x, axis, [(i, i ^ 1 << distance) for i in range(lax.axis_siz...]
    ppermute x5 -> x3, waiting for transfers between devices: 0.03 us -> 1.36 us  [swapped(): lax.ppermute(x, axis, [(i, i ^ 1 << distance) for i in range(lax.axis_siz...]
  transfers between devices with their start and end apart: 8 -> 6, of which waited for: 2 -> 3; matrix products, arithmetic and copies ran while one was open for 0% -> 0% of each run, Pallas kernels for 27% -> 29%
where the time goes in v4:
time: 22.2 us; the launch traced here: 22 us
  starting transfers between devices  8.16 us (37%)
  Pallas kernels  8.12 us (37%)
  waiting for transfers between devices  4.33 us (20%)
  local copies, waits for them, and re-layouts  1.29 us (6%)
    ppermute x3, starting transfers between devices, fast(): images[distance] = lax.ppermute(images[distance], 'pulse', pairs)  4.61 us
    ppermute x3, starting transfers between devices, swapped(): lax.ppermute(x, axis, [(i, i ^ 1 << distance) for i in range(lax.axis_siz...  3.55 us
    ppermute x3, waiting for transfers between devices, fast(): images[distance] = lax.ppermute(images[distance], 'pulse', pairs)  2.97 us
    pallas_call x4, Pallas kernels, merge(): pl.pallas_call(functools.partial(inner_kernel, last - distance, place), o...  2.73 us
    ppermute x3, waiting for transfers between devices, swapped(): lax.ppermute(x, axis, [(i, i ^ 1 << distance) for i in range(lax.axis_siz...  1.36 us
    unnamed x10, local copies, waits for them, and re-layouts  1.29 us
    pallas_call x1, Pallas kernels, fast(): pl.pallas_call(functools.partial(tables_kernel, (pulses, channels, rx_cou...  1.24 us
    pallas_call x1, Pallas kernels, fast(): pl.pallas_call(outer_kernel, out_shape=shape((2, beams, piece_width), f32...  1.02 us
  transfers between devices with their start and end apart: 6, of which 3 were waited for; matrix products, arithmetic and copies ran while one was open for 0% of the time, Pallas kernels for 29%

profile of v4, /device:TPU:0, one launch (start us, length us, event | category | flops | bytes accessed | tf_op | source)
XLA Modules:
  0.0 22.0 jit_solution(15332054970089612310)
XLA Ops:
  0.0 0.0 copy-start
  0.0 0.0 copy-start.1
  0.0 0.5 %collective-permute-start = (bf16[2,8,8,2048]{3,2,1,0:T(8,128)(2,1)}, bf16[2,8,8,2048]{3,2,1,0:T(8,128)(2,1)S(1)}, u32[]{:S(2)}, u32[]{:S(2)}) collective-permute-start(bf16[2,8,8,2048]{3,2,1,0:T(8,128)(2,1)} %echo_ref.3), channel_id=1, source_target_pairs={{0,1},{1,0},{2,3},{3,2},{4,5},{5,4},{6,7},{7,6},{8,9},{9,8},{10,11... | collective-permute-start | bytes 1572872 | tf_op jit(solution)/shard_map/ppermute | solution.py:35
  0.5 1.1 %copy-done = bf16[16,256,256]{2,1,0:T(8,128)(2,1)S(1)} copy-done((bf16[16,256,256]{2,1,0:T(8,128)(2,1)S(1)}, bf16[16,256,256]{2,1,0:T(8,128)(2,1)}, u32[]{:S(2)}) %copy-start) | copy-done | bytes 2097176
  1.6 0.1 copy-done.1
  1.7 0.0 copy-start.2
  1.7 0.9 %interior.1.inner_ref = bf16[128,2688]{1,0:T(8,128)(2,1)S(1)} custom-call(bf16[2,8,8,2048]{3,2,1,0:T(8,128)(2,1)S(1)} %copy-done.1, bf16[16,256,256]{2,1,0:T(8,128)(2,1)S(1)} %copy-done, f32[8,128]{1,0:T(8,128)S(1)} %mask.1.mask_ref), custom_call_target="tpu_custom_call" | custom-call | tf_op jit(solution)/shard_map/interior/pallas_call | solution.py:694
  2.6 0.0 copy-start.3
  2.6 0.0 copy-start.4
  2.6 0.0 collective-permute-done.across_ref
  2.6 0.1 copy-done.2
  2.7 0.7 %edges.1 = (bf16[128,2688]{1,0:T(8,128)(2,1)S(1)}, bf16[2,8,16,256]{3,2,1,0:T(8,128)(2,1)S(1)}) custom-call(bf16[128,2688]{1,0:T(8,128)(2,1)S(1)} %interior.1.inner_ref, bf16[2,8,8,2048]{3,2,1,0:T(8,128)(2,1)S(1)} %copy-done.1, bf16[2,8,8,2048]{3,2,1,0:T(8,128)(2,1)S(1)} %collective-permute-done.across_ref, ...), custom_call_target="tpu_custom_call", output_to_operand_aliasing={{0}: (0, {})} | custom-call | tf_op jit(solution)/shard_map/edges/pallas_call | solution.py:712
  3.4 3.0 %collective-permute-start.2 = (bf16[2,8,16,256]{3,2,1,0:T(8,128)(2,1)S(1)}, bf16[2,8,16,256]{3,2,1,0:T(8,128)(2,1)S(1)}, u32[]{:S(2)}, u32[]{:S(2)}) collective-permute-start(bf16[2,8,16,256]{3,2,1,0:T(8,128)(2,1)S(1)} %get-tuple-element.22), channel_id=1, source_target_pairs={{0,2},{2,0},{1,3},{3,1},{4,6},{6,4},{5,7},{7,5},{8,10},{10,8},{9,1... | collective-permute-start | bytes 393224 | tf_op jit(solution)/shard_map/ppermute | solution.py:35
  6.4 0.0 copy-done.3
  6.4 0.0 copy-done.4
  6.4 1.2 %tables.1 = (bf16[8,128,64]{2,1,0:T(8,128)(2,1)S(1)}, bf16[6,64,64]{2,1,0:T(8,128)(2,1)S(1)}, f32[4,4,2,64,256]{4,3,2,1,0:T(8,128)S(1)}) custom-call(s32[1,64]{1,0:T(1,128)S(1)} %bitcast.4, s32[64,64]{1,0:T(8,128)S(1)} %bitcast.2), custom_call_target="tpu_custom_call" | custom-call | tf_op jit(solution)/shard_map/tables/pallas_call | solution.py:726
  7.6 0.8 %rest.1 = (bf16[4,8,16,256]{3,2,1,0:T(8,128)(2,1)S(1)}, bf16[2,8,16,256]{3,2,1,0:T(8,128)(2,1)S(1)}) custom-call(bf16[128,2688]{1,0:T(8,128)(2,1)S(1)} %get-tuple-element.14.filtered_ref, bf16[768,256]{1,0:T(8,128)(2,1)S(1)} %copy-done.2, bf16[8,128,64]{2,1,0:T(8,128)(2,1)S(1)} %get-tuple-element.15.after_ref.first_ref), custom_call_target="tpu_custom_call" | custom-call | tf_op jit(solution)/shard_map/rest/pallas_call | solution.py:738
  8.4 0.1 collective-permute-start.1
  8.5 1.4 %collective-permute-done.2.other_ref = bf16[2,8,16,256]{3,2,1,0:T(8,128)(2,1)S(1)} collective-permute-done((bf16[2,8,16,256]{3,2,1,0:T(8,128)(2,1)S(1)}, bf16[2,8,16,256]{3,2,1,0:T(8,128)(2,1)S(1)}, u32[]{:S(2)}, u32[]{:S(2)}) %collective-permute-start.2) | collective-permute-done | bytes 131104 | tf_op jit(solution)/shard_map/ppermute | solution.py:35
  9.9 0.7 %inner.5 = bf16[2,64,256]{2,1,0:T(8,128)(2,1)S(1)} custom-call(bf16[4,8,16,256]{3,2,1,0:T(8,128)(2,1)S(1)} %get-tuple-element.16.keep_ref, bf16[2,8,16,256]{3,2,1,0:T(8,128)(2,1)S(1)} %collective-permute-done.2.other_ref, bf16[8,128,64]{2,1,0:T(8,128)(2,1)S(1)} %get-tuple-element.15.after_ref.first_ref, bf16[6,64,64]{2,1,0:T(8,128)(2,1)S(1)} %get-tuple-element.18.inner_ref, ...), custom_call_target="tpu_custom_call" | custom-call | tf_op jit(solution)/shard_map/inner/pallas_call | solution.py:755
  10.6 3.9 %collective-permute-start.3 = (bf16[2,64,256]{2,1,0:T(8,128)(2,1)S(1)}, bf16[2,64,256]{2,1,0:T(8,128)(2,1)S(1)}, u32[]{:S(2)}, u32[]{:S(2)}) collective-permute-start(bf16[2,64,256]{2,1,0:T(8,128)(2,1)S(1)} %inner.5), channel_id=1, source_target_pairs={{0,12},{4,8},{8,4},{12,0},{1,13},{5,9},{9,5},{13,1},{2,14},{6,10},... | collective-permute-start | bytes 196616 | tf_op jit(solution)/shard_map/ppermute | solution.py:773
  14.5 0.7 %inner.6 = bf16[2,64,256]{2,1,0:T(8,128)(2,1)S(1)} custom-call(bf16[4,8,16,256]{3,2,1,0:T(8,128)(2,1)S(1)} %get-tuple-element.16.keep_ref, bf16[2,8,16,256]{3,2,1,0:T(8,128)(2,1)S(1)} %collective-permute-done.2.other_ref, bf16[8,128,64]{2,1,0:T(8,128)(2,1)S(1)} %get-tuple-element.15.after_ref.first_ref, bf16[6,64,64]{2,1,0:T(8,128)(2,1)S(1)} %get-tuple-element.18.inner_ref, ...), custom_call_target="tpu_custom_call" | custom-call | tf_op jit(solution)/shard_map/inner/pallas_call | solution.py:755
  15.2 0.1 collective-permute-start.4
  15.3 0.0 collective-permute-done.1.other_ref
  15.3 0.7 %inner.7 = bf16[2,64,256]{2,1,0:T(8,128)(2,1)S(1)} custom-call(bf16[4,8,16,256]{3,2,1,0:T(8,128)(2,1)S(1)} %get-tuple-element.16.keep_ref, bf16[2,8,16,256]{3,2,1,0:T(8,128)(2,1)S(1)} %collective-permute-done.1.other_ref, bf16[8,128,64]{2,1,0:T(8,128)(2,1)S(1)} %get-tuple-element.15.after_ref.first_ref, bf16[6,64,64]{2,1,0:T(8,128)(2,1)S(1)} %get-tuple-element.18.inner_ref, ...), custom_call_target="tpu_custom_call" | custom-call | tf_op jit(solution)/shard_map/inner/pallas_call | solution.py:755
  16.0 0.6 %collective-permute-start.5 = (bf16[2,64,256]{2,1,0:T(8,128)(2,1)S(1)}, bf16[2,64,256]{2,1,0:T(8,128)(2,1)S(1)}, u32[]{:S(2)}, u32[]{:S(2)}) collective-permute-start(bf16[2,64,256]{2,1,0:T(8,128)(2,1)S(1)} %inner.7), channel_id=1, source_target_pairs={{0,4},{4,0},{8,12},{12,8},{1,5},{5,1},{9,13},{13,9},{2,6},{6,2},{1... | collective-permute-start | bytes 196616 | tf_op jit(solution)/shard_map/ppermute | solution.py:773
  16.6 0.7 %inner.4.after_ref.rest_3_ = bf16[2,64,256]{2,1,0:T(8,128)(2,1)S(1)} custom-call(bf16[4,8,16,256]{3,2,1,0:T(8,128)(2,1)S(1)} %get-tuple-element.16.keep_ref, bf16[2,8,16,256]{3,2,1,0:T(8,128)(2,1)S(1)} %collective-permute-done.1.other_ref, bf16[8,128,64]{2,1,0:T(8,128)(2,1)S(1)} %get-tuple-element.15.after_ref.first_ref, ...), custom_call_target="tpu_custom_call" | custom-call | tf_op jit(solution)/shard_map/inner/pallas_call | solution.py:755
  17.3 0.7 %outer_tables.1 = (bf16[6,64,64]{2,1,0:T(8,128)(2,1)S(1)}, f32[6,2,64,256]{3,2,1,0:T(8,128)S(1)}) custom-call(s32[1,64]{1,0:T(1,128)S(1)} %bitcast.5, s32[64,64]{1,0:T(8,128)S(1)} %bitcast.3, bf16[2,64,256]{2,1,0:T(8,128)(2,1)S(1)} %inner.4.after_ref.rest_3_), custom_call_target="tpu_custom_call" | custom-call | tf_op jit(solution)/shard_map/outer_tables/pallas_call | solution.py:775
  18.0 0.0 collective-permute-done.3.rest_0_
  18.0 2.5 %collective-permute-done.4.rest_1_ = bf16[2,64,256]{2,1,0:T(8,128)(2,1)S(1)} collective-permute-done((bf16[2,64,256]{2,1,0:T(8,128)(2,1)S(1)}, bf16[2,64,256]{2,1,0:T(8,128)(2,1)S(1)}, u32[]{:S(2)}, u32[]{:S(2)}) %collective-permute-start.4) | collective-permute-done | bytes 65568 | tf_op jit(solution)/shard_map/ppermute | solution.py:773
  20.5 0.5 %collective-permute-done.5.rest_2_ = bf16[2,64,256]{2,1,0:T(8,128)(2,1)S(1)} collective-permute-done((bf16[2,64,256]{2,1,0:T(8,128)(2,1)S(1)}, bf16[2,64,256]{2,1,0:T(8,128)(2,1)S(1)}, u32[]{:S(2)}, u32[]{:S(2)}) %collective-permute-start.5) | collective-permute-done | bytes 65568 | tf_op jit(solution)/shard_map/ppermute | solution.py:773
  21.0 1.0 %outer.1 = f32[2,64,256]{2,1,0:T(8,128)} custom-call(bf16[6,64,64]{2,1,0:T(8,128)(2,1)S(1)} %get-tuple-element.20.outer_ref, f32[6,2,64,256]{3,2,1,0:T(8,128)S(1)} %get-tuple-element.21.phase_ref, bf16[2,64,256]{2,1,0:T(8,128)(2,1)S(1)} %collective-permute-done.3.rest_0_, bf16[2,64,256]{2,1,0:T(8,128)(2,1)S(1)} %collective-permute-done.4.rest_1_, ...), custom_call_target="tpu_custom_call" | custom-call | tf_op jit(solution)/shard_map/outer/pallas_call | solution.py:786
  (1 shorter events, 0.0 us)
Async XLA Ops:
  0.0 1.6 %copy-start = (bf16[16,256,256]{2,1,0:T(8,128)(2,1)S(1)}, bf16[16,256,256]{2,1,0:T(8,128)(2,1)}, u32[]{:S(2)}) copy-start(bf16[16,256,256]{2,1,0:T(8,128)(2,1)} %constant.4.clone.bands_ref) | copy-start | bytes 6291460
  0.0 1.7 %copy-start.1 = (bf16[2,8,8,2048]{3,2,1,0:T(8,128)(2,1)S(1)}, bf16[2,8,8,2048]{3,2,1,0:T(8,128)(2,1)}, u32[]{:S(2)}) copy-start(bf16[2,8,8,2048]{3,2,1,0:T(8,128)(2,1)} %echo_ref.3) | copy-start | bytes 1572868
  0.0 2.6 %collective-permute-start = (bf16[2,8,8,2048]{3,2,1,0:T(8,128)(2,1)}, bf16[2,8,8,2048]{3,2,1,0:T(8,128)(2,1)S(1)}, u32[]{:S(2)}, u32[]{:S(2)}) collective-permute-start(bf16[2,8,8,2048]{3,2,1,0:T(8,128)(2,1)} %echo_ref.3), channel_id=1, source_target_pairs={{0,1},{1,0},{2,3},{3,2},{4,5},{5,4},{6,7},{7,6},{8,9},{9,8},{10,11... | collective-permute-start | bytes 1572872 | tf_op jit(solution)/shard_map/ppermute | solution.py:35
  1.7 1.0 %copy-start.2 = (bf16[768,256]{1,0:T(8,128)(2,1)S(1)}, bf16[768,256]{1,0:T(8,128)(2,1)}, u32[]{:S(2)}) copy-start(bf16[768,256]{1,0:T(8,128)(2,1)} %constant.5.clone.chirp_ref) | copy-start | bytes 1179652
  2.6 3.8 %copy-start.3 = (s32[32,2,64]{2,1,0:T(2,128)S(1)}, s32[32,2,64]{2,1,0:T(2,128)}, u32[]{:S(2)}) copy-start(s32[32,2,64]{2,1,0:T(2,128)} %param.7) | copy-start | bytes 49156
  2.6 3.8 %copy-start.4 = (s32[64]{0:T(128)S(1)}, s32[64]{0:T(128)}, u32[]{:S(2)}) copy-start(s32[64]{0:T(128)} %param.6) | copy-start | bytes 772
  3.4 6.5 %collective-permute-start.2 = (bf16[2,8,16,256]{3,2,1,0:T(8,128)(2,1)S(1)}, bf16[2,8,16,256]{3,2,1,0:T(8,128)(2,1)S(1)}, u32[]{:S(2)}, u32[]{:S(2)}) collective-permute-start(bf16[2,8,16,256]{3,2,1,0:T(8,128)(2,1)S(1)} %get-tuple-element.22), channel_id=1, source_target_pairs={{0,2},{2,0},{1,3},{3,1},{4,6},{6,4},{5,7},{7,5},{8,10},{10,8},{9,1... | collective-permute-start | bytes 393224 | tf_op jit(solution)/shard_map/ppermute | solution.py:35
  8.4 6.8 %collective-permute-start.1 = (bf16[2,8,16,256]{3,2,1,0:T(8,128)(2,1)S(1)}, bf16[2,8,16,256]{3,2,1,0:T(8,128)(2,1)S(1)}, u32[]{:S(2)}, u32[]{:S(2)}) collective-permute-start(bf16[2,8,16,256]{3,2,1,0:T(8,128)(2,1)S(1)} %get-tuple-element.17), channel_id=1, source_target_pairs={{0,2},{2,0},{1,3},{3,1},{4,6},{6,4},{5,7},{7,5},{8,10},{10,8},{9,1... | collective-permute-start | bytes 393224 | tf_op jit(solution)/shard_map/ppermute | solution.py:35
  10.6 7.5 %collective-permute-start.3 = (bf16[2,64,256]{2,1,0:T(8,128)(2,1)S(1)}, bf16[2,64,256]{2,1,0:T(8,128)(2,1)S(1)}, u32[]{:S(2)}, u32[]{:S(2)}) collective-permute-start(bf16[2,64,256]{2,1,0:T(8,128)(2,1)S(1)} %inner.5), channel_id=1, source_target_pairs={{0,12},{4,8},{8,4},{12,0},{1,13},{5,9},{9,5},{13,1},{2,14},{6,10},... | collective-permute-start | bytes 196616 | tf_op jit(solution)/shard_map/ppermute | solution.py:773
  15.2 5.3 %collective-permute-start.4 = (bf16[2,64,256]{2,1,0:T(8,128)(2,1)S(1)}, bf16[2,64,256]{2,1,0:T(8,128)(2,1)S(1)}, u32[]{:S(2)}, u32[]{:S(2)}) collective-permute-start(bf16[2,64,256]{2,1,0:T(8,128)(2,1)S(1)} %inner.6), channel_id=1, source_target_pairs={{0,8},{4,12},{8,0},{12,4},{1,9},{5,13},{9,1},{13,5},{2,10},{6,14},... | collective-permute-start | bytes 196616 | tf_op jit(solution)/shard_map/ppermute | solution.py:773
  16.0 5.0 %collective-permute-start.5 = (bf16[2,64,256]{2,1,0:T(8,128)(2,1)S(1)}, bf16[2,64,256]{2,1,0:T(8,128)(2,1)S(1)}, u32[]{:S(2)}, u32[]{:S(2)}) collective-permute-start(bf16[2,64,256]{2,1,0:T(8,128)(2,1)S(1)} %inner.7), channel_id=1, source_target_pairs={{0,4},{4,0},{8,12},{12,8},{1,5},{5,1},{9,13},{13,9},{2,6},{6,2},{1... | collective-permute-start | bytes 196616 | tf_op jit(solution)/shard_map/ppermute | solution.py:773

commit v5 on v4

--- a/solution.py
+++ b/solution.py
@@ -243,22 +243,6 @@
     return pl.BlockSpec(memory_space=pl.ANY)
 
 
-def rx_bands_table(receivers):
-    step = np.arange(RTAPS, dtype=np.float64)
-    window = 0.5 - 0.5 * np.cos(full_turn * (step + 0.5) / RTAPS)
-    window = window / np.sqrt(np.sum(window * window))
-    channel = np.arange(receivers, dtype=np.float64)[:, None] + 1.0
-    angle = full_turn * channel * (step - RTAPS // 2) / (4 * RTAPS)
-    offset = np.arange(RX_TILE)[:, None] - np.arange(LANES)[None, :]
-    inside = (offset >= 0) & (offset < RTAPS)
-    place = np.clip(offset, 0, RTAPS - 1)
-    bands = [
-        np.where(inside, taps[:, place], 0.0)
-        for taps in (window * np.cos(angle), window * np.sin(angle))
-    ]
-    return np.concatenate(bands, axis=-1).astype(ml_dtypes.bfloat16)
-
-
 def chirp_bands_table():
     offset = np.arange(CTAPS) - CTAPS // 2
     angle = math.pi * np.mod(offset * offset, 2 * CTAPS) / CTAPS
@@ -281,14 +265,30 @@
     return real, imag
 
 
-def mask_kernel(mask_ref):
-    lane = lax.broadcasted_iota(jnp.int32, mask_ref.shape, 1)
-    mask_ref[...] = jnp.where(lane >= LANES - RTAPS // 2, 1.0, 0.0)
-
-
-def interior_kernel(echo_ref, bands_ref, mask_ref, filtered_ref, rows_in, rows_out):
+def bands_kernel(bands_ref):
+    channels = bands_ref.shape[0]
+    first_channel = lax.axis_index("rx") * channels
+    lane = lax.broadcasted_iota(jnp.int32, (channels, LANES), 1)
+    channel = lax.broadcasted_iota(jnp.int32, (channels, LANES), 0) + first_channel + 1
+    tap = jnp.bitwise_and(LANES - lane, LANES - 1)
+    unit = 1024 // RTAPS
+    window = 0.5 - 0.5 * turn_parts(tap * unit + unit // 2)[0]
+    window = jnp.where(tap < RTAPS, window * (1.0 / math.sqrt(RTAPS * 3 / 8)), 0.0)
+    turn = channel * (tap - RTAPS // 2) * (1024 // (4 * RTAPS))
+    row = lax.broadcasted_iota(jnp.int32, (LANES, LANES), 0)
+    upper = lax.broadcasted_iota(jnp.int32, (LANES, LANES), 1) <= row
+    for part, wave in enumerate(turn_parts(jnp.bitwise_and(turn, 1023))):
+        taps = window * wave
+        span = slice(part * LANES, (part + 1) * LANES)
+        for index in range(channels):
+            spread = jnp.broadcast_to(taps[index : index + 1], (LANES, LANES))
+            rolled = pltpu.roll(spread, 0, 1, stride=1, stride_axis=0)
+            bands_ref[index, :LANES, span] = jnp.where(upper, rolled, 0.0).astype(jnp.bfloat16)
+            bands_ref[index, LANES:, span] = jnp.where(upper, 0.0, rolled).astype(jnp.bfloat16)
+
+
+def interior_kernel(echo_ref, bands_ref, filtered_ref, rows_in, rows_out):
     _, pulses, channels, length = echo_ref.shape
-    first_channel = lax.axis_index("rx") * channels
     tiles = length // LANES
     group = 2 * pulses
     empty = jnp.zeros(rows_in.shape[1:], jnp.float32)
@@ -300,13 +300,14 @@
             block = echo_ref[part, pulse].astype(jnp.float32)
             for tile in range(tiles):
                 rows_in[tile + 1, where, :] = block[:, tile * LANES : (tile + 1) * LANES]
-    mask = mask_ref[...]
+    lane = lax.broadcasted_iota(jnp.int32, (pulses, LANES), 1)
+    mask = jnp.where(lane >= LANES - RTAPS // 2, 1.0, 0.0)
     for channel in range(channels):
         rows = rows_in[:, channel * group : (channel + 1) * group, :].astype(jnp.bfloat16)
         windows = jnp.concatenate(
             [rows[:-1].reshape(-1, LANES), rows[1:].reshape(-1, LANES)], axis=1
         )
-        real, imag = filter_channel(windows, bands_ref[first_channel + channel], pulses)
+        real, imag = filter_channel(windows, bands_ref[channel], pulses)
         for tile in range(tiles + 1):
             tile_re, tile_im = real[tile], imag[tile]
             if tile == 0:
@@ -357,7 +358,6 @@
     *send_refs, rows_in, rows_out = rest
     del inner_ref
     _, pulses, channels, length = echo_ref.shape
-    first_channel = lax.axis_index("rx") * channels
     tiles = length // LANES
     group = 2 * pulses
     lowest = lax.axis_index("rng") == 0
@@ -378,7 +378,7 @@
         windows = jnp.concatenate(
             [rows[:-1].reshape(-1, LANES), rows[1:].reshape(-1, LANES)], axis=1
         )
-        real, imag = filter_channel(windows, bands_ref[first_channel + channel], pulses)
+        real, imag = filter_channel(windows, bands_ref[channel], pulses)
         for tile in range(HALO_TILES):
             rows_out[tile, pl.ds(channel, pulses, stride=2 * channels), :] = real[tile]
             rows_out[tile, pl.ds(channels + channel, pulses, stride=2 * channels), :] = imag[tile]
@@ -450,21 +450,16 @@
     return picked.T.astype(jnp.int32)
 
 
-def tables_kernel(sizes, angle_ref, codes_ref, first_ref, inner_ref, phase_ref):
-    pulses, channels, rx_count, width = sizes
-    rng_place = lax.axis_index("rng")
+def weights_kernel(sizes, angle_ref, codes_ref, after_ref, first_ref, inner_ref):
+    pulses, channels, rx_count, piece_count = sizes
     rx_place = lax.axis_index("rx")
     pulse_place = lax.axis_index("pulse")
     beams = angle_ref.shape[1]
-    piece_count = phase_ref.shape[0]
-    piece_tiles = phase_ref.shape[4] // LANES
     angle = as_column(angle_ref[...])
-    factors = []
     rows = []
     now = pulses
     while now > 1:
         base = now * piece_count + pulse_place * now
-        factors.append(base + 1)
         rows.extend(base + index for index in range(now))
         now //= 2
     codes = code_columns(codes_ref, rows)
@@ -501,6 +496,22 @@
             ).astype(jnp.bfloat16)
     for index, matrix in enumerate(matrices[pulses:]):
         inner_ref[index] = matrix
+
+
+def phases_kernel(sizes, angle_ref, phase_ref):
+    pulses, rx_count, width = sizes
+    rng_place = lax.axis_index("rng")
+    rx_place = lax.axis_index("rx")
+    pulse_place = lax.axis_index("pulse")
+    piece_count = phase_ref.shape[0]
+    piece_tiles = phase_ref.shape[4] // LANES
+    angle = as_column(angle_ref[...])
+    factors = []
+    now = pulses
+    while now > 1:
+        base = now * piece_count + pulse_place * now
+        factors.extend(base + 1 + index for index in range(0, now, 2))
+        now //= 2
     lane = lax.broadcasted_iota(jnp.int32, (1, LANES), 1)
     block = (rng_place * rx_count + rx_place) * width + 1
     base = jnp.bitwise_and(angle * (block + lane), 1023)
@@ -548,73 +559,81 @@
 ROWS = 8
 
 
-def inner_kernel(index, other, keep_ref, other_ref, first_ref, inner_ref, phase_ref, *rest):
-    out_ref, moved_ref, picture_ref, level_ref = rest[-4:]
+def inner_kernel(indices, keep_ref, other_ref, first_ref, inner_ref, phase_ref, *rest):
+    *out_refs, moved_ref, picture_ref, level_ref = rest
     pulses = keep_ref.shape[1]
-    beams = inner_ref.shape[1]
-    columns = keep_ref.shape[3]
-    for image in range(pulses):
-        rows = jnp.concatenate([keep_ref[index, image], other_ref[other, image]], axis=0)
-        moved_ref[image] = jnp.dot(
-            first_ref[image],
-            jnp.concatenate([rows, rows], axis=0),
-            preferred_element_type=jnp.float32,
-        )
-
-    def merge(count, level, read, write):
+    beams, columns = out_refs[0].shape[1:]
+    pieces = range(len(indices))
+
+    def merge(piece, count, base, read, write):
+        index = indices[piece]
         for row in range(0, beams, ROWS):
             span = slice(row, row + ROWS)
             step = (phase_ref[index, 0, 0, span], phase_ref[index, 0, 1, span])
-            phase = (phase_ref[index, level, 0, span], phase_ref[index, level, 1, span])
-            for image in range(count):
-                term = turned(*read(image, row), *phase)
-                if image & 1:
-                    write(image // 2, row, left[0] + term[0], left[1] + term[1])
-                left = term
-                if image < count - 1:
-                    phase = turned(*phase, *step)
-
-    def write_picture(image, row, real, imag):
-        picture_ref[image, row : row + ROWS, :columns] = real
-        picture_ref[image, row : row + ROWS, columns:] = imag
-
-    def write_out(image, row, real, imag):
-        picture_ref[0, row : row + ROWS, :columns] = real
-        picture_ref[0, row : row + ROWS, columns:] = imag
-
-    merge(
-        pulses,
-        1,
-        lambda image, row: (
-            moved_ref[image, row : row + ROWS],
-            moved_ref[image, beams + row : beams + row + ROWS],
-        ),
-        write_picture,
-    )
-    slot = 0
-    level = 2
+            for image in range(0, count, 2):
+                slot = base + image // 2
+                left = read(image, row)
+                right = turned(*read(image + 1, row), *step)
+                phase = (phase_ref[index, slot, 0, span], phase_ref[index, slot, 1, span])
+                write(
+                    image // 2, row, *turned(left[0] + right[0], left[1] + right[1], *phase)
+                )
+
+    def lift(piece, image, slot):
+        level_ref[piece, image] = jnp.dot(
+            inner_ref[slot],
+            picture_ref[piece, image].astype(jnp.bfloat16),
+            preferred_element_type=jnp.float32,
+        )
+
+    for piece in pieces:
+        for image in range(pulses):
+            rows = jnp.concatenate(
+                [keep_ref[indices[piece], image], other_ref[piece, image]], axis=0
+            )
+            moved_ref[piece, image] = jnp.dot(
+                first_ref[image],
+                jnp.concatenate([rows, rows], axis=0),
+                preferred_element_type=jnp.float32,
+            )
+
+    def read_first(piece):
+        return lambda image, row: (
+            moved_ref[piece, image, row : row + ROWS],
+            moved_ref[piece, image, beams + row : beams + row + ROWS],
+        )
+
+    def read_level(piece):
+        return lambda image, row: (
+            level_ref[piece, image, row : row + ROWS, :columns],
+            level_ref[piece, image, row : row + ROWS, columns:],
+        )
+
+    def write_picture(piece):
+        def write(image, row, real, imag):
+            picture_ref[piece, image, row : row + ROWS, :columns] = real
+            picture_ref[piece, image, row : row + ROWS, columns:] = imag
+
+        return write
+
+    for piece in pieces:
+        merge(piece, pulses, 1, read_first(piece), write_picture(piece))
+        for image in range(pulses // 2):
+            lift(piece, image, image)
+    base = 1 + pulses // 2
+    slot = pulses // 2
     count = pulses // 2
     while count > 1:
-        for image in range(count):
-            level_ref[image] = jnp.dot(
-                inner_ref[slot],
-                picture_ref[image].astype(jnp.bfloat16),
-                preferred_element_type=jnp.float32,
-            )
-            slot += 1
-        merge(
-            count,
-            level,
-            lambda image, row: (
-                level_ref[image, row : row + ROWS, :columns],
-                level_ref[image, row : row + ROWS, columns:],
-            ),
-            write_picture,
-        )
+        for piece in pieces:
+            merge(piece, count, base, read_level(piece), write_picture(piece))
+            for image in range(count // 2 if count > 2 else 0):
+                lift(piece, image, slot + image)
         count //= 2
-        level += 1
-    out_ref[0] = picture_ref[0, :, :columns].astype(jnp.bfloat16)
-    out_ref[1] = picture_ref[0, :, columns:].astype(jnp.bfloat16)
+        base += count
+        slot += count
+    for piece in pieces:
+        out_refs[piece][0] = picture_ref[piece, 0, :, :columns].astype(jnp.bfloat16)
+        out_refs[piece][1] = picture_ref[piece, 0, :, columns:].astype(jnp.bfloat16)
 
 
 def outer_kernel(outer_ref, phase_ref, *rest):
@@ -673,7 +692,6 @@
     piece_tiles = piece_width // LANES
     rows = 2 * channels
     group = 2 * pulses
-    bands = jnp.asarray(rx_bands_table(channels * rx_count))
     chirp = jnp.asarray(chirp_bands_table())
     angles = beam_angle.reshape(1, beams)
     codes = interp_table.reshape(-1, beams)
@@ -681,11 +699,11 @@
     f32 = jnp.float32
     shape = jax.ShapeDtypeStruct
     across = swapped(echoes, "rng", 0)
-    mask = pl.pallas_call(
-        mask_kernel,
-        out_shape=shape((pulses, LANES), f32),
+    bands = pl.pallas_call(
+        bands_kernel,
+        out_shape=shape((channels, RX_TILE, 2 * LANES), bf16),
         out_specs=vmem(),
-        name="mask",
+        name="bands",
         cost_estimate=cost(10.0),
         **PARAMS,
     )()
@@ -694,7 +712,7 @@
     filtered = pl.pallas_call(
         interior_kernel,
         out_shape=filtered_shape,
-        in_specs=[vmem()] * 3,
+        in_specs=[vmem()] * 2,
         out_specs=vmem(),
         scratch_shapes=[
             pltpu.VMEM((tiles + 2, channels * group, LANES), f32),
@@ -702,7 +720,7 @@
         ],
         name="interior",
         **PARAMS,
-    )(echoes, bands, mask)
+    )(echoes, bands)
 
     def pieces(count):
         return shape((count, pulses, rows, piece_width), bf16)
@@ -722,19 +740,14 @@
         name="edges",
         **PARAMS,
     )(filtered, echoes, across, bands, chirp)
-    levels = pulses.bit_length() - 1
-    first, inner, phase = pl.pallas_call(
-        functools.partial(tables_kernel, (pulses, channels, rx_count, width)),
-        out_shape=[
-            shape((pulses, 2 * beams, 8 * channels), bf16),
-            shape((pulses - 2, beams, beams), bf16),
-            shape((pulse_count, levels + 1, 2, beams, piece_width), f32),
-        ],
-        in_specs=[vmem()] * 2,
-        out_specs=[vmem()] * 3,
-        name="tables",
+    phase = pl.pallas_call(
+        functools.partial(phases_kernel, (pulses, rx_count, width)),
+        out_shape=shape((pulse_count, pulses, 2, beams, piece_width), f32),
+        in_specs=[vmem()],
+        out_specs=vmem(),
+        name="phases",
         **PARAMS,
-    )(angles, codes)
+    )(angles)
     kept, *sent = pl.pallas_call(
         functools.partial(rest_kernel, pulse_count, groups[1:]),
         out_shape=[pieces(pulse_count)] + [pieces(len(members)) for members in groups[1:]],
@@ -742,32 +755,37 @@
         out_specs=[vmem()] * len(groups),
         name="rest",
         **PARAMS,
-    )(filtered, chirp, first)
-    received = {}
+    )(filtered, chirp, phase)
+    first, inner = pl.pallas_call(
+        functools.partial(weights_kernel, (pulses, channels, rx_count, pulse_count)),
+        out_shape=[
+            shape((pulses, 2 * beams, 8 * channels), bf16),
+            shape((pulses - 2, beams, beams), bf16),
+        ],
+        in_specs=[vmem()] * 2 + [anywhere()],
+        out_specs=[vmem()] * 2,
+        name="weights",
+        **PARAMS,
+    )(angles, codes, kept)
+    images = [None] * pulse_count
     for members, piece in zip(groups, [first_sent, *sent]):
-        piece = swapped(piece, "rx", 0)
-        for index, distance in enumerate(members):
-            received[distance] = (piece, index)
-    images = [None] * pulse_count
-
-    def merge(distance):
-        other, place = received[distance]
-        return pl.pallas_call(
-            functools.partial(inner_kernel, last - distance, place),
-            out_shape=shape((2, beams, piece_width), bf16),
+        other = swapped(piece, "rx", 0)
+        size = len(members)
+        merged = pl.pallas_call(
+            functools.partial(inner_kernel, [last - distance for distance in members]),
+            out_shape=[shape((2, beams, piece_width), bf16)] * size,
             in_specs=[vmem()] * 5,
-            out_specs=vmem(),
+            out_specs=[vmem()] * size,
             scratch_shapes=[
-                pltpu.VMEM((pulses, 2 * beams, piece_width), f32),
-                pltpu.VMEM((pulses // 2, beams, 2 * piece_width), f32),
-                pltpu.VMEM((pulses // 2, beams, 2 * piece_width), f32),
+                pltpu.VMEM((size, pulses, 2 * beams, piece_width), f32),
+                pltpu.VMEM((size, pulses // 2, beams, 2 * piece_width), f32),
+                pltpu.VMEM((size, pulses // 2, beams, 2 * piece_width), f32),
             ],
             name="inner",
             **PARAMS,
         )(kept, other, first, inner, phase)
-
-    for distance in [*range(1, pulse_count), 0]:
-        images[distance] = merge(distance)
+        for distance, image in zip(members, merged):
+            images[distance] = image
     for distance in range(1, pulse_count):
         pairs = [(i, i ^ distance) for i in range(pulse_count)]
         images[distance] = lax.ppermute(images[distance], "pulse", pairs)

time: 22.2 us -> 21.4 us (0.964)
  local copies, waits for them, and re-layouts: 1.29 us -> 0.37 us
  waiting for transfers between devices: 4.33 us -> 4.84 us
    unnamed x10 -> x8, local copies, waits for them, and re-layouts: 1.29 us -> 0.37 us
    ppermute x3, waiting for transfers between devices: 2.97 us -> 3.61 us  [fast(): images[distance] = lax.ppermute(images[distance], 'pulse', pairs)]
    pallas_call x6 -> x5, Pallas kernels: 3.97 us -> 3.78 us  [the longest x2 1.62 us: fast(): pl.pallas_call(functools.partial(inner_kernel, [last - distance for dista...]
  transfers between devices with their start and end apart: 6 -> 6, of which waited for: 3 -> 5; matrix products, arithmetic and copies ran while one was open for 0% -> 0% of each run, Pallas kernels for 29% -> 29%
where the time goes in v5:
time: 21.4 us; the launch traced here: 21.3 us
  starting transfers between devices  8.1 us (38%)
  Pallas kernels  7.92 us (37%)
  waiting for transfers between devices  4.84 us (23%)
  local copies, waits for them, and re-layouts  0.37 us (2%)
    ppermute x3, starting transfers between devices, fast(): images[distance] = lax.ppermute(images[distance], 'pulse', pairs)  4.62 us
    ppermute x3, waiting for transfers between devices, fast(): images[distance] = lax.ppermute(images[distance], 'pulse', pairs)  3.61 us
    ppermute x3, starting transfers between devices, swapped(): lax.ppermute(x, axis, [(i, i ^ 1 << distance) for i in range(lax.axis_siz...  3.47 us
    pallas_call x2, Pallas kernels, fast(): pl.pallas_call(functools.partial(inner_kernel, [last - distance for dista...  1.62 us
    ppermute x3, waiting for transfers between devices, swapped(): lax.ppermute(x, axis, [(i, i ^ 1 << distance) for i in range(lax.axis_siz...  1.22 us
    pallas_call x1, Pallas kernels, fast(): pl.pallas_call(functools.partial(phases_kernel, (pulses, rx_count, width)...  1.19 us
    pallas_call x1, Pallas kernels, fast(): pl.pallas_call(outer_kernel, out_shape=shape((2, beams, piece_width), f32...  1.02 us
    pallas_call x1, Pallas kernels, fast(): pl.pallas_call(interior_kernel, out_shape=filtered_shape, in_specs=[vmem(...  0.88 us
  transfers between devices with their start and end apart: 6, of which 5 were waited for; matrix products, arithmetic and copies ran while one was open for 0% of the time, Pallas kernels for 29%

profile of v5, /device:TPU:0, one launch (start us, length us, event | category | flops | bytes accessed | tf_op | source)
XLA Modules:
  0.0 21.3 jit_solution(16321810509833955091)
XLA Ops:
  0.0 0.0 copy-start.1
  0.0 0.0 copy-start
  0.0 0.5 %collective-permute-start = (bf16[2,8,8,2048]{3,2,1,0:T(8,128)(2,1)}, bf16[2,8,8,2048]{3,2,1,0:T(8,128)(2,1)S(1)}, u32[]{:S(2)}, u32[]{:S(2)}) collective-permute-start(bf16[2,8,8,2048]{3,2,1,0:T(8,128)(2,1)} %echo_ref.3), channel_id=1, source_target_pairs={{0,1},{1,0},{2,3},{3,2},{4,5},{5,4},{6,7},{7,6},{8,9},{9,8},{10,11... | collective-permute-start | bytes 1572872 | tf_op jit(solution)/shard_map/ppermute | solution.py:35
  0.5 0.3 %bands.1.bands_ref = bf16[8,256,256]{2,1,0:T(8,128)(2,1)S(1)} custom-call(), custom_call_target="tpu_custom_call" | custom-call | flops 11000000512 | bytes 36000000 | tf_op jit(solution)/shard_map/bands/pallas_call | solution.py:702
  0.7 0.4 %copy-done = bf16[2,8,8,2048]{3,2,1,0:T(8,128)(2,1)S(1)} copy-done((bf16[2,8,8,2048]{3,2,1,0:T(8,128)(2,1)S(1)}, bf16[2,8,8,2048]{3,2,1,0:T(8,128)(2,1)}, u32[]{:S(2)}) %copy-start) | copy-done | bytes 524312
  1.1 0.0 copy-start.3
  1.1 0.9 %interior.1.inner_ref = bf16[128,2688]{1,0:T(8,128)(2,1)S(1)} custom-call(bf16[2,8,8,2048]{3,2,1,0:T(8,128)(2,1)S(1)} %copy-done, bf16[8,256,256]{2,1,0:T(8,128)(2,1)S(1)} %bands.1.bands_ref), custom_call_target="tpu_custom_call" | custom-call | tf_op jit(solution)/shard_map/interior/pallas_call | solution.py:712
  2.0 0.2 %collective-permute-done.across_ref = bf16[2,8,8,2048]{3,2,1,0:T(8,128)(2,1)S(1)} collective-permute-done((bf16[2,8,8,2048]{3,2,1,0:T(8,128)(2,1)}, bf16[2,8,8,2048]{3,2,1,0:T(8,128)(2,1)S(1)}, u32[]{:S(2)}, u32[]{:S(2)}) %collective-permute-start) | collective-permute-done | bytes 524320 | tf_op jit(solution)/shard_map/ppermute | solution.py:35
  2.2 0.0 copy-done.1
  2.2 0.7 %edges.1 = (bf16[128,2688]{1,0:T(8,128)(2,1)S(1)}, bf16[2,8,16,256]{3,2,1,0:T(8,128)(2,1)S(1)}) custom-call(bf16[128,2688]{1,0:T(8,128)(2,1)S(1)} %interior.1.inner_ref, bf16[2,8,8,2048]{3,2,1,0:T(8,128)(2,1)S(1)} %copy-done, bf16[2,8,8,2048]{3,2,1,0:T(8,128)(2,1)S(1)} %collective-permute-done.across_ref, ...), custom_call_target="tpu_custom_call", output_to_operand_aliasing={{0}: (0, {})} | custom-call | tf_op jit(solution)/shard_map/edges/pallas_call | solution.py:730
  2.9 2.9 %collective-permute-start.2 = (bf16[2,8,16,256]{3,2,1,0:T(8,128)(2,1)S(1)}, bf16[2,8,16,256]{3,2,1,0:T(8,128)(2,1)S(1)}, u32[]{:S(2)}, u32[]{:S(2)}) collective-permute-start(bf16[2,8,16,256]{3,2,1,0:T(8,128)(2,1)S(1)} %get-tuple-element.25), channel_id=1, source_target_pairs={{0,2},{2,0},{1,3},{3,1},{4,6},{6,4},{5,7},{7,5},{8,10},{10,8},{9,1... | collective-permute-start | bytes 393224 | tf_op jit(solution)/shard_map/ppermute | solution.py:35
  5.8 0.0 copy-done.3
  5.8 0.0 copy-start.2
  5.8 1.2 %phases.1.after_ref.phase_ref = f32[4,8,2,64,256]{4,3,2,1,0:T(8,128)S(1)} custom-call(s32[1,64]{1,0:T(1,128)S(1)} %bitcast.4), custom_call_target="tpu_custom_call" | custom-call | tf_op jit(solution)/shard_map/phases/pallas_call | solution.py:743
  7.0 0.8 %rest.1 = (bf16[4,8,16,256]{3,2,1,0:T(8,128)(2,1)S(1)}, bf16[2,8,16,256]{3,2,1,0:T(8,128)(2,1)S(1)}) custom-call(bf16[128,2688]{1,0:T(8,128)(2,1)S(1)} %get-tuple-element.17.filtered_ref, bf16[768,256]{1,0:T(8,128)(2,1)S(1)} %copy-done.1, f32[4,8,2,64,256]{4,3,2,1,0:T(8,128)S(1)} %phases.1.after_ref.phase_ref), custom_call_target="tpu_custom_call" | custom-call | tf_op jit(solution)/shard_map/rest/pallas_call | solution.py:751
  7.8 0.1 collective-permute-start.1
  7.9 0.0 copy-done.2
  7.9 0.7 %weights.1 = (bf16[8,128,64]{2,1,0:T(8,128)(2,1)S(1)}, bf16[6,64,64]{2,1,0:T(8,128)(2,1)S(1)}) custom-call(s32[1,64]{1,0:T(1,128)S(1)} %bitcast.5, s32[64,64]{1,0:T(8,128)S(1)} %bitcast.2, bf16[4,8,16,256]{3,2,1,0:T(8,128)(2,1)S(1)} %get-tuple-element.18.after_ref.keep_ref), custom_call_target="tpu_custom_call" | custom-call | tf_op jit(solution)/shard_map/weights/pallas_call | solution.py:759
  8.6 1.0 %collective-permute-done.2.other_ref = bf16[2,8,16,256]{3,2,1,0:T(8,128)(2,1)S(1)} collective-permute-done((bf16[2,8,16,256]{3,2,1,0:T(8,128)(2,1)S(1)}, bf16[2,8,16,256]{3,2,1,0:T(8,128)(2,1)S(1)}, u32[]{:S(2)}, u32[]{:S(2)}) %collective-permute-start.2) | collective-permute-done | bytes 131104 | tf_op jit(solution)/shard_map/ppermute | solution.py:35
  9.6 0.8 %inner.3 = (bf16[2,64,256]{2,1,0:T(8,128)(2,1)S(1)}, bf16[2,64,256]{2,1,0:T(8,128)(2,1)S(1)}) custom-call(bf16[4,8,16,256]{3,2,1,0:T(8,128)(2,1)S(1)} %get-tuple-element.18.after_ref.keep_ref, bf16[2,8,16,256]{3,2,1,0:T(8,128)(2,1)S(1)} %collective-permute-done.2.other_ref, bf16[8,128,64]{2,1,0:T(8,128)(2,1)S(1)} %get-tuple-element.20.first_ref, ...), custom_call_target="tpu_custom_call" | custom-call | tf_op jit(solution)/shard_map/inner/pallas_call | solution.py:774
  10.5 3.9 %collective-permute-start.3 = (bf16[2,64,256]{2,1,0:T(8,128)(2,1)S(1)}, bf16[2,64,256]{2,1,0:T(8,128)(2,1)S(1)}, u32[]{:S(2)}, u32[]{:S(2)}) collective-permute-start(bf16[2,64,256]{2,1,0:T(8,128)(2,1)S(1)} %get-tuple-element.26), channel_id=1, source_target_pairs={{0,12},{4,8},{8,4},{12,0},{1,13},{5,9},{9,5},{13,1},{2,14},{6,10},... | collective-permute-start | bytes 196616 | tf_op jit(solution)/shard_map/ppermute | solution.py:791
  14.4 0.0 collective-permute-start.4
  14.4 0.0 collective-permute-done.1.other_ref
  14.4 0.8 %inner.2 = (bf16[2,64,256]{2,1,0:T(8,128)(2,1)S(1)}, bf16[2,64,256]{2,1,0:T(8,128)(2,1)S(1)}) custom-call(bf16[4,8,16,256]{3,2,1,0:T(8,128)(2,1)S(1)} %get-tuple-element.18.after_ref.keep_ref, bf16[2,8,16,256]{3,2,1,0:T(8,128)(2,1)S(1)} %collective-permute-done.1.other_ref, bf16[8,128,64]{2,1,0:T(8,128)(2,1)S(1)} %get-tuple-element.20.first_ref, ...), custom_call_target="tpu_custom_call" | custom-call | tf_op jit(solution)/shard_map/inner/pallas_call | solution.py:774
  15.2 0.7 %collective-permute-start.5 = (bf16[2,64,256]{2,1,0:T(8,128)(2,1)S(1)}, bf16[2,64,256]{2,1,0:T(8,128)(2,1)S(1)}, u32[]{:S(2)}, u32[]{:S(2)}) collective-permute-start(bf16[2,64,256]{2,1,0:T(8,128)(2,1)S(1)} %get-tuple-element.28), channel_id=1, source_target_pairs={{0,4},{4,0},{8,12},{12,8},{1,5},{5,1},{9,13},{13,9},{2,6},{6,2},{1... | collective-permute-start | bytes 196616 | tf_op jit(solution)/shard_map/ppermute | solution.py:791
  15.9 0.7 %outer_tables.1 = (bf16[6,64,64]{2,1,0:T(8,128)(2,1)S(1)}, f32[6,2,64,256]{3,2,1,0:T(8,128)S(1)}) custom-call(s32[1,64]{1,0:T(1,128)S(1)} %bitcast.6, s32[64,64]{1,0:T(8,128)S(1)} %bitcast.3, bf16[2,64,256]{2,1,0:T(8,128)(2,1)S(1)} %get-tuple-element.22.after_ref.rest_3_), custom_call_target="tpu_custom_call" | custom-call | tf_op jit(solution)/shard_map/outer_tables/pallas_call | solution.py:793
  16.7 0.8 %collective-permute-done.3.rest_0_ = bf16[2,64,256]{2,1,0:T(8,128)(2,1)S(1)} collective-permute-done((bf16[2,64,256]{2,1,0:T(8,128)(2,1)S(1)}, bf16[2,64,256]{2,1,0:T(8,128)(2,1)S(1)}, u32[]{:S(2)}, u32[]{:S(2)}) %collective-permute-start.3) | collective-permute-done | bytes 65568 | tf_op jit(solution)/shard_map/ppermute | solution.py:791
  17.5 2.2 %collective-permute-done.4.rest_1_ = bf16[2,64,256]{2,1,0:T(8,128)(2,1)S(1)} collective-permute-done((bf16[2,64,256]{2,1,0:T(8,128)(2,1)S(1)}, bf16[2,64,256]{2,1,0:T(8,128)(2,1)S(1)}, u32[]{:S(2)}, u32[]{:S(2)}) %collective-permute-start.4) | collective-permute-done | bytes 65568 | tf_op jit(solution)/shard_map/ppermute | solution.py:791
  19.6 0.6 %collective-permute-done.5.rest_2_ = bf16[2,64,256]{2,1,0:T(8,128)(2,1)S(1)} collective-permute-done((bf16[2,64,256]{2,1,0:T(8,128)(2,1)S(1)}, bf16[2,64,256]{2,1,0:T(8,128)(2,1)S(1)}, u32[]{:S(2)}, u32[]{:S(2)}) %collective-permute-start.5) | collective-permute-done | bytes 65568 | tf_op jit(solution)/shard_map/ppermute | solution.py:791
  20.3 1.0 %outer.1 = f32[2,64,256]{2,1,0:T(8,128)} custom-call(bf16[6,64,64]{2,1,0:T(8,128)(2,1)S(1)} %get-tuple-element.23.outer_ref, f32[6,2,64,256]{3,2,1,0:T(8,128)S(1)} %get-tuple-element.24.phase_ref, bf16[2,64,256]{2,1,0:T(8,128)(2,1)S(1)} %collective-permute-done.3.rest_0_, bf16[2,64,256]{2,1,0:T(8,128)(2,1)S(1)} %collective-permute-done.4.rest_1_, ...), custom_call_target="tpu_custom_call" | custom-call | tf_op jit(solution)/shard_map/outer/pallas_call | solution.py:804
Async XLA Ops:
  0.0 2.2 %copy-start.1 = (bf16[768,256]{1,0:T(8,128)(2,1)S(1)}, bf16[768,256]{1,0:T(8,128)(2,1)}, u32[]{:S(2)}) copy-start(bf16[768,256]{1,0:T(8,128)(2,1)} %constant.2.clone.chirp_ref) | copy-start | bytes 1179652
  0.0 1.1 %copy-start = (bf16[2,8,8,2048]{3,2,1,0:T(8,128)(2,1)S(1)}, bf16[2,8,8,2048]{3,2,1,0:T(8,128)(2,1)}, u32[]{:S(2)}) copy-start(bf16[2,8,8,2048]{3,2,1,0:T(8,128)(2,1)} %echo_ref.3) | copy-start | bytes 1572868
  0.0 2.2 %collective-permute-start = (bf16[2,8,8,2048]{3,2,1,0:T(8,128)(2,1)}, bf16[2,8,8,2048]{3,2,1,0:T(8,128)(2,1)S(1)}, u32[]{:S(2)}, u32[]{:S(2)}) collective-permute-start(bf16[2,8,8,2048]{3,2,1,0:T(8,128)(2,1)} %echo_ref.3), channel_id=1, source_target_pairs={{0,1},{1,0},{2,3},{3,2},{4,5},{5,4},{6,7},{7,6},{8,9},{9,8},{10,11... | collective-permute-start | bytes 1572872 | tf_op jit(solution)/shard_map/ppermute | solution.py:35
  1.1 4.8 %copy-start.3 = (s32[64]{0:T(128)S(1)}, s32[64]{0:T(128)}, u32[]{:S(2)}) copy-start(s32[64]{0:T(128)} %param.5) | copy-start | bytes 772
  2.9 6.7 %collective-permute-start.2 = (bf16[2,8,16,256]{3,2,1,0:T(8,128)(2,1)S(1)}, bf16[2,8,16,256]{3,2,1,0:T(8,128)(2,1)S(1)}, u32[]{:S(2)}, u32[]{:S(2)}) collective-permute-start(bf16[2,8,16,256]{3,2,1,0:T(8,128)(2,1)S(1)} %get-tuple-element.25), channel_id=1, source_target_pairs={{0,2},{2,0},{1,3},{3,1},{4,6},{6,4},{5,7},{7,5},{8,10},{10,8},{9,1... | collective-permute-start | bytes 393224 | tf_op jit(solution)/shard_map/ppermute | solution.py:35
  5.8 2.1 %copy-start.2 = (s32[32,2,64]{2,1,0:T(2,128)S(1)}, s32[32,2,64]{2,1,0:T(2,128)}, u32[]{:S(2)}) copy-start(s32[32,2,64]{2,1,0:T(2,128)} %param.6) | copy-start | bytes 49156
  7.8 6.6 %collective-permute-start.1 = (bf16[2,8,16,256]{3,2,1,0:T(8,128)(2,1)S(1)}, bf16[2,8,16,256]{3,2,1,0:T(8,128)(2,1)S(1)}, u32[]{:S(2)}, u32[]{:S(2)}) collective-permute-start(bf16[2,8,16,256]{3,2,1,0:T(8,128)(2,1)S(1)} %get-tuple-element.19), channel_id=1, source_target_pairs={{0,2},{2,0},{1,3},{3,1},{4,6},{6,4},{5,7},{7,5},{8,10},{10,8},{9,1... | collective-permute-start | bytes 393224 | tf_op jit(solution)/shard_map/ppermute | solution.py:35
  10.5 7.0 %collective-permute-start.3 = (bf16[2,64,256]{2,1,0:T(8,128)(2,1)S(1)}, bf16[2,64,256]{2,1,0:T(8,128)(2,1)S(1)}, u32[]{:S(2)}, u32[]{:S(2)}) collective-permute-start(bf16[2,64,256]{2,1,0:T(8,128)(2,1)S(1)} %get-tuple-element.26), channel_id=1, source_target_pairs={{0,12},{4,8},{8,4},{12,0},{1,13},{5,9},{9,5},{13,1},{2,14},{6,10},... | collective-permute-start | bytes 196616 | tf_op jit(solution)/shard_map/ppermute | solution.py:791
  14.4 5.3 %collective-permute-start.4 = (bf16[2,64,256]{2,1,0:T(8,128)(2,1)S(1)}, bf16[2,64,256]{2,1,0:T(8,128)(2,1)S(1)}, u32[]{:S(2)}, u32[]{:S(2)}) collective-permute-start(bf16[2,64,256]{2,1,0:T(8,128)(2,1)S(1)} %get-tuple-element.27), channel_id=1, source_target_pairs={{0,8},{4,12},{8,0},{12,4},{1,9},{5,13},{9,1},{13,5},{2,10},{6,14},... | collective-permute-start | bytes 196616 | tf_op jit(solution)/shard_map/ppermute | solution.py:791
  15.2 5.1 %collective-permute-start.5 = (bf16[2,64,256]{2,1,0:T(8,128)(2,1)S(1)}, bf16[2,64,256]{2,1,0:T(8,128)(2,1)S(1)}, u32[]{:S(2)}, u32[]{:S(2)}) collective-permute-start(bf16[2,64,256]{2,1,0:T(8,128)(2,1)S(1)} %get-tuple-element.28), channel_id=1, source_target_pairs={{0,4},{4,0},{8,12},{12,8},{1,5},{5,1},{9,13},{13,9},{2,6},{6,2},{1... | collective-permute-start | bytes 196616 | tf_op jit(solution)/shard_map/ppermute | solution.py:791

commit v6 on v5

--- a/solution.py
+++ b/solution.py
@@ -225,7 +225,7 @@
 
 
 LANES = 128
-RX_TILE = 2 * LANES
+RX_TILE = LANES + RTAPS
 CHIRP_TILE = 6 * LANES
 HALO_TILES = 3
 HALO = HALO_TILES * LANES
@@ -284,7 +284,8 @@
             spread = jnp.broadcast_to(taps[index : index + 1], (LANES, LANES))
             rolled = pltpu.roll(spread, 0, 1, stride=1, stride_axis=0)
             bands_ref[index, :LANES, span] = jnp.where(upper, rolled, 0.0).astype(jnp.bfloat16)
-            bands_ref[index, LANES:, span] = jnp.where(upper, 0.0, rolled).astype(jnp.bfloat16)
+            lower = jnp.where(upper, 0.0, rolled)[:RTAPS]
+            bands_ref[index, LANES:, span] = lower.astype(jnp.bfloat16)
 
 
 def interior_kernel(echo_ref, bands_ref, filtered_ref, rows_in, rows_out):
@@ -305,7 +306,7 @@
     for channel in range(channels):
         rows = rows_in[:, channel * group : (channel + 1) * group, :].astype(jnp.bfloat16)
         windows = jnp.concatenate(
-            [rows[:-1].reshape(-1, LANES), rows[1:].reshape(-1, LANES)], axis=1
+            [rows[:-1].reshape(-1, LANES), rows[1:].reshape(-1, LANES)[:, :RTAPS]], axis=1
         )
         real, imag = filter_channel(windows, bands_ref[channel], pulses)
         for tile in range(tiles + 1):
@@ -325,31 +326,30 @@
         filtered_ref[:, spot : spot + LANES] = rows_out[tile].astype(jnp.bfloat16)
 
 
-def chirp_piece(filtered_ref, chirp_ref, starts, out_ref):
-    windows = [filtered_ref[:, pl.ds(start, CHIRP_TILE)] for start in starts]
+def chirp_pieces(filtered_ref, chirp_ref, owner, piece_count, distances, out_ref):
+    pulse_place = lax.axis_index("pulse")
+    _, pulses, rows, width = out_ref.shape
+    tiles = width // LANES
+    channels = rows // 2
+    windows = []
+    for distance in distances:
+        piece = jnp.bitwise_xor(pulse_place, distance)
+        first = (owner * piece_count + piece) * tiles
+        for tile in range(tiles):
+            start = pl.multiple_of((first + tile) * LANES, LANES)
+            windows.append(filtered_ref[:, pl.ds(start, CHIRP_TILE)])
     product = jnp.dot(
         jnp.concatenate(windows, axis=0), chirp_ref[...], preferred_element_type=jnp.float32
     )
-    pulses, rows, _ = out_ref.shape
-    channels = rows // 2
-    product = product.reshape(len(starts), pulses, rows, 2 * LANES)
-    for tile in range(len(starts)):
-        block = product[tile]
-        real = block[:, :channels, :LANES] - block[:, channels:, LANES:]
-        imag = block[:, :channels, LANES:] + block[:, channels:, :LANES]
-        out_ref[:, :, tile * LANES : (tile + 1) * LANES] = jnp.concatenate(
-            [real, imag], axis=1
-        ).astype(jnp.bfloat16)
-
-
-def chirp_pieces(filtered_ref, chirp_ref, owner, piece_count, distances, out_ref):
-    pulse_place = lax.axis_index("pulse")
-    piece_tiles = out_ref.shape[3] // LANES
-    for index, distance in enumerate(distances):
-        piece = jnp.bitwise_xor(pulse_place, distance)
-        first = (owner * piece_count + piece) * piece_tiles
-        starts = [pl.multiple_of((first + t) * LANES, LANES) for t in range(piece_tiles)]
-        chirp_piece(filtered_ref, chirp_ref, starts, out_ref.at[index])
+    product = product.reshape(len(windows), pulses, rows, 2 * LANES)
+    for index in range(len(distances)):
+        for tile in range(tiles):
+            block = product[index * tiles + tile]
+            real = block[:, :channels, :LANES] - block[:, channels:, LANES:]
+            imag = block[:, :channels, LANES:] + block[:, channels:, :LANES]
+            out_ref[index, :, :, tile * LANES : (tile + 1) * LANES] = jnp.concatenate(
+                [real, imag], axis=1
+            ).astype(jnp.bfloat16)
 
 
 def edges_kernel(
@@ -376,7 +376,7 @@
     for channel in range(channels):
         rows = rows_in[:, channel * group : (channel + 1) * group, :].astype(jnp.bfloat16)
         windows = jnp.concatenate(
-            [rows[:-1].reshape(-1, LANES), rows[1:].reshape(-1, LANES)], axis=1
+            [rows[:-1].reshape(-1, LANES), rows[1:].reshape(-1, LANES)[:, :RTAPS]], axis=1
         )
         real, imag = filter_channel(windows, bands_ref[channel], pulses)
         for tile in range(HALO_TILES):
@@ -498,7 +498,7 @@
         inner_ref[index] = matrix
 
 
-def phases_kernel(sizes, angle_ref, phase_ref):
+def phases_kernel(sizes, angle_ref, after_ref, phase_ref):
     pulses, rx_count, width = sizes
     rng_place = lax.axis_index("rng")
     rx_place = lax.axis_index("rx")
@@ -528,11 +528,14 @@
             real, imag = turned(real, imag, *step)
 
 
-def outer_levels(piece_count):
-    return [piece_count >> level for level in range(piece_count.bit_length() - 1)]
-
-
-def outer_tables_kernel(sizes, angle_ref, codes_ref, after_ref, outer_ref, phase_ref):
+def risen(outer_ref, phase_ref, slot, real, imag):
+    matrix = outer_ref[slot]
+    moved_re = jnp.dot(matrix, real.astype(jnp.bfloat16), preferred_element_type=jnp.float32)
+    moved_im = jnp.dot(matrix, imag.astype(jnp.bfloat16), preferred_element_type=jnp.float32)
+    return turned(moved_re, moved_im, phase_ref[slot, 0], phase_ref[slot, 1])
+
+
+def outer_tables_kernel(sizes, angle_ref, codes_ref, image_ref, outer_ref, phase_ref, own_ref):
     rx_count, width, piece_count = sizes
     rng_place = lax.axis_index("rng")
     rx_place = lax.axis_index("rx")
@@ -542,18 +545,17 @@
     lane = lax.broadcasted_iota(jnp.int32, (1, piece_width), 1)
     block = (rng_place * rx_count + rx_place) * width + 1
     base = jnp.bitwise_and(angle * (block + pulse_place * piece_width + lane), 1023)
-    rows = [row + level for level in outer_levels(piece_count) for row in range(level)]
+    counts = [piece_count >> level for level in range(piece_count.bit_length() - 1)]
+    rows = [count + index for count in counts for index in range(count)]
     codes = code_columns(codes_ref, rows)
-    slot = 0
-    now = piece_count
-    while now > 1:
-        for index in range(now):
-            outer_ref[slot] = interp_matrix(codes[:, slot : slot + 1])
-            real, imag = turn_parts(jnp.bitwise_and(base * (now + index + 1), 1023))
-            phase_ref[slot, 0] = real * half_root
-            phase_ref[slot, 1] = imag * half_root
-            slot += 1
-        now //= 2
+    for slot, row in enumerate(rows):
+        outer_ref[slot] = interp_matrix(codes[:, slot : slot + 1])
+        real, imag = turn_parts(jnp.bitwise_and(base * (row + 1), 1023))
+        phase_ref[slot, 0] = real * half_root
+        phase_ref[slot, 1] = imag * half_root
+    own_ref[0], own_ref[1] = risen(
+        outer_ref, phase_ref, pulse_place, image_ref[0], image_ref[1]
+    )
 
 
 ROWS = 8
@@ -636,34 +638,30 @@
         out_refs[piece][1] = picture_ref[piece, 0, :, columns:].astype(jnp.bfloat16)
 
 
-def outer_kernel(outer_ref, phase_ref, *rest):
-    image_refs, out_ref = rest[-2::-1], rest[-1]
+def far_kernel(distances, *rest):
+    *image_refs, outer_ref, phase_ref, far_ref = rest
     pulse_place = lax.axis_index("pulse")
-    pictures = [(ref[0], ref[1]) for ref in image_refs]
-    base = 0
-    level = 0
-    while len(pictures) > 1:
-        count = len(pictures)
-        place = jnp.right_shift(pulse_place, level)
-        merged = []
-        for distance, (real, imag) in enumerate(pictures):
-            slot = base + jnp.bitwise_xor(place, distance)
-            matrix = outer_ref[slot]
-            moved_re = jnp.dot(
-                matrix, real.astype(jnp.bfloat16), preferred_element_type=jnp.float32
-            )
-            moved_im = jnp.dot(
-                matrix, imag.astype(jnp.bfloat16), preferred_element_type=jnp.float32
-            )
-            merged.append(turned(moved_re, moved_im, phase_ref[slot, 0], phase_ref[slot, 1]))
-            if distance & 1:
-                right, left = merged.pop(), merged.pop()
-                merged.append((left[0] + right[0], left[1] + right[1]))
-        pictures = merged
-        base += count
-        level += 1
-    out_ref[0] = pictures[0][0]
-    out_ref[1] = pictures[0][1]
+    terms = [
+        risen(outer_ref, phase_ref, jnp.bitwise_xor(pulse_place, distance), ref[0], ref[1])
+        for distance, ref in zip(distances, image_refs)
+    ]
+    real = terms[0][0] + terms[1][0]
+    imag = terms[0][1] + terms[1][1]
+    half = jnp.bitwise_xor(jnp.right_shift(pulse_place, 1), 1)
+    far_ref[0], far_ref[1] = risen(outer_ref, phase_ref, 4 + half, real, imag)
+
+
+def near_kernel(far_ref, image_ref, own_ref, outer_ref, phase_ref, out_ref):
+    pulse_place = lax.axis_index("pulse")
+    near = risen(
+        outer_ref, phase_ref, jnp.bitwise_xor(pulse_place, 1), image_ref[0], image_ref[1]
+    )
+    real = own_ref[0] + near[0]
+    imag = own_ref[1] + near[1]
+    half = jnp.right_shift(pulse_place, 1)
+    real, imag = risen(outer_ref, phase_ref, 4 + half, real, imag)
+    out_ref[0] = real + far_ref[0]
+    out_ref[1] = imag + far_ref[1]
 
 
 def cost(micros):
@@ -673,13 +671,6 @@
 
 
 PARAMS = dict(compiler_params=pltpu.CompilerParams(vmem_limit_bytes=40 * 1024 * 1024))
-
-
-def send_groups(pulse_count):
-    last = pulse_count - 1
-    if pulse_count < 4:
-        return [[distance] for distance in range(last, -1, -1)]
-    return [[last, last - 1], list(range(last - 2, -1, -1))]
 
 
 def fast(echoes, beam_angle, interp_table):
@@ -726,7 +717,7 @@
         return shape((count, pulses, rows, piece_width), bf16)
 
     last = pulse_count - 1
-    groups = send_groups(pulse_count)
+    groups = [[3, 2], [1, 0]]
     filtered, first_sent = pl.pallas_call(
         functools.partial(edges_kernel, (pulse_count, groups[:1])),
         out_shape=[filtered_shape, pieces(len(groups[0]))],
@@ -743,16 +734,16 @@
     phase = pl.pallas_call(
         functools.partial(phases_kernel, (pulses, rx_count, width)),
         out_shape=shape((pulse_count, pulses, 2, beams, piece_width), f32),
-        in_specs=[vmem()],
+        in_specs=[vmem(), anywhere()],
         out_specs=vmem(),
         name="phases",
         **PARAMS,
-    )(angles)
+    )(angles, first_sent)
     kept, *sent = pl.pallas_call(
-        functools.partial(rest_kernel, pulse_count, groups[1:]),
-        out_shape=[pieces(pulse_count)] + [pieces(len(members)) for members in groups[1:]],
+        functools.partial(rest_kernel, pulse_count, groups[1:2]),
+        out_shape=[pieces(pulse_count), pieces(len(groups[1]))],
         in_specs=[vmem()] * 2 + [anywhere()],
-        out_specs=[vmem()] * len(groups),
+        out_specs=[vmem()] * 2,
         name="rest",
         **PARAMS,
     )(filtered, chirp, phase)
@@ -768,7 +759,8 @@
         **PARAMS,
     )(angles, codes, kept)
     images = [None] * pulse_count
-    for members, piece in zip(groups, [first_sent, *sent]):
+
+    def merge(members, piece):
         other = swapped(piece, "rx", 0)
         size = len(members)
         merged = pl.pallas_call(
@@ -782,33 +774,47 @@
                 pltpu.VMEM((size, pulses // 2, beams, 2 * piece_width), f32),
             ],
             name="inner",
+            cost_estimate=cost(3.0),
             **PARAMS,
         )(kept, other, first, inner, phase)
         for distance, image in zip(members, merged):
             images[distance] = image
+
+    merge(groups[0], first_sent)
+    merge(groups[1], sent[0])
     for distance in range(1, pulse_count):
         pairs = [(i, i ^ distance) for i in range(pulse_count)]
         images[distance] = lax.ppermute(images[distance], "pulse", pairs)
     outer_count = 2 * pulse_count - 2
-    outer, outer_phase = pl.pallas_call(
+    picture_shape = shape((2, beams, piece_width), f32)
+    outer, outer_phase, own = pl.pallas_call(
         functools.partial(outer_tables_kernel, (rx_count, width, pulse_count)),
         out_shape=[
             shape((outer_count, beams, beams), bf16),
             shape((outer_count, 2, beams, piece_width), f32),
+            picture_shape,
         ],
-        in_specs=[vmem(), vmem(), anywhere()],
-        out_specs=[vmem()] * 2,
+        in_specs=[vmem()] * 3,
+        out_specs=[vmem()] * 3,
         name="outer_tables",
         **PARAMS,
     )(angles, codes, images[0])
+    far = pl.pallas_call(
+        functools.partial(far_kernel, (3, 2)),
+        out_shape=picture_shape,
+        in_specs=[vmem()] * 4,
+        out_specs=vmem(),
+        name="far",
+        **PARAMS,
+    )(images[3], images[2], outer, outer_phase)
     return pl.pallas_call(
-        outer_kernel,
-        out_shape=shape((2, beams, piece_width), f32),
-        in_specs=[vmem()] * (2 + pulse_count),
+        near_kernel,
+        out_shape=picture_shape,
+        in_specs=[vmem()] * 5,
         out_specs=vmem(),
-        name="outer",
+        name="near",
         **PARAMS,
-    )(outer, outer_phase, *images[::-1])
+    )(far, images[1], own, outer, outer_phase)
 
 
 def power_of_two(count):
@@ -825,8 +831,7 @@
         and rx_count == 2
         and channels == 8
         and pulses == 8
-        and power_of_two(pulse_count)
-        and pulse_count > 1
+        and pulse_count == 4
         and power_of_two(beam_angle.shape[0])
         and beam_angle.shape[0] % 16 == 0
         and piece_width % LANES == 0

time: 21.4 us -> 21.3 us (level)
  waiting for transfers between devices: 4.84 us -> 4.44 us
  Pallas kernels: 7.92 us -> 8.2 us
    ppermute x3, waiting for transfers between devices: 3.61 us -> 3.22 us  [fast(): images[distance] = lax.ppermute(images[distance], 'pulse', pairs)]
    pallas_call x4 -> x5, Pallas kernels: 3.44 us -> 3.69 us  [the longest x2 1.64 us: merge(): pl.pallas_call(functools.partial(inner_kernel, [last - distance for dista...]
  transfers between devices with their start and end apart: 6 -> 6, of which waited for: 5 -> 5; matrix products, arithmetic and copies ran while one was open for 0% -> 0% of each run, Pallas kernels for 29% -> 31%
where the time goes in v6:
time: 21.3 us; the launch traced here: 21.2 us
  Pallas kernels  8.2 us (38%)
  starting transfers between devices  8.09 us (38%)
  waiting for transfers between devices  4.44 us (21%)
  local copies, waits for them, and re-layouts  0.41 us (2%)
    ppermute x3, starting transfers between devices, fast(): images[distance] = lax.ppermute(images[distance], 'pulse', pairs)  4.61 us
    ppermute x3, starting transfers between devices, swapped(): lax.ppermute(x, axis, [(i, i ^ 1 << distance) for i in range(lax.axis_siz...  3.48 us
    ppermute x3, waiting for transfers between devices, fast(): images[distance] = lax.ppermute(images[distance], 'pulse', pairs)  3.22 us
    pallas_call x2, Pallas kernels, merge(): pl.pallas_call(functools.partial(inner_kernel, [last - distance for dista...  1.64 us
    ppermute x3, waiting for transfers between devices, swapped(): lax.ppermute(x, axis, [(i, i ^ 1 << distance) for i in range(lax.axis_siz...  1.23 us
    pallas_call x1, Pallas kernels, fast(): pl.pallas_call(functools.partial(phases_kernel, (pulses, rx_count, width)...  1.19 us
    pallas_call x1, Pallas kernels, fast(): pl.pallas_call(near_kernel, out_shape=picture_shape, in_specs=[vmem()] *...  0.95 us
    pallas_call x1, Pallas kernels, fast(): pl.pallas_call(interior_kernel, out_shape=filtered_shape, in_specs=[vmem(...  0.89 us
  transfers between devices with their start and end apart: 6, of which 5 were waited for; matrix products, arithmetic and copies ran while one was open for 0% of the time, Pallas kernels for 31%

profile of v6, /device:TPU:0, one launch (start us, length us, event | category | flops | bytes accessed | tf_op | source)
XLA Modules:
  0.0 21.2 jit_solution(6842001023950542183)
XLA Ops:
  0.0 0.0 copy-start.1
  0.0 0.0 copy-start
  0.0 0.5 %collective-permute-start = (bf16[2,8,8,2048]{3,2,1,0:T(8,128)(2,1)}, bf16[2,8,8,2048]{3,2,1,0:T(8,128)(2,1)S(1)}, u32[]{:S(2)}, u32[]{:S(2)}) collective-permute-start(bf16[2,8,8,2048]{3,2,1,0:T(8,128)(2,1)} %echo_ref.3), channel_id=1, source_target_pairs={{0,1},{1,0},{2,3},{3,2},{4,5},{5,4},{6,7},{7,6},{8,9},{9,8},{10,11... | collective-permute-start | bytes 1572872 | tf_op jit(solution)/shard_map/ppermute | solution.py:35
  0.5 0.2 %bands.1.bands_ref = bf16[8,192,256]{2,1,0:T(8,128)(2,1)S(1)} custom-call(), custom_call_target="tpu_custom_call" | custom-call | flops 11000000512 | bytes 36000000 | tf_op jit(solution)/shard_map/bands/pallas_call | solution.py:693
  0.7 0.4 %copy-done = bf16[2,8,8,2048]{3,2,1,0:T(8,128)(2,1)S(1)} copy-done((bf16[2,8,8,2048]{3,2,1,0:T(8,128)(2,1)S(1)}, bf16[2,8,8,2048]{3,2,1,0:T(8,128)(2,1)}, u32[]{:S(2)}) %copy-start) | copy-done | bytes 524312
  1.1 0.0 copy-start.3
  1.1 0.9 %interior.1.inner_ref = bf16[128,2688]{1,0:T(8,128)(2,1)S(1)} custom-call(bf16[2,8,8,2048]{3,2,1,0:T(8,128)(2,1)S(1)} %copy-done, bf16[8,192,256]{2,1,0:T(8,128)(2,1)S(1)} %bands.1.bands_ref), custom_call_target="tpu_custom_call" | custom-call | tf_op jit(solution)/shard_map/interior/pallas_call | solution.py:703
  2.0 0.2 %collective-permute-done.across_ref = bf16[2,8,8,2048]{3,2,1,0:T(8,128)(2,1)S(1)} collective-permute-done((bf16[2,8,8,2048]{3,2,1,0:T(8,128)(2,1)}, bf16[2,8,8,2048]{3,2,1,0:T(8,128)(2,1)S(1)}, u32[]{:S(2)}, u32[]{:S(2)}) %collective-permute-start) | collective-permute-done | bytes 524320 | tf_op jit(solution)/shard_map/ppermute | solution.py:35
  2.2 0.0 copy-done.1
  2.2 0.7 %edges.1 = (bf16[128,2688]{1,0:T(8,128)(2,1)S(1)}, bf16[2,8,16,256]{3,2,1,0:T(8,128)(2,1)S(1)}) custom-call(bf16[128,2688]{1,0:T(8,128)(2,1)S(1)} %interior.1.inner_ref, bf16[2,8,8,2048]{3,2,1,0:T(8,128)(2,1)S(1)} %copy-done, bf16[2,8,8,2048]{3,2,1,0:T(8,128)(2,1)S(1)} %collective-permute-done.across_ref, ...), custom_call_target="tpu_custom_call", output_to_operand_aliasing={{0}: (0, {})} | custom-call | tf_op jit(solution)/shard_map/edges/pallas_call | solution.py:721
  2.9 2.9 %collective-permute-start.1 = (bf16[2,8,16,256]{3,2,1,0:T(8,128)(2,1)S(1)}, bf16[2,8,16,256]{3,2,1,0:T(8,128)(2,1)S(1)}, u32[]{:S(2)}, u32[]{:S(2)}) collective-permute-start(bf16[2,8,16,256]{3,2,1,0:T(8,128)(2,1)S(1)} %get-tuple-element.19.after_ref), channel_id=1, source_target_pairs={{0,2},{2,0},{1,3},{3,1},{4,6},{6,4},{5,7},{7,5},{8,10},{10,8},{9,1... | collective-permute-start | bytes 393224 | tf_op jit(solution)/shard_map/ppermute | solution.py:35
  5.8 0.0 copy-done.3
  5.8 0.0 copy-start.2
  5.8 1.2 %phases.1.after_ref.phase_ref = f32[4,8,2,64,256]{4,3,2,1,0:T(8,128)S(1)} custom-call(s32[1,64]{1,0:T(1,128)S(1)} %bitcast.4, bf16[2,8,16,256]{3,2,1,0:T(8,128)(2,1)S(1)} %get-tuple-element.19.after_ref), custom_call_target="tpu_custom_call" | custom-call | tf_op jit(solution)/shard_map/phases/pallas_call | solution.py:734
  7.0 0.8 %rest.1 = (bf16[4,8,16,256]{3,2,1,0:T(8,128)(2,1)S(1)}, bf16[2,8,16,256]{3,2,1,0:T(8,128)(2,1)S(1)}) custom-call(bf16[128,2688]{1,0:T(8,128)(2,1)S(1)} %get-tuple-element.18.filtered_ref, bf16[768,256]{1,0:T(8,128)(2,1)S(1)} %copy-done.1, f32[4,8,2,64,256]{4,3,2,1,0:T(8,128)S(1)} %phases.1.after_ref.phase_ref), custom_call_target="tpu_custom_call" | custom-call | tf_op jit(solution)/shard_map/rest/pallas_call | solution.py:742
  7.8 0.1 collective-permute-start.4
  7.9 0.0 copy-done.2
  7.9 0.7 %weights.1 = (bf16[8,128,64]{2,1,0:T(8,128)(2,1)S(1)}, bf16[6,64,64]{2,1,0:T(8,128)(2,1)S(1)}) custom-call(s32[1,64]{1,0:T(1,128)S(1)} %bitcast.5, s32[64,64]{1,0:T(8,128)S(1)} %bitcast.2, bf16[4,8,16,256]{3,2,1,0:T(8,128)(2,1)S(1)} %get-tuple-element.20.after_ref.keep_ref), custom_call_target="tpu_custom_call" | custom-call | tf_op jit(solution)/shard_map/weights/pallas_call | solution.py:750
  8.6 1.0 %collective-permute-done.1.other_ref = bf16[2,8,16,256]{3,2,1,0:T(8,128)(2,1)S(1)} collective-permute-done((bf16[2,8,16,256]{3,2,1,0:T(8,128)(2,1)S(1)}, bf16[2,8,16,256]{3,2,1,0:T(8,128)(2,1)S(1)}, u32[]{:S(2)}, u32[]{:S(2)}) %collective-permute-start.1) | collective-permute-done | bytes 131104 | tf_op jit(solution)/shard_map/ppermute | solution.py:35
  9.6 0.8 %inner.2 = (bf16[2,64,256]{2,1,0:T(8,128)(2,1)S(1)}, bf16[2,64,256]{2,1,0:T(8,128)(2,1)S(1)}) custom-call(bf16[4,8,16,256]{3,2,1,0:T(8,128)(2,1)S(1)} %get-tuple-element.20.after_ref.keep_ref, bf16[2,8,16,256]{3,2,1,0:T(8,128)(2,1)S(1)} %collective-permute-done.1.other_ref, bf16[8,128,64]{2,1,0:T(8,128)(2,1)S(1)} %get-tuple-element.21.first_ref, ...), custom_call_target="tpu_custom_call" | custom-call | flops 3300000000 | bytes 10800000 | tf_op jit(solution)/shard_map/inner/pallas_call | solution.py:766
  10.5 3.9 %collective-permute-start.2 = (bf16[2,64,256]{2,1,0:T(8,128)(2,1)S(1)}, bf16[2,64,256]{2,1,0:T(8,128)(2,1)S(1)}, u32[]{:S(2)}, u32[]{:S(2)}) collective-permute-start(bf16[2,64,256]{2,1,0:T(8,128)(2,1)S(1)} %get-tuple-element.23), channel_id=1, source_target_pairs={{0,12},{4,8},{8,4},{12,0},{1,13},{5,9},{9,5},{13,1},{2,14},{6,10},... | collective-permute-start | bytes 196616 | tf_op jit(solution)/shard_map/ppermute | solution.py:787
  14.4 0.0 collective-permute-start.3
  14.4 0.0 collective-permute-done.4.other_ref
  14.4 0.8 %inner.3 = (bf16[2,64,256]{2,1,0:T(8,128)(2,1)S(1)}, bf16[2,64,256]{2,1,0:T(8,128)(2,1)S(1)}) custom-call(bf16[4,8,16,256]{3,2,1,0:T(8,128)(2,1)S(1)} %get-tuple-element.20.after_ref.keep_ref, bf16[2,8,16,256]{3,2,1,0:T(8,128)(2,1)S(1)} %collective-permute-done.4.other_ref, bf16[8,128,64]{2,1,0:T(8,128)(2,1)S(1)} %get-tuple-element.21.first_ref, ...), custom_call_target="tpu_custom_call" | custom-call | flops 3300000000 | bytes 10800000 | tf_op jit(solution)/shard_map/inner/pallas_call | solution.py:766
  15.2 0.7 %collective-permute-start.5 = (bf16[2,64,256]{2,1,0:T(8,128)(2,1)S(1)}, bf16[2,64,256]{2,1,0:T(8,128)(2,1)S(1)}, u32[]{:S(2)}, u32[]{:S(2)}) collective-permute-start(bf16[2,64,256]{2,1,0:T(8,128)(2,1)S(1)} %get-tuple-element.29), channel_id=1, source_target_pairs={{0,4},{4,0},{8,12},{12,8},{1,5},{5,1},{9,13},{13,9},{2,6},{6,2},{1... | collective-permute-start | bytes 196616 | tf_op jit(solution)/shard_map/ppermute | solution.py:787
  15.9 0.8 %outer_tables.1 = (bf16[6,64,64]{2,1,0:T(8,128)(2,1)S(1)}, f32[6,2,64,256]{3,2,1,0:T(8,128)S(1)}, f32[2,64,256]{2,1,0:T(8,128)S(1)}) custom-call(s32[1,64]{1,0:T(1,128)S(1)} %bitcast.6, s32[64,64]{1,0:T(8,128)S(1)} %bitcast.3, bf16[2,64,256]{2,1,0:T(8,128)(2,1)S(1)} %get-tuple-element.26.image_ref), custom_call_target="tpu_custom_call" | custom-call | tf_op jit(solution)/shard_map/outer_tables/pallas_call | solution.py:790
  16.7 0.8 %collective-permute-done.2.rest_0_ = bf16[2,64,256]{2,1,0:T(8,128)(2,1)S(1)} collective-permute-done((bf16[2,64,256]{2,1,0:T(8,128)(2,1)S(1)}, bf16[2,64,256]{2,1,0:T(8,128)(2,1)S(1)}, u32[]{:S(2)}, u32[]{:S(2)}) %collective-permute-start.2) | collective-permute-done | bytes 65568 | tf_op jit(solution)/shard_map/ppermute | solution.py:787
  17.5 2.1 %collective-permute-done.3.rest_1_ = bf16[2,64,256]{2,1,0:T(8,128)(2,1)S(1)} collective-permute-done((bf16[2,64,256]{2,1,0:T(8,128)(2,1)S(1)}, bf16[2,64,256]{2,1,0:T(8,128)(2,1)S(1)}, u32[]{:S(2)}, u32[]{:S(2)}) %collective-permute-start.3) | collective-permute-done | bytes 65568 | tf_op jit(solution)/shard_map/ppermute | solution.py:787
  19.6 0.3 %far.1.far_ref = f32[2,64,256]{2,1,0:T(8,128)S(1)} custom-call(bf16[2,64,256]{2,1,0:T(8,128)(2,1)S(1)} %collective-permute-done.2.rest_0_, bf16[2,64,256]{2,1,0:T(8,128)(2,1)S(1)} %collective-permute-done.3.rest_1_, bf16[6,64,64]{2,1,0:T(8,128)(2,1)S(1)} %get-tuple-element.27.rest_2_.outer_ref, f32[6,2,64,256]{3,2,1,0:T(8,128)S(1)} %get-tuple-element.28.rest_3_.phase_ref), custom_call_target="tpu_custom_call" | custom-call | tf_op jit(solution)/shard_map/far/pallas_call | solution.py:802
  19.9 0.3 %collective-permute-done.5.image_ref = bf16[2,64,256]{2,1,0:T(8,128)(2,1)S(1)} collective-permute-done((bf16[2,64,256]{2,1,0:T(8,128)(2,1)S(1)}, bf16[2,64,256]{2,1,0:T(8,128)(2,1)S(1)}, u32[]{:S(2)}, u32[]{:S(2)}) %collective-permute-start.5) | collective-permute-done | bytes 65568 | tf_op jit(solution)/shard_map/ppermute | solution.py:787
  20.3 0.9 %near.1 = f32[2,64,256]{2,1,0:T(8,128)} custom-call(f32[2,64,256]{2,1,0:T(8,128)S(1)} %far.1.far_ref, bf16[2,64,256]{2,1,0:T(8,128)(2,1)S(1)} %collective-permute-done.5.image_ref, f32[2,64,256]{2,1,0:T(8,128)S(1)} %get-tuple-element.30.own_ref, bf16[6,64,64]{2,1,0:T(8,128)(2,1)S(1)} %get-tuple-element.27.rest_2_.outer_ref, ...), custom_call_target="tpu_custom_call" | custom-call | tf_op jit(solution)/shard_map/near/pallas_call | solution.py:810
Async XLA Ops:
  0.0 2.2 %copy-start.1 = (bf16[768,256]{1,0:T(8,128)(2,1)S(1)}, bf16[768,256]{1,0:T(8,128)(2,1)}, u32[]{:S(2)}) copy-start(bf16[768,256]{1,0:T(8,128)(2,1)} %constant.2.clone.chirp_ref) | copy-start | bytes 1179652
  0.0 1.1 %copy-start = (bf16[2,8,8,2048]{3,2,1,0:T(8,128)(2,1)S(1)}, bf16[2,8,8,2048]{3,2,1,0:T(8,128)(2,1)}, u32[]{:S(2)}) copy-start(bf16[2,8,8,2048]{3,2,1,0:T(8,128)(2,1)} %echo_ref.3) | copy-start | bytes 1572868
  0.0 2.2 %collective-permute-start = (bf16[2,8,8,2048]{3,2,1,0:T(8,128)(2,1)}, bf16[2,8,8,2048]{3,2,1,0:T(8,128)(2,1)S(1)}, u32[]{:S(2)}, u32[]{:S(2)}) collective-permute-start(bf16[2,8,8,2048]{3,2,1,0:T(8,128)(2,1)} %echo_ref.3), channel_id=1, source_target_pairs={{0,1},{1,0},{2,3},{3,2},{4,5},{5,4},{6,7},{7,6},{8,9},{9,8},{10,11... | collective-permute-start | bytes 1572872 | tf_op jit(solution)/shard_map/ppermute | solution.py:35
  1.1 4.7 %copy-start.3 = (s32[64]{0:T(128)S(1)}, s32[64]{0:T(128)}, u32[]{:S(2)}) copy-start(s32[64]{0:T(128)} %param.5) | copy-start | bytes 772
  2.9 6.7 %collective-permute-start.1 = (bf16[2,8,16,256]{3,2,1,0:T(8,128)(2,1)S(1)}, bf16[2,8,16,256]{3,2,1,0:T(8,128)(2,1)S(1)}, u32[]{:S(2)}, u32[]{:S(2)}) collective-permute-start(bf16[2,8,16,256]{3,2,1,0:T(8,128)(2,1)S(1)} %get-tuple-element.19.after_ref), channel_id=1, source_target_pairs={{0,2},{2,0},{1,3},{3,1},{4,6},{6,4},{5,7},{7,5},{8,10},{10,8},{9,1... | collective-permute-start | bytes 393224 | tf_op jit(solution)/shard_map/ppermute | solution.py:35
  5.8 2.1 %copy-start.2 = (s32[32,2,64]{2,1,0:T(2,128)S(1)}, s32[32,2,64]{2,1,0:T(2,128)}, u32[]{:S(2)}) copy-start(s32[32,2,64]{2,1,0:T(2,128)} %param.6) | copy-start | bytes 49156
  7.8 6.6 %collective-permute-start.4 = (bf16[2,8,16,256]{3,2,1,0:T(8,128)(2,1)S(1)}, bf16[2,8,16,256]{3,2,1,0:T(8,128)(2,1)S(1)}, u32[]{:S(2)}, u32[]{:S(2)}) collective-permute-start(bf16[2,8,16,256]{3,2,1,0:T(8,128)(2,1)S(1)} %get-tuple-element.25), channel_id=1, source_target_pairs={{0,2},{2,0},{1,3},{3,1},{4,6},{6,4},{5,7},{7,5},{8,10},{10,8},{9,1... | collective-permute-start | bytes 393224 | tf_op jit(solution)/shard_map/ppermute | solution.py:35
  10.5 7.0 %collective-permute-start.2 = (bf16[2,64,256]{2,1,0:T(8,128)(2,1)S(1)}, bf16[2,64,256]{2,1,0:T(8,128)(2,1)S(1)}, u32[]{:S(2)}, u32[]{:S(2)}) collective-permute-start(bf16[2,64,256]{2,1,0:T(8,128)(2,1)S(1)} %get-tuple-element.23), channel_id=1, source_target_pairs={{0,12},{4,8},{8,4},{12,0},{1,13},{5,9},{9,5},{13,1},{2,14},{6,10},... | collective-permute-start | bytes 196616 | tf_op jit(solution)/shard_map/ppermute | solution.py:787
  14.4 5.3 %collective-permute-start.3 = (bf16[2,64,256]{2,1,0:T(8,128)(2,1)S(1)}, bf16[2,64,256]{2,1,0:T(8,128)(2,1)S(1)}, u32[]{:S(2)}, u32[]{:S(2)}) collective-permute-start(bf16[2,64,256]{2,1,0:T(8,128)(2,1)S(1)} %get-tuple-element.24), channel_id=1, source_target_pairs={{0,8},{4,12},{8,0},{12,4},{1,9},{5,13},{9,1},{13,5},{2,10},{6,14},... | collective-permute-start | bytes 196616 | tf_op jit(solution)/shard_map/ppermute | solution.py:787
  15.2 5.0 %collective-permute-start.5 = (bf16[2,64,256]{2,1,0:T(8,128)(2,1)S(1)}, bf16[2,64,256]{2,1,0:T(8,128)(2,1)S(1)}, u32[]{:S(2)}, u32[]{:S(2)}) collective-permute-start(bf16[2,64,256]{2,1,0:T(8,128)(2,1)S(1)} %get-tuple-element.29), channel_id=1, source_target_pairs={{0,4},{4,0},{8,12},{12,8},{1,5},{5,1},{9,13},{13,9},{2,6},{6,2},{1... | collective-permute-start | bytes 196616 | tf_op jit(solution)/shard_map/ppermute | solution.py:787

commit v7 on v6

--- a/solution.py
+++ b/solution.py
@@ -800,13 +800,13 @@
         **PARAMS,
     )(angles, codes, images[0])
     far = pl.pallas_call(
-        functools.partial(far_kernel, (3, 2)),
+        functools.partial(far_kernel, (2, 3)),
         out_shape=picture_shape,
         in_specs=[vmem()] * 4,
         out_specs=vmem(),
         name="far",
         **PARAMS,
-    )(images[3], images[2], outer, outer_phase)
+    )(images[2], images[3], outer, outer_phase)
     return pl.pallas_call(
         near_kernel,
         out_shape=picture_shape,

time: 21.3 us -> 21.3 us (level)
  transfers between devices with their start and end apart: 6 -> 6, of which waited for: 5 -> 4; matrix products, arithmetic and copies ran while one was open for 0% -> 0% of each run, Pallas kernels for 31% -> 31%
where the time goes in v7:
time: 21.3 us; the launch traced here: 21.2 us
  Pallas kernels  8.19 us (38%)
  starting transfers between devices  8.02 us (38%)
  waiting for transfers between devices  4.46 us (21%)
  local copies, waits for them, and re-layouts  0.41 us (2%)
    ppermute x3, starting transfers between devices, fast(): images[distance] = lax.ppermute(images[distance], 'pulse', pairs)  4.54 us
    ppermute x3, starting transfers between devices, swapped(): lax.ppermute(x, axis, [(i, i ^ 1 << distance) for i in range(lax.axis_siz...  3.48 us
    ppermute x3, waiting for transfers between devices, fast(): images[distance] = lax.ppermute(images[distance], 'pulse', pairs)  3.23 us
    pallas_call x2, Pallas kernels, merge(): pl.pallas_call(functools.partial(inner_kernel, [last - distance for dista...  1.64 us
    ppermute x3, waiting for transfers between devices, swapped(): lax.ppermute(x, axis, [(i, i ^ 1 << distance) for i in range(lax.axis_siz...  1.23 us
    pallas_call x1, Pallas kernels, fast(): pl.pallas_call(functools.partial(phases_kernel, (pulses, rx_count, width)...  1.19 us
    pallas_call x1, Pallas kernels, fast(): pl.pallas_call(near_kernel, out_shape=picture_shape, in_specs=[vmem()] *...  0.95 us
    pallas_call x1, Pallas kernels, fast(): pl.pallas_call(interior_kernel, out_shape=filtered_shape, in_specs=[vmem(...  0.89 us
  transfers between devices with their start and end apart: 6, of which 4 were waited for; matrix products, arithmetic and copies ran while one was open for 0% of the time, Pallas kernels for 31%

profile of v7, /device:TPU:0, one launch (start us, length us, event | category | flops | bytes accessed | tf_op | source)
XLA Modules:
  0.0 21.2 jit_solution(18177951535457150807)
XLA Ops:
  0.0 0.0 copy-start.1
  0.0 0.0 copy-start
  0.0 0.5 %collective-permute-start = (bf16[2,8,8,2048]{3,2,1,0:T(8,128)(2,1)}, bf16[2,8,8,2048]{3,2,1,0:T(8,128)(2,1)S(1)}, u32[]{:S(2)}, u32[]{:S(2)}) collective-permute-start(bf16[2,8,8,2048]{3,2,1,0:T(8,128)(2,1)} %echo_ref.3), channel_id=1, source_target_pairs={{0,1},{1,0},{2,3},{3,2},{4,5},{5,4},{6,7},{7,6},{8,9},{9,8},{10,11... | collective-permute-start | bytes 1572872 | tf_op jit(solution)/shard_map/ppermute | solution.py:35
  0.5 0.2 %bands.1.bands_ref = bf16[8,192,256]{2,1,0:T(8,128)(2,1)S(1)} custom-call(), custom_call_target="tpu_custom_call" | custom-call | flops 11000000512 | bytes 36000000 | tf_op jit(solution)/shard_map/bands/pallas_call | solution.py:693
  0.7 0.4 %copy-done = bf16[2,8,8,2048]{3,2,1,0:T(8,128)(2,1)S(1)} copy-done((bf16[2,8,8,2048]{3,2,1,0:T(8,128)(2,1)S(1)}, bf16[2,8,8,2048]{3,2,1,0:T(8,128)(2,1)}, u32[]{:S(2)}) %copy-start) | copy-done | bytes 524312
  1.1 0.0 copy-start.3
  1.1 0.9 %interior.1.inner_ref = bf16[128,2688]{1,0:T(8,128)(2,1)S(1)} custom-call(bf16[2,8,8,2048]{3,2,1,0:T(8,128)(2,1)S(1)} %copy-done, bf16[8,192,256]{2,1,0:T(8,128)(2,1)S(1)} %bands.1.bands_ref), custom_call_target="tpu_custom_call" | custom-call | tf_op jit(solution)/shard_map/interior/pallas_call | solution.py:703
  2.0 0.2 %collective-permute-done.across_ref = bf16[2,8,8,2048]{3,2,1,0:T(8,128)(2,1)S(1)} collective-permute-done((bf16[2,8,8,2048]{3,2,1,0:T(8,128)(2,1)}, bf16[2,8,8,2048]{3,2,1,0:T(8,128)(2,1)S(1)}, u32[]{:S(2)}, u32[]{:S(2)}) %collective-permute-start) | collective-permute-done | bytes 524320 | tf_op jit(solution)/shard_map/ppermute | solution.py:35
  2.2 0.0 copy-done.1
  2.2 0.7 %edges.1 = (bf16[128,2688]{1,0:T(8,128)(2,1)S(1)}, bf16[2,8,16,256]{3,2,1,0:T(8,128)(2,1)S(1)}) custom-call(bf16[128,2688]{1,0:T(8,128)(2,1)S(1)} %interior.1.inner_ref, bf16[2,8,8,2048]{3,2,1,0:T(8,128)(2,1)S(1)} %copy-done, bf16[2,8,8,2048]{3,2,1,0:T(8,128)(2,1)S(1)} %collective-permute-done.across_ref, ...), custom_call_target="tpu_custom_call", output_to_operand_aliasing={{0}: (0, {})} | custom-call | tf_op jit(solution)/shard_map/edges/pallas_call | solution.py:721
  2.9 2.9 %collective-permute-start.1 = (bf16[2,8,16,256]{3,2,1,0:T(8,128)(2,1)S(1)}, bf16[2,8,16,256]{3,2,1,0:T(8,128)(2,1)S(1)}, u32[]{:S(2)}, u32[]{:S(2)}) collective-permute-start(bf16[2,8,16,256]{3,2,1,0:T(8,128)(2,1)S(1)} %get-tuple-element.19.after_ref), channel_id=1, source_target_pairs={{0,2},{2,0},{1,3},{3,1},{4,6},{6,4},{5,7},{7,5},{8,10},{10,8},{9,1... | collective-permute-start | bytes 393224 | tf_op jit(solution)/shard_map/ppermute | solution.py:35
  5.8 0.0 copy-done.3
  5.8 0.0 copy-start.2
  5.8 1.2 %phases.1.after_ref.phase_ref = f32[4,8,2,64,256]{4,3,2,1,0:T(8,128)S(1)} custom-call(s32[1,64]{1,0:T(1,128)S(1)} %bitcast.4, bf16[2,8,16,256]{3,2,1,0:T(8,128)(2,1)S(1)} %get-tuple-element.19.after_ref), custom_call_target="tpu_custom_call" | custom-call | tf_op jit(solution)/shard_map/phases/pallas_call | solution.py:734
  7.0 0.8 %rest.1 = (bf16[4,8,16,256]{3,2,1,0:T(8,128)(2,1)S(1)}, bf16[2,8,16,256]{3,2,1,0:T(8,128)(2,1)S(1)}) custom-call(bf16[128,2688]{1,0:T(8,128)(2,1)S(1)} %get-tuple-element.18.filtered_ref, bf16[768,256]{1,0:T(8,128)(2,1)S(1)} %copy-done.1, f32[4,8,2,64,256]{4,3,2,1,0:T(8,128)S(1)} %phases.1.after_ref.phase_ref), custom_call_target="tpu_custom_call" | custom-call | tf_op jit(solution)/shard_map/rest/pallas_call | solution.py:742
  7.8 0.1 collective-permute-start.4
  7.9 0.0 copy-done.2
  7.9 0.7 %weights.1 = (bf16[8,128,64]{2,1,0:T(8,128)(2,1)S(1)}, bf16[6,64,64]{2,1,0:T(8,128)(2,1)S(1)}) custom-call(s32[1,64]{1,0:T(1,128)S(1)} %bitcast.5, s32[64,64]{1,0:T(8,128)S(1)} %bitcast.2, bf16[4,8,16,256]{3,2,1,0:T(8,128)(2,1)S(1)} %get-tuple-element.20.after_ref.keep_ref), custom_call_target="tpu_custom_call" | custom-call | tf_op jit(solution)/shard_map/weights/pallas_call | solution.py:750
  8.6 1.0 %collective-permute-done.1.other_ref = bf16[2,8,16,256]{3,2,1,0:T(8,128)(2,1)S(1)} collective-permute-done((bf16[2,8,16,256]{3,2,1,0:T(8,128)(2,1)S(1)}, bf16[2,8,16,256]{3,2,1,0:T(8,128)(2,1)S(1)}, u32[]{:S(2)}, u32[]{:S(2)}) %collective-permute-start.1) | collective-permute-done | bytes 131104 | tf_op jit(solution)/shard_map/ppermute | solution.py:35
  9.6 0.8 %inner.2 = (bf16[2,64,256]{2,1,0:T(8,128)(2,1)S(1)}, bf16[2,64,256]{2,1,0:T(8,128)(2,1)S(1)}) custom-call(bf16[4,8,16,256]{3,2,1,0:T(8,128)(2,1)S(1)} %get-tuple-element.20.after_ref.keep_ref, bf16[2,8,16,256]{3,2,1,0:T(8,128)(2,1)S(1)} %collective-permute-done.1.other_ref, bf16[8,128,64]{2,1,0:T(8,128)(2,1)S(1)} %get-tuple-element.21.first_ref, ...), custom_call_target="tpu_custom_call" | custom-call | flops 3300000000 | bytes 10800000 | tf_op jit(solution)/shard_map/inner/pallas_call | solution.py:766
  10.5 2.9 %collective-permute-start.2 = (bf16[2,64,256]{2,1,0:T(8,128)(2,1)S(1)}, bf16[2,64,256]{2,1,0:T(8,128)(2,1)S(1)}, u32[]{:S(2)}, u32[]{:S(2)}) collective-permute-start(bf16[2,64,256]{2,1,0:T(8,128)(2,1)S(1)} %get-tuple-element.23), channel_id=1, source_target_pairs={{0,8},{4,12},{8,0},{12,4},{1,9},{5,13},{9,1},{13,5},{2,10},{6,14},... | collective-permute-start | bytes 196616 | tf_op jit(solution)/shard_map/ppermute | solution.py:787
  13.4 1.3 %collective-permute-start.3 = (bf16[2,64,256]{2,1,0:T(8,128)(2,1)S(1)}, bf16[2,64,256]{2,1,0:T(8,128)(2,1)S(1)}, u32[]{:S(2)}, u32[]{:S(2)}) collective-permute-start(bf16[2,64,256]{2,1,0:T(8,128)(2,1)S(1)} %get-tuple-element.24), channel_id=1, source_target_pairs={{0,12},{4,8},{8,4},{12,0},{1,13},{5,9},{9,5},{13,1},{2,14},{6,10},... | collective-permute-start | bytes 196616 | tf_op jit(solution)/shard_map/ppermute | solution.py:787
  14.7 0.0 collective-permute-done.4.other_ref
  14.7 0.8 %inner.3 = (bf16[2,64,256]{2,1,0:T(8,128)(2,1)S(1)}, bf16[2,64,256]{2,1,0:T(8,128)(2,1)S(1)}) custom-call(bf16[4,8,16,256]{3,2,1,0:T(8,128)(2,1)S(1)} %get-tuple-element.20.after_ref.keep_ref, bf16[2,8,16,256]{3,2,1,0:T(8,128)(2,1)S(1)} %collective-permute-done.4.other_ref, bf16[8,128,64]{2,1,0:T(8,128)(2,1)S(1)} %get-tuple-element.21.first_ref, ...), custom_call_target="tpu_custom_call" | custom-call | flops 3300000000 | bytes 10800000 | tf_op jit(solution)/shard_map/inner/pallas_call | solution.py:766
  15.5 0.3 %collective-permute-start.5 = (bf16[2,64,256]{2,1,0:T(8,128)(2,1)S(1)}, bf16[2,64,256]{2,1,0:T(8,128)(2,1)S(1)}, u32[]{:S(2)}, u32[]{:S(2)}) collective-permute-start(bf16[2,64,256]{2,1,0:T(8,128)(2,1)S(1)} %get-tuple-element.29), channel_id=1, source_target_pairs={{0,4},{4,0},{8,12},{12,8},{1,5},{5,1},{9,13},{13,9},{2,6},{6,2},{1... | collective-permute-start | bytes 196616 | tf_op jit(solution)/shard_map/ppermute | solution.py:787
  15.8 0.8 %outer_tables.1 = (bf16[6,64,64]{2,1,0:T(8,128)(2,1)S(1)}, f32[6,2,64,256]{3,2,1,0:T(8,128)S(1)}, f32[2,64,256]{2,1,0:T(8,128)S(1)}) custom-call(s32[1,64]{1,0:T(1,128)S(1)} %bitcast.6, s32[64,64]{1,0:T(8,128)S(1)} %bitcast.3, bf16[2,64,256]{2,1,0:T(8,128)(2,1)S(1)} %get-tuple-element.26.image_ref), custom_call_target="tpu_custom_call" | custom-call | tf_op jit(solution)/shard_map/outer_tables/pallas_call | solution.py:790
  16.7 0.0 collective-permute-done.2.rest_0_
  16.7 2.9 %collective-permute-done.3.rest_1_ = bf16[2,64,256]{2,1,0:T(8,128)(2,1)S(1)} collective-permute-done((bf16[2,64,256]{2,1,0:T(8,128)(2,1)S(1)}, bf16[2,64,256]{2,1,0:T(8,128)(2,1)S(1)}, u32[]{:S(2)}, u32[]{:S(2)}) %collective-permute-start.3) | collective-permute-done | bytes 65568 | tf_op jit(solution)/shard_map/ppermute | solution.py:787
  19.5 0.3 %far.1.far_ref = f32[2,64,256]{2,1,0:T(8,128)S(1)} custom-call(bf16[2,64,256]{2,1,0:T(8,128)(2,1)S(1)} %collective-permute-done.2.rest_0_, bf16[2,64,256]{2,1,0:T(8,128)(2,1)S(1)} %collective-permute-done.3.rest_1_, bf16[6,64,64]{2,1,0:T(8,128)(2,1)S(1)} %get-tuple-element.27.rest_2_.outer_ref, f32[6,2,64,256]{3,2,1,0:T(8,128)S(1)} %get-tuple-element.28.rest_3_.phase_ref), custom_call_target="tpu_custom_call" | custom-call | tf_op jit(solution)/shard_map/far/pallas_call | solution.py:802
  19.8 0.4 %collective-permute-done.5.image_ref = bf16[2,64,256]{2,1,0:T(8,128)(2,1)S(1)} collective-permute-done((bf16[2,64,256]{2,1,0:T(8,128)(2,1)S(1)}, bf16[2,64,256]{2,1,0:T(8,128)(2,1)S(1)}, u32[]{:S(2)}, u32[]{:S(2)}) %collective-permute-start.5) | collective-permute-done | bytes 65568 | tf_op jit(solution)/shard_map/ppermute | solution.py:787
  20.2 1.0 %near.1 = f32[2,64,256]{2,1,0:T(8,128)} custom-call(f32[2,64,256]{2,1,0:T(8,128)S(1)} %far.1.far_ref, bf16[2,64,256]{2,1,0:T(8,128)(2,1)S(1)} %collective-permute-done.5.image_ref, f32[2,64,256]{2,1,0:T(8,128)S(1)} %get-tuple-element.30.own_ref, bf16[6,64,64]{2,1,0:T(8,128)(2,1)S(1)} %get-tuple-element.27.rest_2_.outer_ref, ...), custom_call_target="tpu_custom_call" | custom-call | tf_op jit(solution)/shard_map/near/pallas_call | solution.py:810
Async XLA Ops:
  0.0 2.2 %copy-start.1 = (bf16[768,256]{1,0:T(8,128)(2,1)S(1)}, bf16[768,256]{1,0:T(8,128)(2,1)}, u32[]{:S(2)}) copy-start(bf16[768,256]{1,0:T(8,128)(2,1)} %constant.2.clone.chirp_ref) | copy-start | bytes 1179652
  0.0 1.1 %copy-start = (bf16[2,8,8,2048]{3,2,1,0:T(8,128)(2,1)S(1)}, bf16[2,8,8,2048]{3,2,1,0:T(8,128)(2,1)}, u32[]{:S(2)}) copy-start(bf16[2,8,8,2048]{3,2,1,0:T(8,128)(2,1)} %echo_ref.3) | copy-start | bytes 1572868
  0.0 2.2 %collective-permute-start = (bf16[2,8,8,2048]{3,2,1,0:T(8,128)(2,1)}, bf16[2,8,8,2048]{3,2,1,0:T(8,128)(2,1)S(1)}, u32[]{:S(2)}, u32[]{:S(2)}) collective-permute-start(bf16[2,8,8,2048]{3,2,1,0:T(8,128)(2,1)} %echo_ref.3), channel_id=1, source_target_pairs={{0,1},{1,0},{2,3},{3,2},{4,5},{5,4},{6,7},{7,6},{8,9},{9,8},{10,11... | collective-permute-start | bytes 1572872 | tf_op jit(solution)/shard_map/ppermute | solution.py:35
  1.1 4.7 %copy-start.3 = (s32[64]{0:T(128)S(1)}, s32[64]{0:T(128)}, u32[]{:S(2)}) copy-start(s32[64]{0:T(128)} %param.5) | copy-start | bytes 772
  2.9 6.7 %collective-permute-start.1 = (bf16[2,8,16,256]{3,2,1,0:T(8,128)(2,1)S(1)}, bf16[2,8,16,256]{3,2,1,0:T(8,128)(2,1)S(1)}, u32[]{:S(2)}, u32[]{:S(2)}) collective-permute-start(bf16[2,8,16,256]{3,2,1,0:T(8,128)(2,1)S(1)} %get-tuple-element.19.after_ref), channel_id=1, source_target_pairs={{0,2},{2,0},{1,3},{3,1},{4,6},{6,4},{5,7},{7,5},{8,10},{10,8},{9,1... | collective-permute-start | bytes 393224 | tf_op jit(solution)/shard_map/ppermute | solution.py:35
  5.8 2.1 %copy-start.2 = (s32[32,2,64]{2,1,0:T(2,128)S(1)}, s32[32,2,64]{2,1,0:T(2,128)}, u32[]{:S(2)}) copy-start(s32[32,2,64]{2,1,0:T(2,128)} %param.6) | copy-start | bytes 49156
  7.8 6.9 %collective-permute-start.4 = (bf16[2,8,16,256]{3,2,1,0:T(8,128)(2,1)S(1)}, bf16[2,8,16,256]{3,2,1,0:T(8,128)(2,1)S(1)}, u32[]{:S(2)}, u32[]{:S(2)}) collective-permute-start(bf16[2,8,16,256]{3,2,1,0:T(8,128)(2,1)S(1)} %get-tuple-element.25), channel_id=1, source_target_pairs={{0,2},{2,0},{1,3},{3,1},{4,6},{6,4},{5,7},{7,5},{8,10},{10,8},{9,1... | collective-permute-start | bytes 393224 | tf_op jit(solution)/shard_map/ppermute | solution.py:35
  10.5 6.2 %collective-permute-start.2 = (bf16[2,64,256]{2,1,0:T(8,128)(2,1)S(1)}, bf16[2,64,256]{2,1,0:T(8,128)(2,1)S(1)}, u32[]{:S(2)}, u32[]{:S(2)}) collective-permute-start(bf16[2,64,256]{2,1,0:T(8,128)(2,1)S(1)} %get-tuple-element.23), channel_id=1, source_target_pairs={{0,8},{4,12},{8,0},{12,4},{1,9},{5,13},{9,1},{13,5},{2,10},{6,14},... | collective-permute-start | bytes 196616 | tf_op jit(solution)/shard_map/ppermute | solution.py:787
  13.4 6.2 %collective-permute-start.3 = (bf16[2,64,256]{2,1,0:T(8,128)(2,1)S(1)}, bf16[2,64,256]{2,1,0:T(8,128)(2,1)S(1)}, u32[]{:S(2)}, u32[]{:S(2)}) collective-permute-start(bf16[2,64,256]{2,1,0:T(8,128)(2,1)S(1)} %get-tuple-element.24), channel_id=1, source_target_pairs={{0,12},{4,8},{8,4},{12,0},{1,13},{5,9},{9,5},{13,1},{2,14},{6,10},... | collective-permute-start | bytes 196616 | tf_op jit(solution)/shard_map/ppermute | solution.py:787
  15.5 4.7 %collective-permute-start.5 = (bf16[2,64,256]{2,1,0:T(8,128)(2,1)S(1)}, bf16[2,64,256]{2,1,0:T(8,128)(2,1)S(1)}, u32[]{:S(2)}, u32[]{:S(2)}) collective-permute-start(bf16[2,64,256]{2,1,0:T(8,128)(2,1)S(1)} %get-tuple-element.29), channel_id=1, source_target_pairs={{0,4},{4,0},{8,12},{12,8},{1,5},{5,1},{9,13},{13,9},{2,6},{6,2},{1... | collective-permute-start | bytes 196616 | tf_op jit(solution)/shard_map/ppermute | solution.py:787

commit v8 on v6

--- a/solution.py
+++ b/solution.py
@@ -463,10 +463,9 @@
         rows.extend(base + index for index in range(now))
         now //= 2
     codes = code_columns(codes_ref, rows)
-    column = lax.broadcasted_iota(jnp.int32, (1, 4 * channels * 2), 1)
-    within = jnp.bitwise_and(column, 4 * channels - 1)
+    within = lax.broadcasted_iota(jnp.int32, (1, 4 * channels), 1)
     owner = jnp.bitwise_xor(rx_place, jnp.where(within >= 2 * channels, 1, 0))
-    receiver = owner * channels + jnp.bitwise_and(column, channels - 1)
+    receiver = owner * channels + jnp.bitwise_and(within, channels - 1)
     is_imag = jnp.bitwise_and(within, channels) != 0
     scale = 1.0 / math.sqrt(channels * rx_count)
     steer_re, steer_im = turn_parts(jnp.bitwise_and(angle * receiver, 1023))
@@ -479,8 +478,7 @@
         ],
         axis=1,
     )
-    low_half = column >= 4 * channels
-    entries = 8 * channels
+    entries = 4 * channels
     matrices = [interp_matrix(codes[:, index : index + 1]) for index in range(len(rows))]
     composed = jnp.dot(
         jnp.concatenate(matrices[:pulses], axis=0), steer, preferred_element_type=jnp.float32
@@ -490,10 +488,7 @@
             value = composed[
                 index * beams : (index + 1) * beams, part * entries : (part + 1) * entries
             ]
-            high = value.astype(jnp.bfloat16).astype(jnp.float32)
-            first_ref[index, part * beams : (part + 1) * beams, :] = jnp.where(
-                low_half, value - high, high
-            ).astype(jnp.bfloat16)
+            first_ref[index, part * beams : (part + 1) * beams, :] = value.astype(jnp.bfloat16)
     for index, matrix in enumerate(matrices[pulses:]):
         inner_ref[index] = matrix
 
@@ -595,7 +590,7 @@
             )
             moved_ref[piece, image] = jnp.dot(
                 first_ref[image],
-                jnp.concatenate([rows, rows], axis=0),
+                rows,
                 preferred_element_type=jnp.float32,
             )
 
@@ -750,7 +745,7 @@
     first, inner = pl.pallas_call(
         functools.partial(weights_kernel, (pulses, channels, rx_count, pulse_count)),
         out_shape=[
-            shape((pulses, 2 * beams, 8 * channels), bf16),
+            shape((pulses, 2 * beams, 4 * channels), bf16),
             shape((pulses - 2, beams, beams), bf16),
         ],
         in_specs=[vmem()] * 2 + [anywhere()],

time: 21.3 us -> 21.4 us (level)
  no operation moved by 1% of the time
where the time goes in v8:
time: 21.4 us; the launch traced here: 21.2 us
  Pallas kernels  8.15 us (38%)
  starting transfers between devices  8.1 us (38%)
  waiting for transfers between devices  4.48 us (21%)
  local copies, waits for them, and re-layouts  0.41 us (2%)
    ppermute x3, starting transfers between devices, fast(): images[distance] = lax.ppermute(images[distance], 'pulse', pairs)  4.62 us
    ppermute x3, starting transfers between devices, swapped(): lax.ppermute(x, axis, [(i, i ^ 1 << distance) for i in range(lax.axis_siz...  3.48 us
    ppermute x3, waiting for transfers between devices, fast(): images[distance] = lax.ppermute(images[distance], 'pulse', pairs)  3.23 us
    pallas_call x2, Pallas kernels, merge(): pl.pallas_call(functools.partial(inner_kernel, [last - distance for dista...  1.62 us
    ppermute x3, waiting for transfers between devices, swapped(): lax.ppermute(x, axis, [(i, i ^ 1 << distance) for i in range(lax.axis_siz...  1.25 us
    pallas_call x1, Pallas kernels, fast(): pl.pallas_call(functools.partial(phases_kernel, (pulses, rx_count, width)...  1.19 us
    pallas_call x1, Pallas kernels, fast(): pl.pallas_call(near_kernel, out_shape=picture_shape, in_specs=[vmem()] *...  0.95 us
    pallas_call x1, Pallas kernels, fast(): pl.pallas_call(interior_kernel, out_shape=filtered_shape, in_specs=[vmem(...  0.89 us
  transfers between devices with their start and end apart: 6, of which 5 were waited for; matrix products, arithmetic and copies ran while one was open for 0% of the time, Pallas kernels for 31%

profile of v8, /device:TPU:0, one launch (start us, length us, event | category | flops | bytes accessed | tf_op | source)
XLA Modules:
  0.0 21.2 jit_solution(6694058950530637758)
XLA Ops:
  0.0 0.0 copy-start.1
  0.0 0.0 copy-start
  0.0 0.5 %collective-permute-start = (bf16[2,8,8,2048]{3,2,1,0:T(8,128)(2,1)}, bf16[2,8,8,2048]{3,2,1,0:T(8,128)(2,1)S(1)}, u32[]{:S(2)}, u32[]{:S(2)}) collective-permute-start(bf16[2,8,8,2048]{3,2,1,0:T(8,128)(2,1)} %echo_ref.3), channel_id=1, source_target_pairs={{0,1},{1,0},{2,3},{3,2},{4,5},{5,4},{6,7},{7,6},{8,9},{9,8},{10,11... | collective-permute-start | bytes 1572872 | tf_op jit(solution)/shard_map/ppermute | solution.py:35
  0.5 0.2 %bands.1.bands_ref = bf16[8,192,256]{2,1,0:T(8,128)(2,1)S(1)} custom-call(), custom_call_target="tpu_custom_call" | custom-call | flops 11000000512 | bytes 36000000 | tf_op jit(solution)/shard_map/bands/pallas_call | solution.py:688
  0.7 0.4 %copy-done = bf16[2,8,8,2048]{3,2,1,0:T(8,128)(2,1)S(1)} copy-done((bf16[2,8,8,2048]{3,2,1,0:T(8,128)(2,1)S(1)}, bf16[2,8,8,2048]{3,2,1,0:T(8,128)(2,1)}, u32[]{:S(2)}) %copy-start) | copy-done | bytes 524312
  1.1 0.0 copy-start.3
  1.1 0.9 %interior.1.inner_ref = bf16[128,2688]{1,0:T(8,128)(2,1)S(1)} custom-call(bf16[2,8,8,2048]{3,2,1,0:T(8,128)(2,1)S(1)} %copy-done, bf16[8,192,256]{2,1,0:T(8,128)(2,1)S(1)} %bands.1.bands_ref), custom_call_target="tpu_custom_call" | custom-call | tf_op jit(solution)/shard_map/interior/pallas_call | solution.py:698
  2.0 0.2 %collective-permute-done.across_ref = bf16[2,8,8,2048]{3,2,1,0:T(8,128)(2,1)S(1)} collective-permute-done((bf16[2,8,8,2048]{3,2,1,0:T(8,128)(2,1)}, bf16[2,8,8,2048]{3,2,1,0:T(8,128)(2,1)S(1)}, u32[]{:S(2)}, u32[]{:S(2)}) %collective-permute-start) | collective-permute-done | bytes 524320 | tf_op jit(solution)/shard_map/ppermute | solution.py:35
  2.2 0.0 copy-done.1
  2.2 0.7 %edges.1 = (bf16[128,2688]{1,0:T(8,128)(2,1)S(1)}, bf16[2,8,16,256]{3,2,1,0:T(8,128)(2,1)S(1)}) custom-call(bf16[128,2688]{1,0:T(8,128)(2,1)S(1)} %interior.1.inner_ref, bf16[2,8,8,2048]{3,2,1,0:T(8,128)(2,1)S(1)} %copy-done, bf16[2,8,8,2048]{3,2,1,0:T(8,128)(2,1)S(1)} %collective-permute-done.across_ref, ...), custom_call_target="tpu_custom_call", output_to_operand_aliasing={{0}: (0, {})} | custom-call | tf_op jit(solution)/shard_map/edges/pallas_call | solution.py:716
  2.9 2.9 %collective-permute-start.1 = (bf16[2,8,16,256]{3,2,1,0:T(8,128)(2,1)S(1)}, bf16[2,8,16,256]{3,2,1,0:T(8,128)(2,1)S(1)}, u32[]{:S(2)}, u32[]{:S(2)}) collective-permute-start(bf16[2,8,16,256]{3,2,1,0:T(8,128)(2,1)S(1)} %get-tuple-element.19.after_ref), channel_id=1, source_target_pairs={{0,2},{2,0},{1,3},{3,1},{4,6},{6,4},{5,7},{7,5},{8,10},{10,8},{9,1... | collective-permute-start | bytes 393224 | tf_op jit(solution)/shard_map/ppermute | solution.py:35
  5.8 0.0 copy-done.3
  5.8 0.0 copy-start.2
  5.8 1.2 %phases.1.after_ref.phase_ref = f32[4,8,2,64,256]{4,3,2,1,0:T(8,128)S(1)} custom-call(s32[1,64]{1,0:T(1,128)S(1)} %bitcast.4, bf16[2,8,16,256]{3,2,1,0:T(8,128)(2,1)S(1)} %get-tuple-element.19.after_ref), custom_call_target="tpu_custom_call" | custom-call | tf_op jit(solution)/shard_map/phases/pallas_call | solution.py:729
  7.0 0.8 %rest.1 = (bf16[4,8,16,256]{3,2,1,0:T(8,128)(2,1)S(1)}, bf16[2,8,16,256]{3,2,1,0:T(8,128)(2,1)S(1)}) custom-call(bf16[128,2688]{1,0:T(8,128)(2,1)S(1)} %get-tuple-element.18.filtered_ref, bf16[768,256]{1,0:T(8,128)(2,1)S(1)} %copy-done.1, f32[4,8,2,64,256]{4,3,2,1,0:T(8,128)S(1)} %phases.1.after_ref.phase_ref), custom_call_target="tpu_custom_call" | custom-call | tf_op jit(solution)/shard_map/rest/pallas_call | solution.py:737
  7.8 0.1 collective-permute-start.4
  7.9 0.0 copy-done.2
  7.9 0.7 %weights.1 = (bf16[8,128,32]{2,1,0:T(8,128)(2,1)S(1)}, bf16[6,64,64]{2,1,0:T(8,128)(2,1)S(1)}) custom-call(s32[1,64]{1,0:T(1,128)S(1)} %bitcast.5, s32[64,64]{1,0:T(8,128)S(1)} %bitcast.2, bf16[4,8,16,256]{3,2,1,0:T(8,128)(2,1)S(1)} %get-tuple-element.20.after_ref.keep_ref), custom_call_target="tpu_custom_call" | custom-call | tf_op jit(solution)/shard_map/weights/pallas_call | solution.py:745
  8.6 1.0 %collective-permute-done.1.other_ref = bf16[2,8,16,256]{3,2,1,0:T(8,128)(2,1)S(1)} collective-permute-done((bf16[2,8,16,256]{3,2,1,0:T(8,128)(2,1)S(1)}, bf16[2,8,16,256]{3,2,1,0:T(8,128)(2,1)S(1)}, u32[]{:S(2)}, u32[]{:S(2)}) %collective-permute-start.1) | collective-permute-done | bytes 131104 | tf_op jit(solution)/shard_map/ppermute | solution.py:35
  9.6 0.8 %inner.2 = (bf16[2,64,256]{2,1,0:T(8,128)(2,1)S(1)}, bf16[2,64,256]{2,1,0:T(8,128)(2,1)S(1)}) custom-call(bf16[4,8,16,256]{3,2,1,0:T(8,128)(2,1)S(1)} %get-tuple-element.20.after_ref.keep_ref, bf16[2,8,16,256]{3,2,1,0:T(8,128)(2,1)S(1)} %collective-permute-done.1.other_ref, bf16[8,128,32]{2,1,0:T(8,128)(2,1)S(1)} %get-tuple-element.21.first_ref, ...), custom_call_target="tpu_custom_call" | custom-call | flops 3300000000 | bytes 10800000 | tf_op jit(solution)/shard_map/inner/pallas_call | solution.py:761
  10.4 3.9 %collective-permute-start.2 = (bf16[2,64,256]{2,1,0:T(8,128)(2,1)S(1)}, bf16[2,64,256]{2,1,0:T(8,128)(2,1)S(1)}, u32[]{:S(2)}, u32[]{:S(2)}) collective-permute-start(bf16[2,64,256]{2,1,0:T(8,128)(2,1)S(1)} %get-tuple-element.23), channel_id=1, source_target_pairs={{0,12},{4,8},{8,4},{12,0},{1,13},{5,9},{9,5},{13,1},{2,14},{6,10},... | collective-permute-start | bytes 196616 | tf_op jit(solution)/shard_map/ppermute | solution.py:782
  14.4 0.0 collective-permute-start.3
  14.4 0.0 collective-permute-done.4.other_ref
  14.4 0.8 %inner.3 = (bf16[2,64,256]{2,1,0:T(8,128)(2,1)S(1)}, bf16[2,64,256]{2,1,0:T(8,128)(2,1)S(1)}) custom-call(bf16[4,8,16,256]{3,2,1,0:T(8,128)(2,1)S(1)} %get-tuple-element.20.after_ref.keep_ref, bf16[2,8,16,256]{3,2,1,0:T(8,128)(2,1)S(1)} %collective-permute-done.4.other_ref, bf16[8,128,32]{2,1,0:T(8,128)(2,1)S(1)} %get-tuple-element.21.first_ref, ...), custom_call_target="tpu_custom_call" | custom-call | flops 3300000000 | bytes 10800000 | tf_op jit(solution)/shard_map/inner/pallas_call | solution.py:761
  15.2 0.7 %collective-permute-start.5 = (bf16[2,64,256]{2,1,0:T(8,128)(2,1)S(1)}, bf16[2,64,256]{2,1,0:T(8,128)(2,1)S(1)}, u32[]{:S(2)}, u32[]{:S(2)}) collective-permute-start(bf16[2,64,256]{2,1,0:T(8,128)(2,1)S(1)} %get-tuple-element.29), channel_id=1, source_target_pairs={{0,4},{4,0},{8,12},{12,8},{1,5},{5,1},{9,13},{13,9},{2,6},{6,2},{1... | collective-permute-start | bytes 196616 | tf_op jit(solution)/shard_map/ppermute | solution.py:782
  15.9 0.8 %outer_tables.1 = (bf16[6,64,64]{2,1,0:T(8,128)(2,1)S(1)}, f32[6,2,64,256]{3,2,1,0:T(8,128)S(1)}, f32[2,64,256]{2,1,0:T(8,128)S(1)}) custom-call(s32[1,64]{1,0:T(1,128)S(1)} %bitcast.6, s32[64,64]{1,0:T(8,128)S(1)} %bitcast.3, bf16[2,64,256]{2,1,0:T(8,128)(2,1)S(1)} %get-tuple-element.26.image_ref), custom_call_target="tpu_custom_call" | custom-call | tf_op jit(solution)/shard_map/outer_tables/pallas_call | solution.py:785
  16.7 0.8 %collective-permute-done.2.rest_0_ = bf16[2,64,256]{2,1,0:T(8,128)(2,1)S(1)} collective-permute-done((bf16[2,64,256]{2,1,0:T(8,128)(2,1)S(1)}, bf16[2,64,256]{2,1,0:T(8,128)(2,1)S(1)}, u32[]{:S(2)}, u32[]{:S(2)}) %collective-permute-start.2) | collective-permute-done | bytes 65568 | tf_op jit(solution)/shard_map/ppermute | solution.py:782
  17.5 2.2 %collective-permute-done.3.rest_1_ = bf16[2,64,256]{2,1,0:T(8,128)(2,1)S(1)} collective-permute-done((bf16[2,64,256]{2,1,0:T(8,128)(2,1)S(1)}, bf16[2,64,256]{2,1,0:T(8,128)(2,1)S(1)}, u32[]{:S(2)}, u32[]{:S(2)}) %collective-permute-start.3) | collective-permute-done | bytes 65568 | tf_op jit(solution)/shard_map/ppermute | solution.py:782
  19.6 0.3 %far.1.far_ref = f32[2,64,256]{2,1,0:T(8,128)S(1)} custom-call(bf16[2,64,256]{2,1,0:T(8,128)(2,1)S(1)} %collective-permute-done.2.rest_0_, bf16[2,64,256]{2,1,0:T(8,128)(2,1)S(1)} %collective-permute-done.3.rest_1_, bf16[6,64,64]{2,1,0:T(8,128)(2,1)S(1)} %get-tuple-element.27.rest_2_.outer_ref, f32[6,2,64,256]{3,2,1,0:T(8,128)S(1)} %get-tuple-element.28.rest_3_.phase_ref), custom_call_target="tpu_custom_call" | custom-call | tf_op jit(solution)/shard_map/far/pallas_call | solution.py:797
  19.9 0.3 %collective-permute-done.5.image_ref = bf16[2,64,256]{2,1,0:T(8,128)(2,1)S(1)} collective-permute-done((bf16[2,64,256]{2,1,0:T(8,128)(2,1)S(1)}, bf16[2,64,256]{2,1,0:T(8,128)(2,1)S(1)}, u32[]{:S(2)}, u32[]{:S(2)}) %collective-permute-start.5) | collective-permute-done | bytes 65568 | tf_op jit(solution)/shard_map/ppermute | solution.py:782
  20.3 1.0 %near.1 = f32[2,64,256]{2,1,0:T(8,128)} custom-call(f32[2,64,256]{2,1,0:T(8,128)S(1)} %far.1.far_ref, bf16[2,64,256]{2,1,0:T(8,128)(2,1)S(1)} %collective-permute-done.5.image_ref, f32[2,64,256]{2,1,0:T(8,128)S(1)} %get-tuple-element.30.own_ref, bf16[6,64,64]{2,1,0:T(8,128)(2,1)S(1)} %get-tuple-element.27.rest_2_.outer_ref, ...), custom_call_target="tpu_custom_call" | custom-call | tf_op jit(solution)/shard_map/near/pallas_call | solution.py:805
Async XLA Ops:
  0.0 2.2 %copy-start.1 = (bf16[768,256]{1,0:T(8,128)(2,1)S(1)}, bf16[768,256]{1,0:T(8,128)(2,1)}, u32[]{:S(2)}) copy-start(bf16[768,256]{1,0:T(8,128)(2,1)} %constant.2.clone.chirp_ref) | copy-start | bytes 1179652
  0.0 1.1 %copy-start = (bf16[2,8,8,2048]{3,2,1,0:T(8,128)(2,1)S(1)}, bf16[2,8,8,2048]{3,2,1,0:T(8,128)(2,1)}, u32[]{:S(2)}) copy-start(bf16[2,8,8,2048]{3,2,1,0:T(8,128)(2,1)} %echo_ref.3) | copy-start | bytes 1572868
  0.0 2.2 %collective-permute-start = (bf16[2,8,8,2048]{3,2,1,0:T(8,128)(2,1)}, bf16[2,8,8,2048]{3,2,1,0:T(8,128)(2,1)S(1)}, u32[]{:S(2)}, u32[]{:S(2)}) collective-permute-start(bf16[2,8,8,2048]{3,2,1,0:T(8,128)(2,1)} %echo_ref.3), channel_id=1, source_target_pairs={{0,1},{1,0},{2,3},{3,2},{4,5},{5,4},{6,7},{7,6},{8,9},{9,8},{10,11... | collective-permute-start | bytes 1572872 | tf_op jit(solution)/shard_map/ppermute | solution.py:35
  1.1 4.7 %copy-start.3 = (s32[64]{0:T(128)S(1)}, s32[64]{0:T(128)}, u32[]{:S(2)}) copy-start(s32[64]{0:T(128)} %param.5) | copy-start | bytes 772
  2.9 6.7 %collective-permute-start.1 = (bf16[2,8,16,256]{3,2,1,0:T(8,128)(2,1)S(1)}, bf16[2,8,16,256]{3,2,1,0:T(8,128)(2,1)S(1)}, u32[]{:S(2)}, u32[]{:S(2)}) collective-permute-start(bf16[2,8,16,256]{3,2,1,0:T(8,128)(2,1)S(1)} %get-tuple-element.19.after_ref), channel_id=1, source_target_pairs={{0,2},{2,0},{1,3},{3,1},{4,6},{6,4},{5,7},{7,5},{8,10},{10,8},{9,1... | collective-permute-start | bytes 393224 | tf_op jit(solution)/shard_map/ppermute | solution.py:35
  5.8 2.1 %copy-start.2 = (s32[32,2,64]{2,1,0:T(2,128)S(1)}, s32[32,2,64]{2,1,0:T(2,128)}, u32[]{:S(2)}) copy-start(s32[32,2,64]{2,1,0:T(2,128)} %param.6) | copy-start | bytes 49156
  7.8 6.5 %collective-permute-start.4 = (bf16[2,8,16,256]{3,2,1,0:T(8,128)(2,1)S(1)}, bf16[2,8,16,256]{3,2,1,0:T(8,128)(2,1)S(1)}, u32[]{:S(2)}, u32[]{:S(2)}) collective-permute-start(bf16[2,8,16,256]{3,2,1,0:T(8,128)(2,1)S(1)} %get-tuple-element.25), channel_id=1, source_target_pairs={{0,2},{2,0},{1,3},{3,1},{4,6},{6,4},{5,7},{7,5},{8,10},{10,8},{9,1... | collective-permute-start | bytes 393224 | tf_op jit(solution)/shard_map/ppermute | solution.py:35
  10.4 7.0 %collective-permute-start.2 = (bf16[2,64,256]{2,1,0:T(8,128)(2,1)S(1)}, bf16[2,64,256]{2,1,0:T(8,128)(2,1)S(1)}, u32[]{:S(2)}, u32[]{:S(2)}) collective-permute-start(bf16[2,64,256]{2,1,0:T(8,128)(2,1)S(1)} %get-tuple-element.23), channel_id=1, source_target_pairs={{0,12},{4,8},{8,4},{12,0},{1,13},{5,9},{9,5},{13,1},{2,14},{6,10},... | collective-permute-start | bytes 196616 | tf_op jit(solution)/shard_map/ppermute | solution.py:782
  14.4 5.3 %collective-permute-start.3 = (bf16[2,64,256]{2,1,0:T(8,128)(2,1)S(1)}, bf16[2,64,256]{2,1,0:T(8,128)(2,1)S(1)}, u32[]{:S(2)}, u32[]{:S(2)}) collective-permute-start(bf16[2,64,256]{2,1,0:T(8,128)(2,1)S(1)} %get-tuple-element.24), channel_id=1, source_target_pairs={{0,8},{4,12},{8,0},{12,4},{1,9},{5,13},{9,1},{13,5},{2,10},{6,14},... | collective-permute-start | bytes 196616 | tf_op jit(solution)/shard_map/ppermute | solution.py:782
  15.2 5.1 %collective-permute-start.5 = (bf16[2,64,256]{2,1,0:T(8,128)(2,1)S(1)}, bf16[2,64,256]{2,1,0:T(8,128)(2,1)S(1)}, u32[]{:S(2)}, u32[]{:S(2)}) collective-permute-start(bf16[2,64,256]{2,1,0:T(8,128)(2,1)S(1)} %get-tuple-element.29), channel_id=1, source_target_pairs={{0,4},{4,0},{8,12},{12,8},{1,5},{5,1},{9,13},{13,9},{2,6},{6,2},{1... | collective-permute-start | bytes 196616 | tf_op jit(solution)/shard_map/ppermute | solution.py:782

commit v9 on v8

--- a/solution.py
+++ b/solution.py
@@ -553,7 +553,7 @@
     )
 
 
-ROWS = 8
+ROWS = 16
 
 
 def inner_kernel(indices, keep_ref, other_ref, first_ref, inner_ref, phase_ref, *rest):
@@ -579,7 +579,7 @@
     def lift(piece, image, slot):
         level_ref[piece, image] = jnp.dot(
             inner_ref[slot],
-            picture_ref[piece, image].astype(jnp.bfloat16),
+            picture_ref[piece, image],
             preferred_element_type=jnp.float32,
         )
 
@@ -608,8 +608,8 @@
 
     def write_picture(piece):
         def write(image, row, real, imag):
-            picture_ref[piece, image, row : row + ROWS, :columns] = real
-            picture_ref[piece, image, row : row + ROWS, columns:] = imag
+            picture_ref[piece, image, row : row + ROWS, :columns] = real.astype(jnp.bfloat16)
+            picture_ref[piece, image, row : row + ROWS, columns:] = imag.astype(jnp.bfloat16)
 
         return write
 
@@ -629,8 +629,8 @@
         base += count
         slot += count
     for piece in pieces:
-        out_refs[piece][0] = picture_ref[piece, 0, :, :columns].astype(jnp.bfloat16)
-        out_refs[piece][1] = picture_ref[piece, 0, :, columns:].astype(jnp.bfloat16)
+        out_refs[piece][0] = picture_ref[piece, 0, :, :columns]
+        out_refs[piece][1] = picture_ref[piece, 0, :, columns:]
 
 
 def far_kernel(distances, *rest):
@@ -765,7 +765,7 @@
             out_specs=[vmem()] * size,
             scratch_shapes=[
                 pltpu.VMEM((size, pulses, 2 * beams, piece_width), f32),
-                pltpu.VMEM((size, pulses // 2, beams, 2 * piece_width), f32),
+                pltpu.VMEM((size, pulses // 2, beams, 2 * piece_width), bf16),
                 pltpu.VMEM((size, pulses // 2, beams, 2 * piece_width), f32),
             ],
             name="inner",

time: 21.4 us -> 21.4 us (level)
  no operation moved by 1% of the time
where the time goes in v9:
time: 21.4 us; the launch traced here: 21.2 us
  Pallas kernels  8.15 us (38%)
  starting transfers between devices  8.1 us (38%)
  waiting for transfers between devices  4.48 us (21%)
  local copies, waits for them, and re-layouts  0.41 us (2%)
    ppermute x3, starting transfers between devices, fast(): images[distance] = lax.ppermute(images[distance], 'pulse', pairs)  4.62 us
    ppermute x3, starting transfers between devices, swapped(): lax.ppermute(x, axis, [(i, i ^ 1 << distance) for i in range(lax.axis_siz...  3.48 us
    ppermute x3, waiting for transfers between devices, fast(): images[distance] = lax.ppermute(images[distance], 'pulse', pairs)  3.23 us
    pallas_call x2, Pallas kernels, merge(): pl.pallas_call(functools.partial(inner_kernel, [last - distance for dista...  1.62 us
    ppermute x3, waiting for transfers between devices, swapped(): lax.ppermute(x, axis, [(i, i ^ 1 << distance) for i in range(lax.axis_siz...  1.25 us
    pallas_call x1, Pallas kernels, fast(): pl.pallas_call(functools.partial(phases_kernel, (pulses, rx_count, width)...  1.19 us
    pallas_call x1, Pallas kernels, fast(): pl.pallas_call(near_kernel, out_shape=picture_shape, in_specs=[vmem()] *...  0.95 us
    pallas_call x1, Pallas kernels, fast(): pl.pallas_call(interior_kernel, out_shape=filtered_shape, in_specs=[vmem(...  0.89 us
  transfers between devices with their start and end apart: 6, of which 5 were waited for; matrix products, arithmetic and copies ran while one was open for 0% of the time, Pallas kernels for 31%

profile of v9, /device:TPU:0, one launch (start us, length us, event | category | flops | bytes accessed | tf_op | source)
XLA Modules:
  0.0 21.2 jit_solution(13491266482674212187)
XLA Ops:
  0.0 0.0 copy-start.1
  0.0 0.0 copy-start
  0.0 0.5 %collective-permute-start = (bf16[2,8,8,2048]{3,2,1,0:T(8,128)(2,1)}, bf16[2,8,8,2048]{3,2,1,0:T(8,128)(2,1)S(1)}, u32[]{:S(2)}, u32[]{:S(2)}) collective-permute-start(bf16[2,8,8,2048]{3,2,1,0:T(8,128)(2,1)} %echo_ref.3), channel_id=1, source_target_pairs={{0,1},{1,0},{2,3},{3,2},{4,5},{5,4},{6,7},{7,6},{8,9},{9,8},{10,11... | collective-permute-start | bytes 1572872 | tf_op jit(solution)/shard_map/ppermute | solution.py:35
  0.5 0.2 %bands.1.bands_ref = bf16[8,192,256]{2,1,0:T(8,128)(2,1)S(1)} custom-call(), custom_call_target="tpu_custom_call" | custom-call | flops 11000000512 | bytes 36000000 | tf_op jit(solution)/shard_map/bands/pallas_call | solution.py:688
  0.7 0.4 %copy-done = bf16[2,8,8,2048]{3,2,1,0:T(8,128)(2,1)S(1)} copy-done((bf16[2,8,8,2048]{3,2,1,0:T(8,128)(2,1)S(1)}, bf16[2,8,8,2048]{3,2,1,0:T(8,128)(2,1)}, u32[]{:S(2)}) %copy-start) | copy-done | bytes 524312
  1.1 0.0 copy-start.3
  1.1 0.9 %interior.1.inner_ref = bf16[128,2688]{1,0:T(8,128)(2,1)S(1)} custom-call(bf16[2,8,8,2048]{3,2,1,0:T(8,128)(2,1)S(1)} %copy-done, bf16[8,192,256]{2,1,0:T(8,128)(2,1)S(1)} %bands.1.bands_ref), custom_call_target="tpu_custom_call" | custom-call | tf_op jit(solution)/shard_map/interior/pallas_call | solution.py:698
  2.0 0.2 %collective-permute-done.across_ref = bf16[2,8,8,2048]{3,2,1,0:T(8,128)(2,1)S(1)} collective-permute-done((bf16[2,8,8,2048]{3,2,1,0:T(8,128)(2,1)}, bf16[2,8,8,2048]{3,2,1,0:T(8,128)(2,1)S(1)}, u32[]{:S(2)}, u32[]{:S(2)}) %collective-permute-start) | collective-permute-done | bytes 524320 | tf_op jit(solution)/shard_map/ppermute | solution.py:35
  2.2 0.0 copy-done.1
  2.2 0.7 %edges.1 = (bf16[128,2688]{1,0:T(8,128)(2,1)S(1)}, bf16[2,8,16,256]{3,2,1,0:T(8,128)(2,1)S(1)}) custom-call(bf16[128,2688]{1,0:T(8,128)(2,1)S(1)} %interior.1.inner_ref, bf16[2,8,8,2048]{3,2,1,0:T(8,128)(2,1)S(1)} %copy-done, bf16[2,8,8,2048]{3,2,1,0:T(8,128)(2,1)S(1)} %collective-permute-done.across_ref, ...), custom_call_target="tpu_custom_call", output_to_operand_aliasing={{0}: (0, {})} | custom-call | tf_op jit(solution)/shard_map/edges/pallas_call | solution.py:716
  2.9 2.9 %collective-permute-start.1 = (bf16[2,8,16,256]{3,2,1,0:T(8,128)(2,1)S(1)}, bf16[2,8,16,256]{3,2,1,0:T(8,128)(2,1)S(1)}, u32[]{:S(2)}, u32[]{:S(2)}) collective-permute-start(bf16[2,8,16,256]{3,2,1,0:T(8,128)(2,1)S(1)} %get-tuple-element.19.after_ref), channel_id=1, source_target_pairs={{0,2},{2,0},{1,3},{3,1},{4,6},{6,4},{5,7},{7,5},{8,10},{10,8},{9,1... | collective-permute-start | bytes 393224 | tf_op jit(solution)/shard_map/ppermute | solution.py:35
  5.8 0.0 copy-done.3
  5.8 0.0 copy-start.2
  5.8 1.2 %phases.1.after_ref.phase_ref = f32[4,8,2,64,256]{4,3,2,1,0:T(8,128)S(1)} custom-call(s32[1,64]{1,0:T(1,128)S(1)} %bitcast.4, bf16[2,8,16,256]{3,2,1,0:T(8,128)(2,1)S(1)} %get-tuple-element.19.after_ref), custom_call_target="tpu_custom_call" | custom-call | tf_op jit(solution)/shard_map/phases/pallas_call | solution.py:729
  7.0 0.8 %rest.1 = (bf16[4,8,16,256]{3,2,1,0:T(8,128)(2,1)S(1)}, bf16[2,8,16,256]{3,2,1,0:T(8,128)(2,1)S(1)}) custom-call(bf16[128,2688]{1,0:T(8,128)(2,1)S(1)} %get-tuple-element.18.filtered_ref, bf16[768,256]{1,0:T(8,128)(2,1)S(1)} %copy-done.1, f32[4,8,2,64,256]{4,3,2,1,0:T(8,128)S(1)} %phases.1.after_ref.phase_ref), custom_call_target="tpu_custom_call" | custom-call | tf_op jit(solution)/shard_map/rest/pallas_call | solution.py:737
  7.8 0.1 collective-permute-start.4
  7.9 0.0 copy-done.2
  7.9 0.7 %weights.1 = (bf16[8,128,32]{2,1,0:T(8,128)(2,1)S(1)}, bf16[6,64,64]{2,1,0:T(8,128)(2,1)S(1)}) custom-call(s32[1,64]{1,0:T(1,128)S(1)} %bitcast.5, s32[64,64]{1,0:T(8,128)S(1)} %bitcast.2, bf16[4,8,16,256]{3,2,1,0:T(8,128)(2,1)S(1)} %get-tuple-element.20.after_ref.keep_ref), custom_call_target="tpu_custom_call" | custom-call | tf_op jit(solution)/shard_map/weights/pallas_call | solution.py:745
  8.6 1.0 %collective-permute-done.1.other_ref = bf16[2,8,16,256]{3,2,1,0:T(8,128)(2,1)S(1)} collective-permute-done((bf16[2,8,16,256]{3,2,1,0:T(8,128)(2,1)S(1)}, bf16[2,8,16,256]{3,2,1,0:T(8,128)(2,1)S(1)}, u32[]{:S(2)}, u32[]{:S(2)}) %collective-permute-start.1) | collective-permute-done | bytes 131104 | tf_op jit(solution)/shard_map/ppermute | solution.py:35
  9.6 0.8 %inner.2 = (bf16[2,64,256]{2,1,0:T(8,128)(2,1)S(1)}, bf16[2,64,256]{2,1,0:T(8,128)(2,1)S(1)}) custom-call(bf16[4,8,16,256]{3,2,1,0:T(8,128)(2,1)S(1)} %get-tuple-element.20.after_ref.keep_ref, bf16[2,8,16,256]{3,2,1,0:T(8,128)(2,1)S(1)} %collective-permute-done.1.other_ref, bf16[8,128,32]{2,1,0:T(8,128)(2,1)S(1)} %get-tuple-element.21.first_ref, ...), custom_call_target="tpu_custom_call" | custom-call | flops 3300000000 | bytes 10800000 | tf_op jit(solution)/shard_map/inner/pallas_call | solution.py:761
  10.4 3.9 %collective-permute-start.2 = (bf16[2,64,256]{2,1,0:T(8,128)(2,1)S(1)}, bf16[2,64,256]{2,1,0:T(8,128)(2,1)S(1)}, u32[]{:S(2)}, u32[]{:S(2)}) collective-permute-start(bf16[2,64,256]{2,1,0:T(8,128)(2,1)S(1)} %get-tuple-element.23), channel_id=1, source_target_pairs={{0,12},{4,8},{8,4},{12,0},{1,13},{5,9},{9,5},{13,1},{2,14},{6,10},... | collective-permute-start | bytes 196616 | tf_op jit(solution)/shard_map/ppermute | solution.py:782
  14.4 0.0 collective-permute-start.3
  14.4 0.0 collective-permute-done.4.other_ref
  14.4 0.8 %inner.3 = (bf16[2,64,256]{2,1,0:T(8,128)(2,1)S(1)}, bf16[2,64,256]{2,1,0:T(8,128)(2,1)S(1)}) custom-call(bf16[4,8,16,256]{3,2,1,0:T(8,128)(2,1)S(1)} %get-tuple-element.20.after_ref.keep_ref, bf16[2,8,16,256]{3,2,1,0:T(8,128)(2,1)S(1)} %collective-permute-done.4.other_ref, bf16[8,128,32]{2,1,0:T(8,128)(2,1)S(1)} %get-tuple-element.21.first_ref, ...), custom_call_target="tpu_custom_call" | custom-call | flops 3300000000 | bytes 10800000 | tf_op jit(solution)/shard_map/inner/pallas_call | solution.py:761
  15.2 0.7 %collective-permute-start.5 = (bf16[2,64,256]{2,1,0:T(8,128)(2,1)S(1)}, bf16[2,64,256]{2,1,0:T(8,128)(2,1)S(1)}, u32[]{:S(2)}, u32[]{:S(2)}) collective-permute-start(bf16[2,64,256]{2,1,0:T(8,128)(2,1)S(1)} %get-tuple-element.29), channel_id=1, source_target_pairs={{0,4},{4,0},{8,12},{12,8},{1,5},{5,1},{9,13},{13,9},{2,6},{6,2},{1... | collective-permute-start | bytes 196616 | tf_op jit(solution)/shard_map/ppermute | solution.py:782
  15.9 0.8 %outer_tables.1 = (bf16[6,64,64]{2,1,0:T(8,128)(2,1)S(1)}, f32[6,2,64,256]{3,2,1,0:T(8,128)S(1)}, f32[2,64,256]{2,1,0:T(8,128)S(1)}) custom-call(s32[1,64]{1,0:T(1,128)S(1)} %bitcast.6, s32[64,64]{1,0:T(8,128)S(1)} %bitcast.3, bf16[2,64,256]{2,1,0:T(8,128)(2,1)S(1)} %get-tuple-element.26.image_ref), custom_call_target="tpu_custom_call" | custom-call | tf_op jit(solution)/shard_map/outer_tables/pallas_call | solution.py:785
  16.7 0.8 %collective-permute-done.2.rest_0_ = bf16[2,64,256]{2,1,0:T(8,128)(2,1)S(1)} collective-permute-done((bf16[2,64,256]{2,1,0:T(8,128)(2,1)S(1)}, bf16[2,64,256]{2,1,0:T(8,128)(2,1)S(1)}, u32[]{:S(2)}, u32[]{:S(2)}) %collective-permute-start.2) | collective-permute-done | bytes 65568 | tf_op jit(solution)/shard_map/ppermute | solution.py:782
  17.5 2.2 %collective-permute-done.3.rest_1_ = bf16[2,64,256]{2,1,0:T(8,128)(2,1)S(1)} collective-permute-done((bf16[2,64,256]{2,1,0:T(8,128)(2,1)S(1)}, bf16[2,64,256]{2,1,0:T(8,128)(2,1)S(1)}, u32[]{:S(2)}, u32[]{:S(2)}) %collective-permute-start.3) | collective-permute-done | bytes 65568 | tf_op jit(solution)/shard_map/ppermute | solution.py:782
  19.6 0.3 %far.1.far_ref = f32[2,64,256]{2,1,0:T(8,128)S(1)} custom-call(bf16[2,64,256]{2,1,0:T(8,128)(2,1)S(1)} %collective-permute-done.2.rest_0_, bf16[2,64,256]{2,1,0:T(8,128)(2,1)S(1)} %collective-permute-done.3.rest_1_, bf16[6,64,64]{2,1,0:T(8,128)(2,1)S(1)} %get-tuple-element.27.rest_2_.outer_ref, f32[6,2,64,256]{3,2,1,0:T(8,128)S(1)} %get-tuple-element.28.rest_3_.phase_ref), custom_call_target="tpu_custom_call" | custom-call | tf_op jit(solution)/shard_map/far/pallas_call | solution.py:797
  19.9 0.3 %collective-permute-done.5.image_ref = bf16[2,64,256]{2,1,0:T(8,128)(2,1)S(1)} collective-permute-done((bf16[2,64,256]{2,1,0:T(8,128)(2,1)S(1)}, bf16[2,64,256]{2,1,0:T(8,128)(2,1)S(1)}, u32[]{:S(2)}, u32[]{:S(2)}) %collective-permute-start.5) | collective-permute-done | bytes 65568 | tf_op jit(solution)/shard_map/ppermute | solution.py:782
  20.3 1.0 %near.1 = f32[2,64,256]{2,1,0:T(8,128)} custom-call(f32[2,64,256]{2,1,0:T(8,128)S(1)} %far.1.far_ref, bf16[2,64,256]{2,1,0:T(8,128)(2,1)S(1)} %collective-permute-done.5.image_ref, f32[2,64,256]{2,1,0:T(8,128)S(1)} %get-tuple-element.30.own_ref, bf16[6,64,64]{2,1,0:T(8,128)(2,1)S(1)} %get-tuple-element.27.rest_2_.outer_ref, ...), custom_call_target="tpu_custom_call" | custom-call | tf_op jit(solution)/shard_map/near/pallas_call | solution.py:805
Async XLA Ops:
  0.0 2.2 %copy-start.1 = (bf16[768,256]{1,0:T(8,128)(2,1)S(1)}, bf16[768,256]{1,0:T(8,128)(2,1)}, u32[]{:S(2)}) copy-start(bf16[768,256]{1,0:T(8,128)(2,1)} %constant.2.clone.chirp_ref) | copy-start | bytes 1179652
  0.0 1.1 %copy-start = (bf16[2,8,8,2048]{3,2,1,0:T(8,128)(2,1)S(1)}, bf16[2,8,8,2048]{3,2,1,0:T(8,128)(2,1)}, u32[]{:S(2)}) copy-start(bf16[2,8,8,2048]{3,2,1,0:T(8,128)(2,1)} %echo_ref.3) | copy-start | bytes 1572868
  0.0 2.2 %collective-permute-start = (bf16[2,8,8,2048]{3,2,1,0:T(8,128)(2,1)}, bf16[2,8,8,2048]{3,2,1,0:T(8,128)(2,1)S(1)}, u32[]{:S(2)}, u32[]{:S(2)}) collective-permute-start(bf16[2,8,8,2048]{3,2,1,0:T(8,128)(2,1)} %echo_ref.3), channel_id=1, source_target_pairs={{0,1},{1,0},{2,3},{3,2},{4,5},{5,4},{6,7},{7,6},{8,9},{9,8},{10,11... | collective-permute-start | bytes 1572872 | tf_op jit(solution)/shard_map/ppermute | solution.py:35
  1.1 4.7 %copy-start.3 = (s32[64]{0:T(128)S(1)}, s32[64]{0:T(128)}, u32[]{:S(2)}) copy-start(s32[64]{0:T(128)} %param.5) | copy-start | bytes 772
  2.9 6.7 %collective-permute-start.1 = (bf16[2,8,16,256]{3,2,1,0:T(8,128)(2,1)S(1)}, bf16[2,8,16,256]{3,2,1,0:T(8,128)(2,1)S(1)}, u32[]{:S(2)}, u32[]{:S(2)}) collective-permute-start(bf16[2,8,16,256]{3,2,1,0:T(8,128)(2,1)S(1)} %get-tuple-element.19.after_ref), channel_id=1, source_target_pairs={{0,2},{2,0},{1,3},{3,1},{4,6},{6,4},{5,7},{7,5},{8,10},{10,8},{9,1... | collective-permute-start | bytes 393224 | tf_op jit(solution)/shard_map/ppermute | solution.py:35
  5.8 2.1 %copy-start.2 = (s32[32,2,64]{2,1,0:T(2,128)S(1)}, s32[32,2,64]{2,1,0:T(2,128)}, u32[]{:S(2)}) copy-start(s32[32,2,64]{2,1,0:T(2,128)} %param.6) | copy-start | bytes 49156
  7.8 6.5 %collective-permute-start.4 = (bf16[2,8,16,256]{3,2,1,0:T(8,128)(2,1)S(1)}, bf16[2,8,16,256]{3,2,1,0:T(8,128)(2,1)S(1)}, u32[]{:S(2)}, u32[]{:S(2)}) collective-permute-start(bf16[2,8,16,256]{3,2,1,0:T(8,128)(2,1)S(1)} %get-tuple-element.25), channel_id=1, source_target_pairs={{0,2},{2,0},{1,3},{3,1},{4,6},{6,4},{5,7},{7,5},{8,10},{10,8},{9,1... | collective-permute-start | bytes 393224 | tf_op jit(solution)/shard_map/ppermute | solution.py:35
  10.4 7.0 %collective-permute-start.2 = (bf16[2,64,256]{2,1,0:T(8,128)(2,1)S(1)}, bf16[2,64,256]{2,1,0:T(8,128)(2,1)S(1)}, u32[]{:S(2)}, u32[]{:S(2)}) collective-permute-start(bf16[2,64,256]{2,1,0:T(8,128)(2,1)S(1)} %get-tuple-element.23), channel_id=1, source_target_pairs={{0,12},{4,8},{8,4},{12,0},{1,13},{5,9},{9,5},{13,1},{2,14},{6,10},... | collective-permute-start | bytes 196616 | tf_op jit(solution)/shard_map/ppermute | solution.py:782
  14.4 5.3 %collective-permute-start.3 = (bf16[2,64,256]{2,1,0:T(8,128)(2,1)S(1)}, bf16[2,64,256]{2,1,0:T(8,128)(2,1)S(1)}, u32[]{:S(2)}, u32[]{:S(2)}) collective-permute-start(bf16[2,64,256]{2,1,0:T(8,128)(2,1)S(1)} %get-tuple-element.24), channel_id=1, source_target_pairs={{0,8},{4,12},{8,0},{12,4},{1,9},{5,13},{9,1},{13,5},{2,10},{6,14},... | collective-permute-start | bytes 196616 | tf_op jit(solution)/shard_map/ppermute | solution.py:782
  15.2 5.1 %collective-permute-start.5 = (bf16[2,64,256]{2,1,0:T(8,128)(2,1)S(1)}, bf16[2,64,256]{2,1,0:T(8,128)(2,1)S(1)}, u32[]{:S(2)}, u32[]{:S(2)}) collective-permute-start(bf16[2,64,256]{2,1,0:T(8,128)(2,1)S(1)} %get-tuple-element.29), channel_id=1, source_target_pairs={{0,4},{4,0},{8,12},{12,8},{1,5},{5,1},{9,13},{13,9},{2,6},{6,2},{1... | collective-permute-start | bytes 196616 | tf_op jit(solution)/shard_map/ppermute | solution.py:782

commit v10 on v6

--- a/solution.py
+++ b/solution.py
@@ -362,17 +362,17 @@
     group = 2 * pulses
     lowest = lax.axis_index("rng") == 0
     far = pl.ds(pl.multiple_of(jnp.where(lowest, 0, length - HALO), LANES), HALO)
+    beside = pl.ds(pl.multiple_of(jnp.where(lowest, length - LANES, 0), LANES), LANES)
+    near_tile = jnp.where(lowest, 0, HALO_TILES)
+    far_tile = jnp.where(lowest, 1, 0)
     for part in range(2):
         for pulse in range(pulses):
             where = pl.ds(part * pulses + pulse, channels, stride=group)
             edge = across_ref[part, pulse, :, far].astype(jnp.float32)
-            near_low = echo_ref[part, pulse, :, :LANES].astype(jnp.float32)
-            near_high = echo_ref[part, pulse, :, length - LANES :].astype(jnp.float32)
-            pieces = [edge[:, t * LANES : (t + 1) * LANES] for t in range(HALO_TILES)]
-            for tile in range(HALO_TILES + 1):
-                high = near_high if tile == 0 else pieces[tile - 1]
-                low = near_low if tile == HALO_TILES else pieces[tile]
-                rows_in[tile, where, :] = jnp.where(lowest, high, low)
+            near = echo_ref[part, pulse, :, beside].astype(jnp.float32)
+            rows_in[near_tile, where, :] = near
+            for tile in range(HALO_TILES):
+                rows_in[far_tile + tile, where, :] = edge[:, tile * LANES : (tile + 1) * LANES]
     for channel in range(channels):
         rows = rows_in[:, channel * group : (channel + 1) * group, :].astype(jnp.bfloat16)
         windows = jnp.concatenate(

time: 21.3 us -> 21.4 us (level)
  no operation moved by 1% of the time
where the time goes in v10:
time: 21.4 us; the launch traced here: 21.2 us
  Pallas kernels  8.21 us (38%)
  starting transfers between devices  8.09 us (38%)
  waiting for transfers between devices  4.46 us (21%)
  local copies, waits for them, and re-layouts  0.41 us (2%)
    ppermute x3, starting transfers between devices, fast(): images[distance] = lax.ppermute(images[distance], 'pulse', pairs)  4.61 us
    ppermute x3, starting transfers between devices, swapped(): lax.ppermute(x, axis, [(i, i ^ 1 << distance) for i in range(lax.axis_siz...  3.48 us
    ppermute x3, waiting for transfers between devices, fast(): images[distance] = lax.ppermute(images[distance], 'pulse', pairs)  3.23 us
    pallas_call x2, Pallas kernels, merge(): pl.pallas_call(functools.partial(inner_kernel, [last - distance for dista...  1.64 us
    ppermute x3, waiting for transfers between devices, swapped(): lax.ppermute(x, axis, [(i, i ^ 1 << distance) for i in range(lax.axis_siz...  1.23 us
    pallas_call x1, Pallas kernels, fast(): pl.pallas_call(functools.partial(phases_kernel, (pulses, rx_count, width)...  1.19 us
    pallas_call x1, Pallas kernels, fast(): pl.pallas_call(near_kernel, out_shape=picture_shape, in_specs=[vmem()] *...  0.95 us
    pallas_call x1, Pallas kernels, fast(): pl.pallas_call(interior_kernel, out_shape=filtered_shape, in_specs=[vmem(...  0.89 us
  transfers between devices with their start and end apart: 6, of which 5 were waited for; matrix products, arithmetic and copies ran while one was open for 0% of the time, Pallas kernels for 31%

profile of v10, /device:TPU:0, one launch (start us, length us, event | category | flops | bytes accessed | tf_op | source)
XLA Modules:
  0.0 21.2 jit_solution(12525207354000380665)
XLA Ops:
  0.0 0.0 copy-start.1
  0.0 0.0 copy-start
  0.0 0.5 %collective-permute-start = (bf16[2,8,8,2048]{3,2,1,0:T(8,128)(2,1)}, bf16[2,8,8,2048]{3,2,1,0:T(8,128)(2,1)S(1)}, u32[]{:S(2)}, u32[]{:S(2)}) collective-permute-start(bf16[2,8,8,2048]{3,2,1,0:T(8,128)(2,1)} %echo_ref.3), channel_id=1, source_target_pairs={{0,1},{1,0},{2,3},{3,2},{4,5},{5,4},{6,7},{7,6},{8,9},{9,8},{10,11... | collective-permute-start | bytes 1572872 | tf_op jit(solution)/shard_map/ppermute | solution.py:35
  0.5 0.2 %bands.1.bands_ref = bf16[8,192,256]{2,1,0:T(8,128)(2,1)S(1)} custom-call(), custom_call_target="tpu_custom_call" | custom-call | flops 11000000512 | bytes 36000000 | tf_op jit(solution)/shard_map/bands/pallas_call | solution.py:693
  0.7 0.4 %copy-done = bf16[2,8,8,2048]{3,2,1,0:T(8,128)(2,1)S(1)} copy-done((bf16[2,8,8,2048]{3,2,1,0:T(8,128)(2,1)S(1)}, bf16[2,8,8,2048]{3,2,1,0:T(8,128)(2,1)}, u32[]{:S(2)}) %copy-start) | copy-done | bytes 524312
  1.1 0.0 copy-start.3
  1.1 0.9 %interior.1.inner_ref = bf16[128,2688]{1,0:T(8,128)(2,1)S(1)} custom-call(bf16[2,8,8,2048]{3,2,1,0:T(8,128)(2,1)S(1)} %copy-done, bf16[8,192,256]{2,1,0:T(8,128)(2,1)S(1)} %bands.1.bands_ref), custom_call_target="tpu_custom_call" | custom-call | tf_op jit(solution)/shard_map/interior/pallas_call | solution.py:703
  2.0 0.2 %collective-permute-done.across_ref = bf16[2,8,8,2048]{3,2,1,0:T(8,128)(2,1)S(1)} collective-permute-done((bf16[2,8,8,2048]{3,2,1,0:T(8,128)(2,1)}, bf16[2,8,8,2048]{3,2,1,0:T(8,128)(2,1)S(1)}, u32[]{:S(2)}, u32[]{:S(2)}) %collective-permute-start) | collective-permute-done | bytes 524320 | tf_op jit(solution)/shard_map/ppermute | solution.py:35
  2.2 0.0 copy-done.1
  2.2 0.7 %edges.1 = (bf16[128,2688]{1,0:T(8,128)(2,1)S(1)}, bf16[2,8,16,256]{3,2,1,0:T(8,128)(2,1)S(1)}) custom-call(bf16[128,2688]{1,0:T(8,128)(2,1)S(1)} %interior.1.inner_ref, bf16[2,8,8,2048]{3,2,1,0:T(8,128)(2,1)S(1)} %copy-done, bf16[2,8,8,2048]{3,2,1,0:T(8,128)(2,1)S(1)} %collective-permute-done.across_ref, ...), custom_call_target="tpu_custom_call", output_to_operand_aliasing={{0}: (0, {})} | custom-call | tf_op jit(solution)/shard_map/edges/pallas_call | solution.py:721
  2.9 2.9 %collective-permute-start.1 = (bf16[2,8,16,256]{3,2,1,0:T(8,128)(2,1)S(1)}, bf16[2,8,16,256]{3,2,1,0:T(8,128)(2,1)S(1)}, u32[]{:S(2)}, u32[]{:S(2)}) collective-permute-start(bf16[2,8,16,256]{3,2,1,0:T(8,128)(2,1)S(1)} %get-tuple-element.19.after_ref), channel_id=1, source_target_pairs={{0,2},{2,0},{1,3},{3,1},{4,6},{6,4},{5,7},{7,5},{8,10},{10,8},{9,1... | collective-permute-start | bytes 393224 | tf_op jit(solution)/shard_map/ppermute | solution.py:35
  5.8 0.0 copy-done.3
  5.8 0.0 copy-start.2
  5.8 1.2 %phases.1.after_ref.phase_ref = f32[4,8,2,64,256]{4,3,2,1,0:T(8,128)S(1)} custom-call(s32[1,64]{1,0:T(1,128)S(1)} %bitcast.4, bf16[2,8,16,256]{3,2,1,0:T(8,128)(2,1)S(1)} %get-tuple-element.19.after_ref), custom_call_target="tpu_custom_call" | custom-call | tf_op jit(solution)/shard_map/phases/pallas_call | solution.py:734
  7.0 0.8 %rest.1 = (bf16[4,8,16,256]{3,2,1,0:T(8,128)(2,1)S(1)}, bf16[2,8,16,256]{3,2,1,0:T(8,128)(2,1)S(1)}) custom-call(bf16[128,2688]{1,0:T(8,128)(2,1)S(1)} %get-tuple-element.18.filtered_ref, bf16[768,256]{1,0:T(8,128)(2,1)S(1)} %copy-done.1, f32[4,8,2,64,256]{4,3,2,1,0:T(8,128)S(1)} %phases.1.after_ref.phase_ref), custom_call_target="tpu_custom_call" | custom-call | tf_op jit(solution)/shard_map/rest/pallas_call | solution.py:742
  7.8 0.1 collective-permute-start.4
  7.9 0.0 copy-done.2
  7.9 0.7 %weights.1 = (bf16[8,128,64]{2,1,0:T(8,128)(2,1)S(1)}, bf16[6,64,64]{2,1,0:T(8,128)(2,1)S(1)}) custom-call(s32[1,64]{1,0:T(1,128)S(1)} %bitcast.5, s32[64,64]{1,0:T(8,128)S(1)} %bitcast.2, bf16[4,8,16,256]{3,2,1,0:T(8,128)(2,1)S(1)} %get-tuple-element.20.after_ref.keep_ref), custom_call_target="tpu_custom_call" | custom-call | tf_op jit(solution)/shard_map/weights/pallas_call | solution.py:750
  8.6 1.0 %collective-permute-done.1.other_ref = bf16[2,8,16,256]{3,2,1,0:T(8,128)(2,1)S(1)} collective-permute-done((bf16[2,8,16,256]{3,2,1,0:T(8,128)(2,1)S(1)}, bf16[2,8,16,256]{3,2,1,0:T(8,128)(2,1)S(1)}, u32[]{:S(2)}, u32[]{:S(2)}) %collective-permute-start.1) | collective-permute-done | bytes 131104 | tf_op jit(solution)/shard_map/ppermute | solution.py:35
  9.6 0.8 %inner.2 = (bf16[2,64,256]{2,1,0:T(8,128)(2,1)S(1)}, bf16[2,64,256]{2,1,0:T(8,128)(2,1)S(1)}) custom-call(bf16[4,8,16,256]{3,2,1,0:T(8,128)(2,1)S(1)} %get-tuple-element.20.after_ref.keep_ref, bf16[2,8,16,256]{3,2,1,0:T(8,128)(2,1)S(1)} %collective-permute-done.1.other_ref, bf16[8,128,64]{2,1,0:T(8,128)(2,1)S(1)} %get-tuple-element.21.first_ref, ...), custom_call_target="tpu_custom_call" | custom-call | flops 3300000000 | bytes 10800000 | tf_op jit(solution)/shard_map/inner/pallas_call | solution.py:766
  10.5 3.9 %collective-permute-start.2 = (bf16[2,64,256]{2,1,0:T(8,128)(2,1)S(1)}, bf16[2,64,256]{2,1,0:T(8,128)(2,1)S(1)}, u32[]{:S(2)}, u32[]{:S(2)}) collective-permute-start(bf16[2,64,256]{2,1,0:T(8,128)(2,1)S(1)} %get-tuple-element.23), channel_id=1, source_target_pairs={{0,12},{4,8},{8,4},{12,0},{1,13},{5,9},{9,5},{13,1},{2,14},{6,10},... | collective-permute-start | bytes 196616 | tf_op jit(solution)/shard_map/ppermute | solution.py:787
  14.4 0.0 collective-permute-start.3
  14.4 0.0 collective-permute-done.4.other_ref
  14.4 0.8 %inner.3 = (bf16[2,64,256]{2,1,0:T(8,128)(2,1)S(1)}, bf16[2,64,256]{2,1,0:T(8,128)(2,1)S(1)}) custom-call(bf16[4,8,16,256]{3,2,1,0:T(8,128)(2,1)S(1)} %get-tuple-element.20.after_ref.keep_ref, bf16[2,8,16,256]{3,2,1,0:T(8,128)(2,1)S(1)} %collective-permute-done.4.other_ref, bf16[8,128,64]{2,1,0:T(8,128)(2,1)S(1)} %get-tuple-element.21.first_ref, ...), custom_call_target="tpu_custom_call" | custom-call | flops 3300000000 | bytes 10800000 | tf_op jit(solution)/shard_map/inner/pallas_call | solution.py:766
  15.2 0.7 %collective-permute-start.5 = (bf16[2,64,256]{2,1,0:T(8,128)(2,1)S(1)}, bf16[2,64,256]{2,1,0:T(8,128)(2,1)S(1)}, u32[]{:S(2)}, u32[]{:S(2)}) collective-permute-start(bf16[2,64,256]{2,1,0:T(8,128)(2,1)S(1)} %get-tuple-element.29), channel_id=1, source_target_pairs={{0,4},{4,0},{8,12},{12,8},{1,5},{5,1},{9,13},{13,9},{2,6},{6,2},{1... | collective-permute-start | bytes 196616 | tf_op jit(solution)/shard_map/ppermute | solution.py:787
  15.9 0.8 %outer_tables.1 = (bf16[6,64,64]{2,1,0:T(8,128)(2,1)S(1)}, f32[6,2,64,256]{3,2,1,0:T(8,128)S(1)}, f32[2,64,256]{2,1,0:T(8,128)S(1)}) custom-call(s32[1,64]{1,0:T(1,128)S(1)} %bitcast.6, s32[64,64]{1,0:T(8,128)S(1)} %bitcast.3, bf16[2,64,256]{2,1,0:T(8,128)(2,1)S(1)} %get-tuple-element.26.image_ref), custom_call_target="tpu_custom_call" | custom-call | tf_op jit(solution)/shard_map/outer_tables/pallas_call | solution.py:790
  16.7 0.8 %collective-permute-done.2.rest_0_ = bf16[2,64,256]{2,1,0:T(8,128)(2,1)S(1)} collective-permute-done((bf16[2,64,256]{2,1,0:T(8,128)(2,1)S(1)}, bf16[2,64,256]{2,1,0:T(8,128)(2,1)S(1)}, u32[]{:S(2)}, u32[]{:S(2)}) %collective-permute-start.2) | collective-permute-done | bytes 65568 | tf_op jit(solution)/shard_map/ppermute | solution.py:787
  17.5 2.2 %collective-permute-done.3.rest_1_ = bf16[2,64,256]{2,1,0:T(8,128)(2,1)S(1)} collective-permute-done((bf16[2,64,256]{2,1,0:T(8,128)(2,1)S(1)}, bf16[2,64,256]{2,1,0:T(8,128)(2,1)S(1)}, u32[]{:S(2)}, u32[]{:S(2)}) %collective-permute-start.3) | collective-permute-done | bytes 65568 | tf_op jit(solution)/shard_map/ppermute | solution.py:787
  19.7 0.3 %far.1.far_ref = f32[2,64,256]{2,1,0:T(8,128)S(1)} custom-call(bf16[2,64,256]{2,1,0:T(8,128)(2,1)S(1)} %collective-permute-done.2.rest_0_, bf16[2,64,256]{2,1,0:T(8,128)(2,1)S(1)} %collective-permute-done.3.rest_1_, bf16[6,64,64]{2,1,0:T(8,128)(2,1)S(1)} %get-tuple-element.27.rest_2_.outer_ref, f32[6,2,64,256]{3,2,1,0:T(8,128)S(1)} %get-tuple-element.28.rest_3_.phase_ref), custom_call_target="tpu_custom_call" | custom-call | tf_op jit(solution)/shard_map/far/pallas_call | solution.py:802
  20.0 0.3 %collective-permute-done.5.image_ref = bf16[2,64,256]{2,1,0:T(8,128)(2,1)S(1)} collective-permute-done((bf16[2,64,256]{2,1,0:T(8,128)(2,1)S(1)}, bf16[2,64,256]{2,1,0:T(8,128)(2,1)S(1)}, u32[]{:S(2)}, u32[]{:S(2)}) %collective-permute-start.5) | collective-permute-done | bytes 65568 | tf_op jit(solution)/shard_map/ppermute | solution.py:787
  20.3 1.0 %near.1 = f32[2,64,256]{2,1,0:T(8,128)} custom-call(f32[2,64,256]{2,1,0:T(8,128)S(1)} %far.1.far_ref, bf16[2,64,256]{2,1,0:T(8,128)(2,1)S(1)} %collective-permute-done.5.image_ref, f32[2,64,256]{2,1,0:T(8,128)S(1)} %get-tuple-element.30.own_ref, bf16[6,64,64]{2,1,0:T(8,128)(2,1)S(1)} %get-tuple-element.27.rest_2_.outer_ref, ...), custom_call_target="tpu_custom_call" | custom-call | tf_op jit(solution)/shard_map/near/pallas_call | solution.py:810
Async XLA Ops:
  0.0 2.2 %copy-start.1 = (bf16[768,256]{1,0:T(8,128)(2,1)S(1)}, bf16[768,256]{1,0:T(8,128)(2,1)}, u32[]{:S(2)}) copy-start(bf16[768,256]{1,0:T(8,128)(2,1)} %constant.2.clone.chirp_ref) | copy-start | bytes 1179652
  0.0 1.1 %copy-start = (bf16[2,8,8,2048]{3,2,1,0:T(8,128)(2,1)S(1)}, bf16[2,8,8,2048]{3,2,1,0:T(8,128)(2,1)}, u32[]{:S(2)}) copy-start(bf16[2,8,8,2048]{3,2,1,0:T(8,128)(2,1)} %echo_ref.3) | copy-start | bytes 1572868
  0.0 2.2 %collective-permute-start = (bf16[2,8,8,2048]{3,2,1,0:T(8,128)(2,1)}, bf16[2,8,8,2048]{3,2,1,0:T(8,128)(2,1)S(1)}, u32[]{:S(2)}, u32[]{:S(2)}) collective-permute-start(bf16[2,8,8,2048]{3,2,1,0:T(8,128)(2,1)} %echo_ref.3), channel_id=1, source_target_pairs={{0,1},{1,0},{2,3},{3,2},{4,5},{5,4},{6,7},{7,6},{8,9},{9,8},{10,11... | collective-permute-start | bytes 1572872 | tf_op jit(solution)/shard_map/ppermute | solution.py:35
  1.1 4.8 %copy-start.3 = (s32[64]{0:T(128)S(1)}, s32[64]{0:T(128)}, u32[]{:S(2)}) copy-start(s32[64]{0:T(128)} %param.5) | copy-start | bytes 772
  2.9 6.7 %collective-permute-start.1 = (bf16[2,8,16,256]{3,2,1,0:T(8,128)(2,1)S(1)}, bf16[2,8,16,256]{3,2,1,0:T(8,128)(2,1)S(1)}, u32[]{:S(2)}, u32[]{:S(2)}) collective-permute-start(bf16[2,8,16,256]{3,2,1,0:T(8,128)(2,1)S(1)} %get-tuple-element.19.after_ref), channel_id=1, source_target_pairs={{0,2},{2,0},{1,3},{3,1},{4,6},{6,4},{5,7},{7,5},{8,10},{10,8},{9,1... | collective-permute-start | bytes 393224 | tf_op jit(solution)/shard_map/ppermute | solution.py:35
  5.8 2.1 %copy-start.2 = (s32[32,2,64]{2,1,0:T(2,128)S(1)}, s32[32,2,64]{2,1,0:T(2,128)}, u32[]{:S(2)}) copy-start(s32[32,2,64]{2,1,0:T(2,128)} %param.6) | copy-start | bytes 49156
  7.8 6.6 %collective-permute-start.4 = (bf16[2,8,16,256]{3,2,1,0:T(8,128)(2,1)S(1)}, bf16[2,8,16,256]{3,2,1,0:T(8,128)(2,1)S(1)}, u32[]{:S(2)}, u32[]{:S(2)}) collective-permute-start(bf16[2,8,16,256]{3,2,1,0:T(8,128)(2,1)S(1)} %get-tuple-element.25), channel_id=1, source_target_pairs={{0,2},{2,0},{1,3},{3,1},{4,6},{6,4},{5,7},{7,5},{8,10},{10,8},{9,1... | collective-permute-start | bytes 393224 | tf_op jit(solution)/shard_map/ppermute | solution.py:35
  10.5 7.0 %collective-permute-start.2 = (bf16[2,64,256]{2,1,0:T(8,128)(2,1)S(1)}, bf16[2,64,256]{2,1,0:T(8,128)(2,1)S(1)}, u32[]{:S(2)}, u32[]{:S(2)}) collective-permute-start(bf16[2,64,256]{2,1,0:T(8,128)(2,1)S(1)} %get-tuple-element.23), channel_id=1, source_target_pairs={{0,12},{4,8},{8,4},{12,0},{1,13},{5,9},{9,5},{13,1},{2,14},{6,10},... | collective-permute-start | bytes 196616 | tf_op jit(solution)/shard_map/ppermute | solution.py:787
  14.4 5.3 %collective-permute-start.3 = (bf16[2,64,256]{2,1,0:T(8,128)(2,1)S(1)}, bf16[2,64,256]{2,1,0:T(8,128)(2,1)S(1)}, u32[]{:S(2)}, u32[]{:S(2)}) collective-permute-start(bf16[2,64,256]{2,1,0:T(8,128)(2,1)S(1)} %get-tuple-element.24), channel_id=1, source_target_pairs={{0,8},{4,12},{8,0},{12,4},{1,9},{5,13},{9,1},{13,5},{2,10},{6,14},... | collective-permute-start | bytes 196616 | tf_op jit(solution)/shard_map/ppermute | solution.py:787
  15.2 5.1 %collective-permute-start.5 = (bf16[2,64,256]{2,1,0:T(8,128)(2,1)S(1)}, bf16[2,64,256]{2,1,0:T(8,128)(2,1)S(1)}, u32[]{:S(2)}, u32[]{:S(2)}) collective-permute-start(bf16[2,64,256]{2,1,0:T(8,128)(2,1)S(1)} %get-tuple-element.29), channel_id=1, source_target_pairs={{0,4},{4,0},{8,12},{12,8},{1,5},{5,1},{9,13},{13,9},{2,6},{6,2},{1... | collective-permute-start | bytes 196616 | tf_op jit(solution)/shard_map/ppermute | solution.py:787
